TPU v7x, 32 devices: a whole 2x2x4 slice. The times are simulated.
32 devices in a mesh: pb: 8 (over y, x, core), ka: 4 (over z).
Axes of the slice: x: 2, y: 2, z: 4, core: 2. Of those that a mesh axis runs over, the one named last changes fastest.
Arguments:
- atoms: bfloat16 [24576, 128], P('pb'), may hold values from -6 to 6
- atom_gain: float32 [128], replicated, may hold values from 0.1 to 1.9
- atom_qkv: bfloat16 [128, 384], replicated, may hold values from -0.5 to 0.5
- atom_proj: bfloat16 [128, 128], replicated, may hold values from -0.5 to 0.5
- atom_bias: bfloat16 [4, 24576, 128], P(None, 'pb'), may hold values from -4 to 250
- window_shift: int32 [768], P('pb'), may hold values from -64 to -32, as said below
- token_of_atom: int32 [24576], P('pb'), may hold values from 0 to 3071, as said below
- agg_weight: bfloat16 [128, 768], replicated, may hold values from -0.5 to 0.5
- token_gain: float32 [768], replicated, may hold values from 0.1 to 1.9
- token_q: bfloat16 [768, 768], replicated, may hold values from -0.21875 to 0.21875
- token_kv: bfloat16 [768, 1536], replicated, may hold values from -0.21875 to 0.21875
- token_o: bfloat16 [768, 768], replicated, may hold values from -0.21875 to 0.21875
- pair_bias: bfloat16 [16, 3072, 3072], P(None, 'pb', 'ka'), may hold values from -4 to 250
Outputs:
- atom_out: bfloat16 [24576, 128], P('pb')
- tokens_out: bfloat16 [3072, 768], P('pb')
Inputs may be any that keep to these rules, and one draw needn't show every extreme that they name: token_of_atom never falls along the atoms and names every token at least once. Of the 3072 atoms of one index of pb, all but its last ones belong to that index's own 384 tokens; for every index but the final one, its last 192 to 384 atoms belong to the tokens of the index after, and the final index's atoms are all its own. In every draw some index has all of its last 384 atoms in the index after. The key window of query block b begins at atom 32 b + window_shift[b]; both ends of the range occur in every draw.
All inputs are finite; a program needn't handle non-finite values.
Results may differ from a plain program's by a relative error of at most 0.0095.
Values may be sent and summed in bfloat16 or wider, within the bound.
No kernel may reach another device: no remote copies, remote signals or barrier semaphores. Data moves between devices by JAX's collectives and lax.ppermute only.
A program may use at most 128 MiB of HBM per device.

v0:
```python
import functools
import math

import jax
import jax.numpy as jnp
from jax import lax
from jax.experimental import pallas as pl
from jax.experimental.pallas import tpu as pltpu
from jax.sharding import PartitionSpec as P

AH = 4
TH = 16
WIN_Q = 32
WIN_K = 128
SHIFT_MAX = 384
PARTS = 2
LANES = 128
F32 = jnp.float32
BF16 = jnp.bfloat16
VMEM_LIMIT = 56 * 1024 * 1024
VMEM_SMALL = 24 * 1024 * 1024


def full(shape):
    return pl.BlockSpec(shape, lambda *_: (0,) * len(shape))


def params(limit=VMEM_LIMIT):
    return pltpu.CompilerParams(vmem_limit_bytes=limit)


def norm_rows(as_float, gain):
    centre = jnp.mean(as_float, axis=-1, keepdims=True)
    spread = jnp.mean(jnp.square(as_float - centre), axis=-1, keepdims=True)
    return (as_float - centre) * lax.rsqrt(spread + 1e-05) * gain


def dot(a, b):
    return jnp.dot(a, b, preferred_element_type=F32)


def atom_kernel(
    chunks,
    atom_total,
    tok_rows,
    shift_ref,
    pos_ref,
    atoms_ref,
    left_ref,
    right_ref,
    gain_ref,
    qkv_ref,
    proj_ref,
    bias_ref,
    tok_ref,
    out_ref,
    msg_ref,
    q_s,
    k_s,
    v_s,
    mix_s,
    x_s,
):
    step = pl.program_id(0)
    rows, width = atoms_ref.shape
    size = out_ref.shape[0]
    half = WIN_K // 2
    head = width // AH
    shard = pos_ref[0]

    @pl.when(step == 0)
    def _():
        gain = gain_ref[...].reshape(1, width)
        x_s[:half, :] = left_ref[...]
        x_s[half : half + rows, :] = atoms_ref[...]
        x_s[half + rows :, :] = right_ref[...]
        total = rows + 2 * half
        tile = 5 * WIN_K if total % (5 * WIN_K) == 0 else WIN_K

        def one(c, carry):
            at = pl.ds(pl.multiple_of(c * tile, tile), tile)
            normed = norm_rows(x_s[at, :].astype(F32), gain).astype(BF16)
            res = dot(normed, qkv_ref[...])
            q_s[at, :] = (res[:, :width] * (1.0 / math.sqrt(head))).astype(BF16)
            k_s[:, at] = res[:, width : 2 * width].T.astype(BF16)
            v_s[at, :width] = res[:, 2 * width :].astype(BF16)
            v_s[at, width:] = jnp.ones((tile, width), BF16)
            return carry

        lax.fori_loop(0, total // tile, one, 0)

    group = WIN_K // WIN_Q
    atoms_group = group * WIN_Q
    span = AH * WIN_Q
    lane_q = lax.broadcasted_iota(jnp.int32, (WIN_Q, width), 1)
    heads = [(lane_q >= h * head) & (lane_q < (h + 1) * head) for h in range(AH)]
    lane = lax.broadcasted_iota(jnp.int32, (span, WIN_K), 1)
    slot = lax.broadcasted_iota(jnp.int32, (1, WIN_K), 1)
    blocks = size // WIN_Q

    def region(n):
        return pl.ds(pl.multiple_of(step * size + n // group * atoms_group, atoms_group), 2 * WIN_K)

    def score(n):
        query = q_s[pl.ds(pl.multiple_of(step * size + n * WIN_Q + half, WIN_Q), WIN_Q), :].astype(F32)
        stacked = jnp.concatenate([jnp.where(m, query, 0.0).astype(BF16) for m in heads], axis=0)
        return dot(stacked, k_s[:, region(n)])

    def soften(n, scores):
        offset = n % group * WIN_Q + half + shift_ref[step * blocks + n]
        early = lane >= offset
        begin = n * WIN_Q
        bias = bias_ref[:, begin : begin + WIN_Q, :].astype(F32).reshape(span, WIN_K)
        index = slot + jnp.where(slot >= offset, 0, WIN_K)
        index = index + (step * size + n // group * atoms_group + shard * rows - half)
        shut = jnp.where((index >= 0) & (index < atom_total), 0.0, -jnp.inf)
        logits = jnp.where(early, scores[:, :WIN_K], scores[:, WIN_K:]) + (
            pltpu.roll(bias, jnp.bitwise_and(offset, WIN_K - 1), 1) + shut
        )
        terms = jnp.exp(logits - jnp.max(logits, axis=-1, keepdims=True))
        return jnp.concatenate(
            [jnp.where(early, terms, 0.0).astype(BF16), jnp.where(early, 0.0, terms).astype(BF16)], axis=1
        )

    def mix(n, weights):
        mixed = dot(weights, v_s[region(n), :])
        values, total = mixed[:WIN_Q, :width], mixed[:WIN_Q, width:]
        for h in range(1, AH):
            part = mixed[h * WIN_Q : (h + 1) * WIN_Q]
            values = jnp.where(heads[h], part[:, :width], values)
            total = jnp.where(heads[h], part[:, width:], total)
        mix_s[n * WIN_Q : (n + 1) * WIN_Q, :] = (values / total).astype(BF16)

    def project_out(g):
        local = g * atoms_group
        at = pl.multiple_of(step * size + local, atoms_group)
        own = atoms_ref[pl.ds(at, atoms_group), :].astype(F32)
        result = own + dot(mix_s[local : local + atoms_group, :], proj_ref[...])
        out_ref[local : local + atoms_group, :] = result.astype(BF16)

    ahead = score(0)
    behind = None
    for n in range(blocks):
        scores = ahead
        if n + 1 < blocks:
            ahead = score(n + 1)
        if n:
            mix(n - 1, behind)
        behind = soften(n, scores)
        if n % group == 0 and n:
            project_out(n // group - 1)
    mix(blocks - 1, behind)
    project_out(blocks // group - 1)

    @pl.when(step == chunks - 1)
    def _():
        ids = tok_ref[tok_ref.shape[0] - 8 :, :]
        code = jnp.maximum(ids - (shard + 1) * tok_rows + 1, 0)
        high = (code >> 4).astype(F32)
        low = (code & 15).astype(F32)
        msg_ref[:SHIFT_MAX, :] = out_ref[size - SHIFT_MAX :, :]
        msg_ref[SHIFT_MAX:, :] = jnp.concatenate([high, low], axis=0).astype(BF16)


def atom_attention(shift, pos, atoms, left, right, gain, qkv, proj, bias, tok2d, tok_rows, atom_total):
    rows, width = atoms.shape
    size = 2 * SHIFT_MAX
    chunks = rows // size
    half = WIN_K // 2
    return pl.pallas_call(
        functools.partial(atom_kernel, chunks, atom_total, tok_rows),
        grid_spec=pltpu.PrefetchScalarGridSpec(
            num_scalar_prefetch=2,
            grid=(chunks,),
            in_specs=[
                full((rows, width)),
                full((half, width)),
                full((half, width)),
                full((width,)),
                full(qkv.shape),
                full(proj.shape),
                pl.BlockSpec((AH, size, WIN_K), lambda i, *_: (0, i, 0)),
                full(tok2d.shape),
            ],
            out_specs=[
                pl.BlockSpec((size, width), lambda i, *_: (i, 0)),
                full((SHIFT_MAX + 16, width)),
            ],
            scratch_shapes=[
                pltpu.VMEM((rows + 2 * half, width), BF16),
                pltpu.VMEM((width, rows + 2 * half), BF16),
                pltpu.VMEM((rows + 2 * half, 2 * width), BF16),
                pltpu.VMEM((size, width), BF16),
                pltpu.VMEM((rows + 2 * half, width), BF16),
            ],
        ),
        out_shape=[
            jax.ShapeDtypeStruct((rows, width), BF16),
            jax.ShapeDtypeStruct((SHIFT_MAX + 16, width), BF16),
        ],
        compiler_params=params(),
        cost_estimate=pl.CostEstimate(flops=8 * 10**9, bytes_accessed=6 * 10**6, transcendentals=2 * 10**6),
        name="atom_attention",
    )(shift, pos, atoms, left, right, gain, qkv, proj, bias, tok2d)


def activate(rows, weight_half):
    u = dot(rows, weight_half)
    return (u + u * jnp.tanh(u)).astype(BF16)


def pool_kernel(tok_rows, pos_ref, out_ref, weight_ref, tok_ref, sum_ref, cnt_ref):
    step = pl.program_id(0)
    size = out_ref.shape[0]
    lines = size // LANES
    base = pos_ref[0] * tok_rows
    token = lax.broadcasted_iota(jnp.int32, (tok_rows, LANES), 0)
    weight_half = (weight_ref[...].astype(F32) * 0.5).astype(BF16)
    hidden = activate(out_ref[...], weight_half)
    ones = []
    for j in range(lines):
        ids = tok_ref[pl.ds(step * lines + j, 1), :] - base
        ones.append(jnp.where(token == ids, 1.0, 0.0))
    hot = jnp.concatenate(ones, axis=1).astype(BF16)
    count = functools.reduce(jnp.add, ones)
    part = dot(hot, hidden)

    @pl.when(step == 0)
    def _():
        sum_ref[...] = part
        cnt_ref[...] = count

    @pl.when(step > 0)
    def _():
        sum_ref[...] += part
        cnt_ref[...] += count


def pool(pos, atom_out, weight, tok2d, tok_rows, part):
    rows, width = atom_out.shape
    feats = weight.shape[1] // PARTS
    size = min(1024, rows)
    return pl.pallas_call(
        functools.partial(pool_kernel, tok_rows),
        grid_spec=pltpu.PrefetchScalarGridSpec(
            num_scalar_prefetch=1,
            grid=(rows // size,),
            in_specs=[
                pl.BlockSpec((size, width), lambda i, *_: (i, 0)),
                pl.BlockSpec((width, feats), lambda i, *_: (0, part)),
                full(tok2d.shape),
            ],
            out_specs=[full((tok_rows, feats)), full((tok_rows, LANES))],
        ),
        out_shape=[
            jax.ShapeDtypeStruct((tok_rows, feats), F32),
            jax.ShapeDtypeStruct((tok_rows, LANES), F32),
        ],
        compiler_params=params(VMEM_SMALL),
        cost_estimate=pl.CostEstimate(flops=2 * 10**9, bytes_accessed=2 * 10**6, transcendentals=10**6),
        name="pool",
    )(pos, atom_out, weight, tok2d)


def finish_kernel(msg_ref, weight_ref, sum_ref, cnt_ref, repr_ref):
    tok_rows = sum_ref.shape[0]
    size = msg_ref.shape[0] - 16
    lines = size // LANES
    token = lax.broadcasted_iota(jnp.int32, (tok_rows, LANES), 0).astype(F32)
    weight_half = (weight_ref[...].astype(F32) * 0.5).astype(BF16)
    hidden = activate(msg_ref[:size, :], weight_half)
    codes = msg_ref[size:, :].astype(F32)
    ids = codes[:8] * 16.0 + codes[8:] - 1.0
    ones = [jnp.where(token == ids[8 - lines + j : 9 - lines + j], 1.0, 0.0) for j in range(lines)]
    hot = jnp.concatenate(ones, axis=1).astype(BF16)
    count = functools.reduce(jnp.add, ones) + cnt_ref[...]
    sums = sum_ref[...] + dot(hot, hidden)
    repr_ref[...] = (sums / jnp.sum(count, axis=1, keepdims=True)).astype(BF16)


def finish(msg, weight, sums, counts, part):
    rows, feats = sums.shape
    return pl.pallas_call(
        finish_kernel,
        grid=(1,),
        in_specs=[
            full(msg.shape),
            pl.BlockSpec((weight.shape[0], feats), lambda i: (0, part)),
            full(sums.shape),
            full(counts.shape),
        ],
        out_specs=full((rows, feats)),
        out_shape=jax.ShapeDtypeStruct((rows, feats), BF16),
        compiler_params=params(VMEM_SMALL),
        cost_estimate=pl.CostEstimate(flops=2 * 10**8, bytes_accessed=2 * 10**6, transcendentals=2 * 10**5),
        name="token_finish",
    )(msg, weight, sums, counts)


def query_kernel(scale, a_ref, b_ref, gain_ref, weight_hbm, out_ref, weight_s, sem):
    copy = pltpu.make_async_copy(weight_hbm, weight_s, sem)
    copy.start()
    rows = jnp.concatenate([a_ref[...].astype(F32), b_ref[...].astype(F32)], axis=1)
    normed = norm_rows(rows, gain_ref[...].reshape(1, -1)).astype(BF16)
    copy.wait()
    out_ref[...] = (dot(normed, weight_s[...]) * scale).astype(BF16)


def project_queries(halves, gain, weight):
    rows = halves[0].shape[0]
    return pl.pallas_call(
        functools.partial(query_kernel, 1.0 / math.sqrt(weight.shape[1] // TH)),
        in_specs=[pl.BlockSpec(memory_space=pltpu.VMEM)] * 3 + [pl.BlockSpec(memory_space=pltpu.HBM)],
        out_shape=jax.ShapeDtypeStruct((rows, weight.shape[1]), BF16),
        scratch_shapes=[pltpu.VMEM(weight.shape, BF16), pltpu.SemaphoreType.DMA],
        compiler_params=params(VMEM_SMALL),
        cost_estimate=pl.CostEstimate(flops=5 * 10**8, bytes_accessed=3 * 10**6, transcendentals=0),
        name="queries",
    )(*halves, gain, weight)


GROUPS = 2
ROW_TILE = 32


def pack_message(mixed, lse, heads):
    lane = lax.broadcasted_iota(jnp.int32, lse.shape, 1)
    high = lse.astype(BF16).astype(F32)
    rest = lse - high
    middle = rest.astype(BF16).astype(F32)
    low = rest - middle
    first = jnp.where(lane < heads, high, pltpu.roll(middle, heads, 1))
    second = jnp.where(lane < heads, low, 0.0)
    turned = jnp.concatenate([first, second], axis=0).T
    return jnp.concatenate([mixed.astype(BF16), turned[: 2 * heads].astype(BF16)], axis=0)


def unpack_message(msg, rows, heads):
    coded = msg[rows:].astype(F32)
    coded = jnp.concatenate([coded, jnp.zeros((LANES - 2 * heads, coded.shape[1]), F32)], axis=0).T
    first = coded[:rows]
    return msg[:rows].astype(F32), first + pltpu.roll(first, LANES - heads, 1) + coded[rows:]


def merge_parts(mixed, lse, other, lse_b, heads):
    rows, feats = mixed.shape
    width = feats // heads
    spot = lax.broadcasted_iota(jnp.int32, (rows, LANES), 1)
    lse_b = jnp.where(spot < heads, lse_b, lse)
    top = jnp.maximum(lse, lse_b)
    part = jnp.exp(lse - top)
    total = part + jnp.exp(lse_b - top)
    share = part / total
    high = share.astype(BF16)
    low = (share - high.astype(F32)).astype(BF16)
    head = lax.broadcasted_iota(jnp.int32, (LANES, feats), 0) * width
    column = lax.broadcasted_iota(jnp.int32, (LANES, feats), 1)
    spread = jnp.where((column >= head) & (column < head + width), 1.0, 0.0).astype(BF16)
    wide = dot(high, spread) + dot(low, spread)
    return other + wide * (mixed - other), top + jnp.log(total)


def attend_group(group, heads, width, half, q_ref, k_ref, v_ref, bias_hbm, scratch):
    score_s, term_s, top_s, bias_s, mix_s, sems = scratch
    rows = mix_s.shape[0]
    at = pl.multiple_of(half * rows, rows)
    pairs = heads // 2
    spot = lax.broadcasted_iota(jnp.int32, (rows, LANES), 1)

    def layout(p):
        first = 2 * p * width
        low = first // LANES * LANES
        wide = -(-(first + 2 * width) // LANES) * LANES - low
        lane = lax.broadcasted_iota(jnp.int32, (rows, wide), 1)
        first -= low
        masks = [(lane >= first + j * width) & (lane < first + (j + 1) * width) for j in range(2)]
        return slice(low, low + wide), first, masks

    keys = score_s[0].shape[1]
    chunk = min(256, keys)
    chunks = keys // chunk
    tiles = 2 * rows // ROW_TILE

    def stack(p):
        window, _, masks = layout(p)
        query = q_ref[pl.ds(at, rows), window].astype(F32)
        return jnp.concatenate([jnp.where(m, query, 0.0).astype(BF16) for m in masks], axis=0)

    def score(p, n, stacked):
        part = slice(n * chunk, (n + 1) * chunk)
        score_s[p % 2][:, part] = dot(stacked, k_ref[layout(p)[0], part])

    def soften(p, n):
        for r in range(n * tiles // chunks * ROW_TILE, (n + 1) * tiles // chunks * ROW_TILE, ROW_TILE):
            bias = bias_s[2 * p + r // rows, r % rows : r % rows + ROW_TILE, :].astype(F32)
            scores = score_s[p % 2][r : r + ROW_TILE, :] + bias
            top = jnp.max(scores, axis=-1, keepdims=True)
            term_s[p % 2][r : r + ROW_TILE, :] = jnp.exp(scores - top).astype(BF16)
            top_s[p % 2][r : r + ROW_TILE, :] = jnp.broadcast_to(top, (ROW_TILE, LANES))

    def mix(p, n, mixed):
        part = slice(n * chunk, (n + 1) * chunk)
        window, first, _ = layout(p)
        values = v_ref[part, window]
        column = lax.broadcasted_iota(jnp.int32, values.shape, 1)
        used = (column >= first) & (column < first + 2 * width)
        more = dot(term_s[p % 2][:, part], jnp.where(used, values.astype(F32), 1.0).astype(BF16))
        return more if mixed is None else mixed + more

    def close(p, mixed, lse):
        window, first, masks = layout(p)
        free = 0 if first >= 16 else 2 * width
        total = mixed[:, free : free + 1]
        mixed = mixed / total
        sums = top_s[p % 2][...] + jnp.log(total)
        result = mix_s[:, window]
        for j in range(2):
            result = jnp.where(masks[j], mixed[j * rows : (j + 1) * rows], result)
            lse = jnp.where(spot == 2 * p + j, sums[j * rows : (j + 1) * rows], lse)
        mix_s[:, window] = result
        return lse

    copies = bias_copies(group, heads, half, bias_hbm, bias_s, sems)
    lse = jnp.zeros((rows, LANES), F32)
    stacked = stack(0)
    for n in range(chunks):
        score(0, n, stacked)
    copies[0].wait()
    for p in range(pairs):
        if p == 1:
            for copy in copies[1:]:
                copy.wait()
        mixed = None
        if p + 1 < pairs:
            stacked = stack(p + 1)
        for n in range(chunks):
            if p + 1 < pairs:
                score(p + 1, n, stacked)
            if p:
                mixed = mix(p - 1, n, mixed)
            soften(p, n)
        if p:
            lse = close(p - 1, mixed, lse)
    mixed = None
    for n in range(chunks):
        mixed = mix(pairs - 1, n, mixed)
    lse = close(pairs - 1, mixed, lse)
    return mix_s[...], lse


def bias_copies(group, heads, half, bias_hbm, bias_s, sems):
    rows = bias_s.shape[1]
    at = pl.multiple_of(half * rows, rows)
    return [
        pltpu.make_async_copy(
            bias_hbm.at[pl.ds(group * heads + 2 * p, 2), pl.ds(at, rows), :],
            bias_s.at[pl.ds(2 * p, 2)],
            sems.at[p],
        )
        for p in range(heads // 2)
    ]


def group_scratch(rows, keys, feats, heads):
    return [
        pltpu.VMEM((2 * rows, keys), F32),
        pltpu.VMEM((2 * rows, keys), F32),
        pltpu.VMEM((2 * rows, keys), BF16),
        pltpu.VMEM((2 * rows, keys), BF16),
        pltpu.VMEM((2 * rows, LANES), F32),
        pltpu.VMEM((2 * rows, LANES), F32),
        pltpu.VMEM((heads, rows, keys), BF16),
        pltpu.VMEM((rows, feats), F32),
        pltpu.SemaphoreType.DMA((heads // 2,)),
        pltpu.VMEM((2, 2 * feats, feats), BF16),
        pltpu.SemaphoreType.DMA((2,)),
    ]


def scratch_of(refs):
    return refs[:2], refs[2:4], refs[4:6], refs[6], refs[7], refs[8]


def weight_copies(group, weight_hbm, refs):
    weight_s, sems = refs[9:11]
    feats = weight_s.shape[2]
    return [
        pltpu.make_async_copy(
            weight_hbm.at[:, pl.ds((part * GROUPS + group) * feats, feats)], weight_s.at[part], sems.at[part]
        )
        for part in range(2)
    ]


def project_keys(x_ref, weight_s, copies, k_ref, v_ref):
    tile = x_ref.shape[0] // 2
    copies[0].wait()
    for r in range(0, x_ref.shape[0], tile):
        k_ref[:, r : r + tile] = dot(x_ref[r : r + tile, :], weight_s[0]).T.astype(BF16)
    copies[1].wait()
    for r in range(0, x_ref.shape[0], tile):
        v_ref[r : r + tile, :] = dot(x_ref[r : r + tile, :], weight_s[1]).astype(BF16)


def first_kernel(heads, width, half_ref, core_ref, q_ref, own_a, own_b, other_a, other_b, gain_ref, weight_hbm,
                 bias_hbm, x_ref, k_ref, v_ref, msg_ref, *refs):
    scratch = scratch_of(refs)
    weights = weight_copies(0, weight_hbm, refs)
    for copy in weights:
        copy.start()
    for copy in bias_copies(0, heads, half_ref[0], bias_hbm, scratch[3], scratch[5]):
        copy.start()
    rows = own_a.shape[0]
    core = core_ref[0]
    gain = gain_ref[...].reshape(1, -1)
    for place, parts in ((core, (own_a, own_b)), (1 - core, (other_a, other_b))):
        values = jnp.concatenate([part[...].astype(F32) for part in parts], axis=1)
        x_ref[pl.ds(pl.multiple_of(place * rows, rows), rows), :] = norm_rows(values, gain).astype(BF16)
    project_keys(x_ref, refs[9], weights, k_ref, v_ref)
    mixed, lse = attend_group(0, heads, width, half_ref[0], q_ref, k_ref, v_ref, bias_hbm, scratch)
    msg_ref[...] = pack_message(mixed, lse, heads)


def next_kernel(group, heads, width, half_ref, q_ref, x_ref, weight_hbm, bias_hbm, k_ref, v_ref, msg_ref, *refs):
    scratch = scratch_of(refs)
    weights = weight_copies(group, weight_hbm, refs)
    for copy in weights:
        copy.start()
    for copy in bias_copies(group, heads, half_ref[0], bias_hbm, scratch[3], scratch[5]):
        copy.start()
    project_keys(x_ref, refs[9], weights, k_ref, v_ref)
    mixed, lse = attend_group(group, heads, width, half_ref[0], q_ref, k_ref, v_ref, bias_hbm, scratch)
    msg_ref[...] = pack_message(mixed, lse, heads)


def keep_kernel(group, heads, width, half_ref, q_ref, k_ref, v_ref, near_ref, bias_hbm, o_ref, lse_ref, msg_ref, *refs):
    scratch = scratch_of(refs)
    for copy in bias_copies(group, heads, half_ref[0], bias_hbm, scratch[3], scratch[5]):
        copy.start()
    mixed, lse = attend_group(group, heads, width, half_ref[0], q_ref, k_ref, v_ref, bias_hbm, scratch)
    rows = mixed.shape[0]
    mixed, lse = merge_parts(mixed, lse, *unpack_message(near_ref[...], rows, heads), heads)
    o_ref[...] = mixed
    lse_ref[...] = lse
    msg_ref[...] = pack_message(mixed, lse, heads)


def group_call(kernel, group, half, scalars, q, arrays, weights, bias, outs, name):
    tok_rows, all_feats = q.shape
    rows, keys, feats = tok_rows // 2, bias.shape[2], all_feats // GROUPS
    heads = TH // GROUPS
    shapes = {
        "x": ((keys, all_feats), BF16),
        "k": ((feats, keys), BF16),
        "v": ((keys, feats), BF16),
        "o": ((rows, feats), F32),
        "lse": ((rows, LANES), F32),
        "msg": ((rows + 2 * heads, feats), BF16),
    }
    return pl.pallas_call(
        functools.partial(kernel, heads, feats // heads),
        grid_spec=pltpu.PrefetchScalarGridSpec(
            num_scalar_prefetch=1 + len(scalars),
            grid=(1,),
            in_specs=[pl.BlockSpec((tok_rows, feats), lambda i, *_: (0, group))]
            + [full(array.shape) for array in arrays]
            + [pl.BlockSpec(memory_space=pltpu.HBM)] * (1 if weights is None else 2),
            out_specs=[full(shapes[out][0]) for out in outs],
            scratch_shapes=group_scratch(rows, keys, feats, heads),
        ),
        out_shape=[jax.ShapeDtypeStruct(*shapes[out]) for out in outs],
        compiler_params=params(),
        cost_estimate=pl.CostEstimate(flops=4 * 10**9, bytes_accessed=4 * 10**6, transcendentals=10**6),
        name=name,
    )(half, *scalars, q, *arrays, *([] if weights is None else [weights]), bias)


def merge_kernel(heads, o_ref, lse_ref, msg_ref, out_ref, sum_ref, back_ref):
    rows = o_ref.shape[0]
    mixed, lse = merge_parts(o_ref[...], lse_ref[...], *unpack_message(msg_ref[...], rows, heads), heads)
    out_ref[...] = mixed
    sum_ref[...] = lse
    back_ref[...] = pack_message(mixed, lse, heads)


def merge(o, lse, msg):
    return pl.pallas_call(
        functools.partial(merge_kernel, TH // GROUPS),
        out_shape=[jax.ShapeDtypeStruct(a.shape, a.dtype) for a in (o, lse, msg)],
        compiler_params=params(VMEM_SMALL),
        name="merge",
    )(o, lse, msg)


def settle_kernel(heads, o_ref, lse_ref, msg_ref, out_ref):
    rows = o_ref.shape[0]
    mixed, _ = merge_parts(o_ref[...], lse_ref[...], *unpack_message(msg_ref[...], rows, heads), heads)
    out_ref[...] = mixed.astype(BF16)


def settle(o, lse, msg):
    return pl.pallas_call(
        functools.partial(settle_kernel, TH // GROUPS),
        out_shape=jax.ShapeDtypeStruct(o.shape, BF16),
        compiler_params=params(VMEM_SMALL),
        name="settle",
    )(o, lse, msg)


def output_kernel(half_ref, own_a, own_b, other_a, other_b, a_ref, b_ref, weight_ref, out_ref):
    rows, feats = own_a.shape
    for place, first, second in ((half_ref[0], own_a, own_b), (1 - half_ref[0], other_a, other_b)):
        mine = pl.ds(pl.multiple_of(place * rows, rows), rows)
        result = dot(first[...], weight_ref[:feats, :]) + dot(second[...], weight_ref[feats:, :])
        out_ref[mine, :feats] = (a_ref[mine, :].astype(F32) + result[:, :feats]).astype(BF16)
        out_ref[mine, feats:] = (b_ref[mine, :].astype(F32) + result[:, feats:]).astype(BF16)


def output_rows(half, own, other, token_repr, weight):
    rows = token_repr[0].shape[0]
    return pl.pallas_call(
        output_kernel,
        in_specs=[pl.BlockSpec(memory_space=pltpu.SMEM)] + [pl.BlockSpec(memory_space=pltpu.VMEM)] * 7,
        out_shape=jax.ShapeDtypeStruct((rows, weight.shape[1]), BF16),
        compiler_params=params(VMEM_SMALL),
        name="output_rows",
    )(half, *own, *other, *token_repr, weight)


def bits_of(count):
    return [1 << b for b in range(count.bit_length() - 1)]


def key_parts(halves):
    n_pb, n_ka = lax.axis_size("pb"), lax.axis_size("ka")
    cores = n_pb // n_ka
    chips = n_pb // cores
    shard, plane = lax.axis_index("pb"), lax.axis_index("ka")
    bits = bits_of(chips)
    core = lax.rem(shard, cores)
    away = jnp.bitwise_xor(shard // cores, plane)
    held = list(halves)
    for r in range(len(bits)):
        pairs = []
        gets = jnp.bool_(False)
        for c in range(cores):
            order = bits if c % 2 == 0 else bits[::-1]
            known = sum(order[:r])
            for k in range(n_ka):
                for j in range(chips):
                    if (j ^ k) & ~known == 0:
                        pairs.append(((j * cores + c) * n_ka + k, ((j ^ order[r]) * cores + c) * n_ka + k))
            fresh = (jnp.bitwise_and(away, ~(known + order[r])) == 0) & (jnp.bitwise_and(away, order[r]) != 0)
            gets = gets | (fresh & (core == c))
        held = [jnp.where(gets, lax.ppermute(part, ("pb", "ka"), pairs), part) for part in held]
    return held, [lax.ppermute(part, "pb", [(p, p ^ 1) for p in range(n_pb)]) for part in held]


def body(
    atoms,
    atom_gain,
    atom_qkv,
    atom_proj,
    atom_bias,
    window_shift,
    token_of_atom,
    agg_weight,
    token_gain,
    token_q,
    token_kv,
    token_o,
    pair_bias,
):
    n_pb, n_ka = lax.axis_size("pb"), lax.axis_size("ka")
    shard, plane = lax.axis_index("pb"), lax.axis_index("ka")
    rows, width = atoms.shape
    tok_rows = pair_bias.shape[1]
    half = WIN_K // 2
    up = [(i, i + 1) for i in range(n_pb - 1)]
    down = [(i + 1, i) for i in range(n_pb - 1)]
    pos = shard.astype(jnp.int32).reshape(1)
    tok2d = token_of_atom.reshape(rows // LANES, LANES)
    left = lax.ppermute(atoms[rows - half :], "pb", up)
    right = lax.ppermute(atoms[:half], "pb", down)
    atom_out, msg = atom_attention(
        window_shift, pos, atoms, left, right, atom_gain, atom_qkv, atom_proj,
        atom_bias, tok2d, tok_rows, rows * n_pb,
    )
    behind = lax.ppermute(msg, "pb", up)
    token_repr, own_keys, other_keys = [], [], []
    for part in range(PARTS):
        sums, counts = pool(pos, atom_out, agg_weight, tok2d, tok_rows, part)
        token_repr.append(finish(behind, agg_weight, sums, counts, part))
    own_keys, other_keys = key_parts(token_repr)
    queries = project_queries(token_repr, token_gain, token_q)
    parity = jnp.bitwise_and(plane ^ (plane >> 1), 1).astype(jnp.int32)
    core = lax.rem(shard, n_pb // n_ka).astype(jnp.int32)
    keep, send = parity.reshape(1), (1 - parity).reshape(1)
    swap = [(i, i ^ 1) for i in range(n_ka)]
    bits = bits_of(n_ka)[1:]

    def far(msg, bit):
        return lax.ppermute(msg, "ka", [(i, i ^ (2 * bit - 1)) for i in range(n_ka)])

    x, k, v, msg = group_call(
        first_kernel, 0, send, (core.reshape(1),), queries, (*own_keys, *other_keys, token_gain), token_kv,
        pair_bias, ("x", "k", "v", "msg"), "attend_first",
    )
    held, near = [(k, v)], [lax.ppermute(msg, "ka", swap)]
    for g in range(1, GROUPS):
        k, v, msg = group_call(
            functools.partial(next_kernel, g), g, send, (), queries, (x,), token_kv,
            pair_bias, ("k", "v", "msg"), "attend_next",
        )
        held.append((k, v))
        near.append(lax.ppermute(msg, "ka", swap))
    sums, gone = [], []
    for g in range(GROUPS):
        o, lse, msg = group_call(
            functools.partial(keep_kernel, g), g, keep, (), queries, (*held[g], near[g]), None,
            pair_bias, ("o", "lse", "msg"), "attend_keep",
        )
        sums.append((o, lse))
        gone.append(far(msg, bits[0]))
    own_mix, other_mix = [], []
    for g in range(GROUPS):
        (o, lse), got = sums[g], gone[g]
        for bit in bits[1:]:
            o, lse, msg = merge(o, lse, got)
            got = far(msg, bit)
        own_mix.append(settle(o, lse, got))
        other_mix.append(lax.ppermute(own_mix[g], "ka", swap))
    return atom_out, output_rows(keep, own_mix, other_mix, token_repr, token_o)


def solution(mesh):
    return jax.shard_map(
        body,
        mesh=mesh,
        in_specs=(
            P("pb", None),
            P(),
            P(),
            P(),
            P(None, "pb", None),
            P("pb"),
            P("pb"),
            P(),
            P(),
            P(),
            P(),
            P(),
            P(None, "pb", "ka"),
        ),
        out_specs=(P("pb", None), P("pb", None)),
        check_vma=False,
    )
```

profile of v0, /device:TPU:0, one launch (start us, length us, event | category | flops | bytes accessed | tf_op | source)
XLA Modules:
  0.0 117.1 jit_solution(4810523807674007861)
XLA Ops:
  0.6 0.7 fusion
  1.4 1.3 %collective-permute-start.1 = (bf16[64,128]{1,0:T(8,128)(2,1)S(1)}, bf16[64,128]{1,0:T(8,128)(2,1)S(1)}, u32[]{:S(2)}, u32[]{:S(2)}) collective-permute-start(bf16[64,128]{1,0:T(8,128)(2,1)S(1)} %get-tuple-element.40), channel_id=1, source_target_pairs={{4,0},{8,4},{12,8},{16,12},{20,16},{24,20},{28,24},{5,1},{9,5},{13... | collective-permute-start | bytes 49160 | tf_op jit(solution)/shard_map/ppermute | solution.py:684
  2.7 3.0 %collective-permute-start = (bf16[64,128]{1,0:T(8,128)(2,1)S(1)}, bf16[64,128]{1,0:T(8,128)(2,1)S(1)}, u32[]{:S(2)}, u32[]{:S(2)}) collective-permute-start(bf16[64,128]{1,0:T(8,128)(2,1)S(1)} %get-tuple-element.41), channel_id=1, source_target_pairs={{0,4},{4,8},{8,12},{12,16},{16,20},{20,24},{24,28},{1,5},{5,9},{9,... | collective-permute-start | bytes 49160 | tf_op jit(solution)/shard_map/ppermute | solution.py:683
  5.7 0.8 collective-permute-done.left_ref
  7.1 18.7 %atom_attention.1 = (bf16[3072,128]{1,0:T(8,128)(2,1)}, bf16[400,128]{1,0:T(8,128)(2,1)}) custom-call(s32[96]{0:T(128)} %shift_ref.1, s32[1]{0:T(128)} %bitcast.pos_ref, bf16[3072,128]{1,0:T(8,128)(2,1)} %atoms_ref.1, bf16[64,128]{1,0:T(8,128)(2,1)} %copy-done.18, bf16[64,128]{1,0:T(8,128)(2,1)} %copy-done.17, f32[128]{0:T(128)} %gain_ref.3, ...), custom_call_target="tpu_custom_call" | custom-call | flops 8000000000 | bytes 6000000 | tf_op jit(solution)/shard_map/atom_attention/pallas_call | solution.py:170
  25.8 4.5 %collective-permute-start.2 = (bf16[400,128]{1,0:T(8,128)(2,1)}, bf16[400,128]{1,0:T(8,128)(2,1)S(1)}, u32[]{:S(2)}, u32[]{:S(2)}) collective-permute-start(bf16[400,128]{1,0:T(8,128)(2,1)} %get-tuple-element.22), channel_id=1, source_target_pairs={{0,4},{4,8},{8,12},{12,16},{16,20},{20,24},{24,28},{1,5},{5,9},{9,... | collective-permute-start | bytes 307208 | tf_op jit(solution)/shard_map/ppermute | solution.py:689
  30.4 1.1 copy-done.10
  31.5 3.0 %pool.3 = (f32[384,384]{1,0:T(8,128)S(1)}, f32[384,128]{1,0:T(8,128)S(1)}) custom-call(s32[1]{0:T(128)} %bitcast.pos_ref, bf16[3072,128]{1,0:T(8,128)(2,1)S(1)} %copy-done.10, bf16[128,768]{1,0:T(8,128)(2,1)S(1)} %copy-done.2, s32[24,128]{1,0:T(8,128)S(1)} %bitcast.6), custom_call_target="tpu_custom_call" | custom-call | flops 2000000000 | bytes 2000000 | tf_op jit(solution)/shard_map/pool/pallas_call | solution.py:243
  35.1 4.3 %collective-permute-start.5 = (bf16[384,384]{1,0:T(8,128)(2,1)S(1)}, bf16[384,384]{1,0:T(8,128)(2,1)S(1)}, u32[]{:S(2)}, u32[]{:S(2)}) collective-permute-start(bf16[384,384]{1,0:T(8,128)(2,1)S(1)} %token_finish.3.b_ref), channel_id=1, source_target_pairs={{0,8},{9,1},{18,26},{27,19},{4,20},{13,29},{22,6},{31,15}} | collective-permute-start | bytes 884744 | tf_op jit(solution)/shard_map/ppermute | solution.py:655
  39.3 3.0 %pool.2 = (f32[384,384]{1,0:T(8,128)S(1)}, f32[384,128]{1,0:T(8,128)S(1)}) custom-call(s32[1]{0:T(128)} %bitcast.pos_ref, bf16[3072,128]{1,0:T(8,128)(2,1)S(1)} %copy-done.10, bf16[128,768]{1,0:T(8,128)(2,1)S(1)} %copy-done.2, s32[24,128]{1,0:T(8,128)S(1)} %bitcast.7), custom_call_target="tpu_custom_call" | custom-call | flops 2000000000 | bytes 2000000 | tf_op jit(solution)/shard_map/pool/pallas_call | solution.py:243
  43.0 1.3 %collective-permute-start.3 = (bf16[384,384]{1,0:T(8,128)(2,1)S(1)}, bf16[384,384]{1,0:T(8,128)(2,1)S(1)}, u32[]{:S(2)}, u32[]{:S(2)}) collective-permute-start(bf16[384,384]{1,0:T(8,128)(2,1)S(1)} %token_finish.2.a_ref), channel_id=1, source_target_pairs={{0,8},{9,1},{18,26},{27,19},{4,20},{13,29},{22,6},{31,15}} | collective-permute-start | bytes 884744 | tf_op jit(solution)/shard_map/ppermute | solution.py:655
  44.4 2.7 %collective-permute-start.6 = (bf16[384,384]{1,0:T(8,128)(2,1)S(1)}, bf16[384,384]{1,0:T(8,128)(2,1)S(1)}, u32[]{:S(2)}, u32[]{:S(2)}) collective-permute-start(bf16[384,384]{1,0:T(8,128)(2,1)S(1)} %broadcast_select_fusion), channel_id=1, source_target_pairs={{0,16},{8,24},{1,17},{9,25},{18,2},{26,10},{19,3},{27,11},{4,12},{... | collective-permute-start | bytes 884744 | tf_op jit(solution)/shard_map/ppermute | solution.py:655
  47.0 2.2 %collective-permute-done.3 = bf16[384,384]{1,0:T(8,128)(2,1)S(1)} collective-permute-done((bf16[384,384]{1,0:T(8,128)(2,1)S(1)}, bf16[384,384]{1,0:T(8,128)(2,1)S(1)}, u32[]{:S(2)}, u32[]{:S(2)}) %collective-permute-start.3) | collective-permute-done | bytes 294944 | tf_op jit(solution)/shard_map/ppermute | solution.py:655
  49.2 1.3 %collective-permute-start.4 = (bf16[384,384]{1,0:T(8,128)(2,1)S(1)}, bf16[384,384]{1,0:T(8,128)(2,1)S(1)}, u32[]{:S(2)}, u32[]{:S(2)}) collective-permute-start(bf16[384,384]{1,0:T(8,128)(2,1)S(1)} %broadcast_select_fusion.1), channel_id=1, source_target_pairs={{0,16},{8,24},{1,17},{9,25},{18,2},{26,10},{19,3},{27,11},{4,12},{... | collective-permute-start | bytes 884744 | tf_op jit(solution)/shard_map/ppermute | solution.py:655
  50.6 1.5 %collective-permute-done.6 = bf16[384,384]{1,0:T(8,128)(2,1)S(1)} collective-permute-done((bf16[384,384]{1,0:T(8,128)(2,1)S(1)}, bf16[384,384]{1,0:T(8,128)(2,1)S(1)}, u32[]{:S(2)}, u32[]{:S(2)}) %collective-permute-start.6) | collective-permute-done | bytes 294944 | tf_op jit(solution)/shard_map/ppermute | solution.py:655
  52.2 3.0 %collective-permute-done.4 = bf16[384,384]{1,0:T(8,128)(2,1)S(1)} collective-permute-done((bf16[384,384]{1,0:T(8,128)(2,1)S(1)}, bf16[384,384]{1,0:T(8,128)(2,1)S(1)}, u32[]{:S(2)}, u32[]{:S(2)}) %collective-permute-start.4) | collective-permute-done | bytes 294944 | tf_op jit(solution)/shard_map/ppermute | solution.py:655
  55.4 1.4 %queries.1.q_ref = bf16[384,768]{1,0:T(8,128)(2,1)S(1)} custom-call(bf16[384,384]{1,0:T(8,128)(2,1)S(1)} %token_finish.2.a_ref, bf16[384,384]{1,0:T(8,128)(2,1)S(1)} %token_finish.3.b_ref, f32[768]{0:T(1024)S(1)} %copy-done.8, bf16[768,768]{1,0:T(8,128)(2,1)S(1)} %copy-done.1), custom_call_target="tpu_custom_call" | custom-call | flops 500000000 | bytes 3000000 | tf_op jit(solution)/shard_map/queries/pallas_call | solution.py:311
  56.9 0.8 copy-done.3
  57.7 0.7 copy-done.13
  58.5 7.4 %attend_first.1 = (bf16[768,768]{1,0:T(8,128)(2,1)}, bf16[384,768]{1,0:T(8,128)(2,1)}, bf16[768,384]{1,0:T(8,128)(2,1)}, bf16[208,384]{1,0:T(8,128)(2,1)}) custom-call(s32[1]{0:T(128)} %bitcast.3.half_ref, s32[1]{0:T(128)} %bitcast.4.core_ref, bf16[384,768]{1,0:T(8,128)(2,1)} %copy-done.3, bf16[384,384]{1,0:T(8,128)(2,1)} %copy-done.12, ...), custom_call_target="tpu_custom_call" | custom-call | flops 4000000000 | bytes 4000000 | tf_op jit(solution)/shard_map/attend_first/pallas_call | solution.py:560
  65.9 5.1 %collective-permute-start.9 = (bf16[208,384]{1,0:T(8,128)(2,1)}, bf16[208,384]{1,0:T(8,128)(2,1)S(1)}, u32[]{:S(2)}, u32[]{:S(2)}) collective-permute-start(bf16[208,384]{1,0:T(8,128)(2,1)} %get-tuple-element.29), channel_id=1, source_target_pairs={{0,1},{1,0},{2,3},{3,2},{4,5},{5,4},{6,7},{7,6},{8,9},{9,8},{10,11... | collective-permute-start | bytes 479240 | tf_op jit(solution)/shard_map/ppermute | solution.py:709
  71.0 7.6 %attend_next.1 = (bf16[384,768]{1,0:T(8,128)(2,1)}, bf16[768,384]{1,0:T(8,128)(2,1)}, bf16[208,384]{1,0:T(8,128)(2,1)}) custom-call(s32[1]{0:T(128)} %bitcast.3.half_ref, bf16[384,768]{1,0:T(8,128)(2,1)} %copy-done.3, bf16[768,768]{1,0:T(8,128)(2,1)} %get-tuple-element.33.x_ref, bf16[768,1536]{1,0:T(8,128)(2,1)} %weight_hbm.5, bf16[16,384,768]{2,1,0:T(8,128)(2,1)} %bias_hbm.7), custom_call_target="tpu_custom_call" | custom-call | flops 4000000000 | bytes 4000000 | tf_op jit(solution)/shard_map/attend_next/pallas_call | solution.py:560
  78.7 0.7 copy-done.16
  79.3 5.7 %attend_keep.2 = (f32[192,384]{1,0:T(8,128)}, f32[192,128]{1,0:T(8,128)}, bf16[208,384]{1,0:T(8,128)(2,1)}) custom-call(s32[1]{0:T(128)} %bitcast.2.half_ref, bf16[384,768]{1,0:T(8,128)(2,1)} %copy-done.3, bf16[384,768]{1,0:T(8,128)(2,1)} %get-tuple-element.27.k_ref, bf16[768,384]{1,0:T(8,128)(2,1)} %get-tuple-element.28.v_ref, bf16[208,384]{1,0:T(8,128)(2,1)} %copy-done.16, ...), custom_call_target="tpu_custom_call" | custom-call | flops 4000000000 | bytes 4000000 | tf_op jit(solution)/shard_map/attend_keep/pallas_call | solution.py:560
  85.0 7.2 %collective-permute-start.10 = (bf16[208,384]{1,0:T(8,128)(2,1)}, bf16[208,384]{1,0:T(8,128)(2,1)S(1)}, u32[]{:S(2)}, u32[]{:S(2)}) collective-permute-start(bf16[208,384]{1,0:T(8,128)(2,1)} %get-tuple-element.32), channel_id=1, source_target_pairs={{0,3},{1,2},{2,1},{3,0},{4,7},{5,6},{6,5},{7,4},{8,11},{9,10},{10,... | collective-permute-start | bytes 479240 | tf_op jit(solution)/shard_map/ppermute | solution.py:703
  92.2 0.7 copy-done.15
  92.8 6.0 %attend_keep.3 = (f32[192,384]{1,0:T(8,128)}, f32[192,128]{1,0:T(8,128)}, bf16[208,384]{1,0:T(8,128)(2,1)}) custom-call(s32[1]{0:T(128)} %bitcast.2.half_ref, bf16[384,768]{1,0:T(8,128)(2,1)} %copy-done.3, bf16[384,768]{1,0:T(8,128)(2,1)} %get-tuple-element.34.k_ref, bf16[768,384]{1,0:T(8,128)(2,1)} %get-tuple-element.35.v_ref, bf16[208,384]{1,0:T(8,128)(2,1)} %copy-done.15, ...), custom_call_target="tpu_custom_call" | custom-call | flops 4000000000 | bytes 4000000 | tf_op jit(solution)/shard_map/attend_keep/pallas_call | solution.py:560
  99.9 8.1 %collective-permute-done.12.msg_ref = bf16[208,384]{1,0:T(8,128)(2,1)S(1)} collective-permute-done((bf16[208,384]{1,0:T(8,128)(2,1)}, bf16[208,384]{1,0:T(8,128)(2,1)S(1)}, u32[]{:S(2)}, u32[]{:S(2)}) %collective-permute-start.12) | collective-permute-done | bytes 159776 | tf_op jit(solution)/shard_map/ppermute | solution.py:703
  108.0 1.0 copy-done.5
  109.0 0.9 copy-done.7
  110.4 5.1 %collective-permute-done.14.other_b = bf16[192,384]{1,0:T(8,128)(2,1)S(1)} collective-permute-done((bf16[192,384]{1,0:T(8,128)(2,1)S(1)}, bf16[192,384]{1,0:T(8,128)(2,1)S(1)}, u32[]{:S(2)}, u32[]{:S(2)}) %collective-permute-start.14) | collective-permute-done | bytes 147488 | tf_op jit(solution)/shard_map/ppermute | solution.py:732
  115.5 1.6 %output_rows.1 = bf16[384,768]{1,0:T(8,128)(2,1)} custom-call(s32[1]{0:T(128)} %bitcast.2.half_ref, bf16[192,384]{1,0:T(8,128)(2,1)S(1)} %settle.2.own_a, bf16[192,384]{1,0:T(8,128)(2,1)S(1)} %settle.3.own_b, bf16[192,384]{1,0:T(8,128)(2,1)S(1)} %collective-permute-done.13.other_a, bf16[192,384]{1,0:T(8,128)(2,1)S(1)} %collective-permute-done.14.other_b, ...), custom_call_target="tpu_custom_call" | custom-call | tf_op jit(solution)/shard_map/output_rows/pallas_call | solution.py:621
  (54 shorter events, 3.8 us)
Async XLA Ops:
  1.4 4.3 %collective-permute-start.1 = (bf16[64,128]{1,0:T(8,128)(2,1)S(1)}, bf16[64,128]{1,0:T(8,128)(2,1)S(1)}, u32[]{:S(2)}, u32[]{:S(2)}) collective-permute-start(bf16[64,128]{1,0:T(8,128)(2,1)S(1)} %get-tuple-element.40), channel_id=1, source_target_pairs={{4,0},{8,4},{12,8},{16,12},{20,16},{24,20},{28,24},{5,1},{9,5},{13... | collective-permute-start | bytes 49160 | tf_op jit(solution)/shard_map/ppermute | solution.py:684
  2.7 3.9 %collective-permute-start = (bf16[64,128]{1,0:T(8,128)(2,1)S(1)}, bf16[64,128]{1,0:T(8,128)(2,1)S(1)}, u32[]{:S(2)}, u32[]{:S(2)}) collective-permute-start(bf16[64,128]{1,0:T(8,128)(2,1)S(1)} %get-tuple-element.41), channel_id=1, source_target_pairs={{0,4},{4,8},{8,12},{12,16},{16,20},{20,24},{24,28},{1,5},{5,9},{9,... | collective-permute-start | bytes 49160 | tf_op jit(solution)/shard_map/ppermute | solution.py:683
  5.7 0.8 copy-start.17
  7.1 23.2 %copy-start.2 = (bf16[128,768]{1,0:T(8,128)(2,1)S(1)}, bf16[128,768]{1,0:T(8,128)(2,1)}, u32[]{:S(2)}) copy-start(bf16[128,768]{1,0:T(8,128)(2,1)} %weight_ref.8) | copy-start | bytes 589828
  7.1 23.2 %copy-start.9 = (s32[3072]{0:T(1024)S(1)}, s32[3072]{0:T(1024)}, u32[]{:S(2)}) copy-start(s32[3072]{0:T(1024)} %param.19) | copy-start | bytes 36868
  25.8 8.6 %collective-permute-start.2 = (bf16[400,128]{1,0:T(8,128)(2,1)}, bf16[400,128]{1,0:T(8,128)(2,1)S(1)}, u32[]{:S(2)}, u32[]{:S(2)}) collective-permute-start(bf16[400,128]{1,0:T(8,128)(2,1)} %get-tuple-element.22), channel_id=1, source_target_pairs={{0,4},{4,8},{8,12},{12,16},{16,20},{20,24},{24,28},{1,5},{5,9},{9,... | collective-permute-start | bytes 307208 | tf_op jit(solution)/shard_map/ppermute | solution.py:689
  30.4 1.1 copy-start.10
  35.1 9.2 %collective-permute-start.5 = (bf16[384,384]{1,0:T(8,128)(2,1)S(1)}, bf16[384,384]{1,0:T(8,128)(2,1)S(1)}, u32[]{:S(2)}, u32[]{:S(2)}) collective-permute-start(bf16[384,384]{1,0:T(8,128)(2,1)S(1)} %token_finish.3.b_ref), channel_id=1, source_target_pairs={{0,8},{9,1},{18,26},{27,19},{4,20},{13,29},{22,6},{31,15}} | collective-permute-start | bytes 884744 | tf_op jit(solution)/shard_map/ppermute | solution.py:655
  42.4 13.1 %copy-start.1 = (bf16[768,768]{1,0:T(8,128)(2,1)S(1)}, bf16[768,768]{1,0:T(8,128)(2,1)}, u32[]{:S(2)}) copy-start(bf16[768,768]{1,0:T(8,128)(2,1)} %weight_hbm.3) | copy-start | bytes 3538948
  42.4 13.1 %copy-start.8 = (f32[768]{0:T(1024)S(1)}, f32[768]{0:T(1024)}, u32[]{:S(2)}) copy-start(f32[768]{0:T(1024)} %gain_ref.5) | copy-start | bytes 9220
  43.0 6.3 %collective-permute-start.3 = (bf16[384,384]{1,0:T(8,128)(2,1)S(1)}, bf16[384,384]{1,0:T(8,128)(2,1)S(1)}, u32[]{:S(2)}, u32[]{:S(2)}) collective-permute-start(bf16[384,384]{1,0:T(8,128)(2,1)S(1)} %token_finish.2.a_ref), channel_id=1, source_target_pairs={{0,8},{9,1},{18,26},{27,19},{4,20},{13,29},{22,6},{31,15}} | collective-permute-start | bytes 884744 | tf_op jit(solution)/shard_map/ppermute | solution.py:655
  44.4 7.8 %collective-permute-start.6 = (bf16[384,384]{1,0:T(8,128)(2,1)S(1)}, bf16[384,384]{1,0:T(8,128)(2,1)S(1)}, u32[]{:S(2)}, u32[]{:S(2)}) collective-permute-start(bf16[384,384]{1,0:T(8,128)(2,1)S(1)} %broadcast_select_fusion), channel_id=1, source_target_pairs={{0,16},{8,24},{1,17},{9,25},{18,2},{26,10},{19,3},{27,11},{4,12},{... | collective-permute-start | bytes 884744 | tf_op jit(solution)/shard_map/ppermute | solution.py:655
  49.2 6.0 %collective-permute-start.4 = (bf16[384,384]{1,0:T(8,128)(2,1)S(1)}, bf16[384,384]{1,0:T(8,128)(2,1)S(1)}, u32[]{:S(2)}, u32[]{:S(2)}) collective-permute-start(bf16[384,384]{1,0:T(8,128)(2,1)S(1)} %broadcast_select_fusion.1), channel_id=1, source_target_pairs={{0,16},{8,24},{1,17},{9,25},{18,2},{26,10},{19,3},{27,11},{4,12},{... | collective-permute-start | bytes 884744 | tf_op jit(solution)/shard_map/ppermute | solution.py:655
  52.2 5.6 %copy-start.11 = (bf16[384,384]{1,0:T(8,128)(2,1)}, bf16[384,384]{1,0:T(8,128)(2,1)S(1)}, u32[]{:S(2)}) copy-start(bf16[384,384]{1,0:T(8,128)(2,1)S(1)} %broadcast_select_fusion.2.own_b) | copy-start | bytes 884740
  52.2 5.5 %collective-permute-start.8 = (bf16[384,384]{1,0:T(8,128)(2,1)S(1)}, bf16[384,384]{1,0:T(8,128)(2,1)S(1)}, u32[]{:S(2)}, u32[]{:S(2)}) collective-permute-start(bf16[384,384]{1,0:T(8,128)(2,1)S(1)} %broadcast_select_fusion.2.own_b), channel_id=1, source_target_pairs={{0,4},{4,0},{8,12},{12,8},{16,20},{20,16},{24,28},{28,24},{1,5},{5... | collective-permute-start | bytes 884744 | tf_op jit(solution)/shard_map/ppermute | solution.py:656
  55.3 2.4 %copy-start.12 = (bf16[384,384]{1,0:T(8,128)(2,1)}, bf16[384,384]{1,0:T(8,128)(2,1)S(1)}, u32[]{:S(2)}) copy-start(bf16[384,384]{1,0:T(8,128)(2,1)S(1)} %broadcast_select_fusion.3.own_a) | copy-start | bytes 884740
  55.3 2.4 %collective-permute-start.7 = (bf16[384,384]{1,0:T(8,128)(2,1)S(1)}, bf16[384,384]{1,0:T(8,128)(2,1)S(1)}, u32[]{:S(2)}, u32[]{:S(2)}) collective-permute-start(bf16[384,384]{1,0:T(8,128)(2,1)S(1)} %broadcast_select_fusion.3.own_a), channel_id=1, source_target_pairs={{0,4},{4,0},{8,12},{12,8},{16,20},{20,16},{24,28},{28,24},{1,5},{5... | collective-permute-start | bytes 884744 | tf_op jit(solution)/shard_map/ppermute | solution.py:656
  56.9 0.8 copy-start.3
  57.7 0.7 copy-start.13
  57.7 0.8 copy-start.14
  65.9 12.7 %collective-permute-start.9 = (bf16[208,384]{1,0:T(8,128)(2,1)}, bf16[208,384]{1,0:T(8,128)(2,1)S(1)}, u32[]{:S(2)}, u32[]{:S(2)}) collective-permute-start(bf16[208,384]{1,0:T(8,128)(2,1)} %get-tuple-element.29), channel_id=1, source_target_pairs={{0,1},{1,0},{2,3},{3,2},{4,5},{5,4},{6,7},{7,6},{8,9},{9,8},{10,11... | collective-permute-start | bytes 479240 | tf_op jit(solution)/shard_map/ppermute | solution.py:709
  78.6 13.6 %collective-permute-start.11 = (bf16[208,384]{1,0:T(8,128)(2,1)}, bf16[208,384]{1,0:T(8,128)(2,1)S(1)}, u32[]{:S(2)}, u32[]{:S(2)}) collective-permute-start(bf16[208,384]{1,0:T(8,128)(2,1)} %get-tuple-element.36), channel_id=1, source_target_pairs={{0,1},{1,0},{2,3},{3,2},{4,5},{5,4},{6,7},{7,6},{8,9},{9,8},{10,11... | collective-permute-start | bytes 479240 | tf_op jit(solution)/shard_map/ppermute | solution.py:716
  78.6 0.7 copy-start.16
  85.0 14.0 %collective-permute-start.10 = (bf16[208,384]{1,0:T(8,128)(2,1)}, bf16[208,384]{1,0:T(8,128)(2,1)S(1)}, u32[]{:S(2)}, u32[]{:S(2)}) collective-permute-start(bf16[208,384]{1,0:T(8,128)(2,1)} %get-tuple-element.32), channel_id=1, source_target_pairs={{0,3},{1,2},{2,1},{3,0},{4,7},{5,6},{6,5},{7,4},{8,11},{9,10},{10,... | collective-permute-start | bytes 479240 | tf_op jit(solution)/shard_map/ppermute | solution.py:703
  92.8 6.2 %copy-start.4 = (f32[192,384]{1,0:T(8,128)S(1)}, f32[192,384]{1,0:T(8,128)}, u32[]{:S(2)}) copy-start(f32[192,384]{1,0:T(8,128)} %get-tuple-element.30.o_ref) | copy-start | bytes 884740
  92.8 6.2 %copy-start.6 = (f32[192,128]{1,0:T(8,128)S(1)}, f32[192,128]{1,0:T(8,128)}, u32[]{:S(2)}) copy-start(f32[192,128]{1,0:T(8,128)} %get-tuple-element.31.lse_ref) | copy-start | bytes 294916
  92.8 22.7 %copy-start = (bf16[768,768]{1,0:T(8,128)(2,1)S(1)}, bf16[768,768]{1,0:T(8,128)(2,1)}, u32[]{:S(2)}) copy-start(bf16[768,768]{1,0:T(8,128)(2,1)} %weight_ref.9) | copy-start | bytes 3538948
  98.9 9.1 %collective-permute-start.12 = (bf16[208,384]{1,0:T(8,128)(2,1)}, bf16[208,384]{1,0:T(8,128)(2,1)S(1)}, u32[]{:S(2)}, u32[]{:S(2)}) collective-permute-start(bf16[208,384]{1,0:T(8,128)(2,1)} %get-tuple-element.39), channel_id=1, source_target_pairs={{0,3},{1,2},{2,1},{3,0},{4,7},{5,6},{6,5},{7,4},{8,11},{9,10},{10,... | collective-permute-start | bytes 479240 | tf_op jit(solution)/shard_map/ppermute | solution.py:703
  99.5 10.9 %collective-permute-start.13 = (bf16[192,384]{1,0:T(8,128)(2,1)S(1)}, bf16[192,384]{1,0:T(8,128)(2,1)S(1)}, u32[]{:S(2)}, u32[]{:S(2)}) collective-permute-start(bf16[192,384]{1,0:T(8,128)(2,1)S(1)} %settle.2.own_a), channel_id=1, source_target_pairs={{0,1},{1,0},{2,3},{3,2},{4,5},{5,4},{6,7},{7,6},{8,9},{9,8},{10,11... | collective-permute-start | bytes 442376 | tf_op jit(solution)/shard_map/ppermute | solution.py:732
  108.0 1.0 copy-start.5
  109.0 0.9 copy-start.7
  110.3 5.2 %collective-permute-start.14 = (bf16[192,384]{1,0:T(8,128)(2,1)S(1)}, bf16[192,384]{1,0:T(8,128)(2,1)S(1)}, u32[]{:S(2)}, u32[]{:S(2)}) collective-permute-start(bf16[192,384]{1,0:T(8,128)(2,1)S(1)} %settle.3.own_b), channel_id=1, source_target_pairs={{0,1},{1,0},{2,3},{3,2},{4,5},{5,4},{6,7},{7,6},{8,9},{9,8},{10,11... | collective-permute-start | bytes 442376 | tf_op jit(solution)/shard_map/ppermute | solution.py:732
  (2 other events, 1.3 us)
where the time goes:
time: 118 us; the launch traced here: 117 us
  Pallas kernels  56.4 us (48%)
  starting transfers between devices  31.5 us (27%)
  waiting for transfers between devices  20.7 us (18%)
  local copies, waits for them, and re-layouts  7.27 us (6%)
    pallas_call x4, Pallas kernels, group_call(): pl.pallas_call(functools.partial(kernel, heads, feats // heads), grid_spe...  26.6 us
    pallas_call x1, Pallas kernels, atom_attention(): pl.pallas_call(functools.partial(atom_kernel, chunks, atom_total, tok_row...  18.7 us
    ppermute x4, starting transfers between devices, key_parts(): lax.ppermute(part, ('pb', 'ka'), pairs)  9.57 us
    ppermute x2, waiting for transfers between devices, far(): return lax.ppermute(msg, 'ka', [(i, i ^ 2 * bit - 1) for i in range(n_ka)])  8.08 us
    ppermute x2, starting transfers between devices, far(): return lax.ppermute(msg, 'ka', [(i, i ^ 2 * bit - 1) for i in range(n_ka)])  7.24 us
    ppermute x4, waiting for transfers between devices, key_parts(): lax.ppermute(part, ('pb', 'ka'), pairs)  6.72 us
    unnamed x38, local copies, waits for them, and re-layouts  6.53 us
    pallas_call x2, Pallas kernels, pool(): pl.pallas_call(functools.partial(pool_kernel, tok_rows), grid_spec=pltpu....  5.97 us
  transfers between devices with their start and end apart: 15, of which 6 were waited for; matrix products, arithmetic and copies ran while one was open for 0% of the time, Pallas kernels for 24%

commit v1 on v0

--- a/solution.py
+++ b/solution.py
@@ -58,7 +58,6 @@
     q_s,
     k_s,
     v_s,
-    mix_s,
     x_s,
 ):
     step = pl.program_id(0)
@@ -87,7 +86,7 @@
             v_s[at, width:] = jnp.ones((tile, width), BF16)
             return carry
 
-        lax.fori_loop(0, total // tile, one, 0)
+        lax.fori_loop(0, total // tile, one, 0, unroll=True)
 
     group = WIN_K // WIN_Q
     atoms_group = group * WIN_Q
@@ -101,10 +100,12 @@
     def region(n):
         return pl.ds(pl.multiple_of(step * size + n // group * atoms_group, atoms_group), 2 * WIN_K)
 
-    def score(n):
-        query = q_s[pl.ds(pl.multiple_of(step * size + n * WIN_Q + half, WIN_Q), WIN_Q), :].astype(F32)
-        stacked = jnp.concatenate([jnp.where(m, query, 0.0).astype(BF16) for m in heads], axis=0)
-        return dot(stacked, k_s[:, region(n)])
+    def score(g):
+        query = q_s[pl.ds(pl.multiple_of(step * size + g * atoms_group + half, half), atoms_group), :].astype(F32)
+        stacked = [
+            jnp.where(m, query[i * WIN_Q : (i + 1) * WIN_Q], 0.0).astype(BF16) for i in range(group) for m in heads
+        ]
+        return dot(jnp.concatenate(stacked, axis=0), k_s[:, region(g * group)])
 
     def soften(n, scores):
         offset = n % group * WIN_Q + half + shift_ref[step * blocks + n]
@@ -122,35 +123,33 @@
             [jnp.where(early, terms, 0.0).astype(BF16), jnp.where(early, 0.0, terms).astype(BF16)], axis=1
         )
 
-    def mix(n, weights):
-        mixed = dot(weights, v_s[region(n), :])
-        values, total = mixed[:WIN_Q, :width], mixed[:WIN_Q, width:]
-        for h in range(1, AH):
-            part = mixed[h * WIN_Q : (h + 1) * WIN_Q]
-            values = jnp.where(heads[h], part[:, :width], values)
-            total = jnp.where(heads[h], part[:, width:], total)
-        mix_s[n * WIN_Q : (n + 1) * WIN_Q, :] = (values / total).astype(BF16)
-
-    def project_out(g):
+    def mix(g, weights):
+        mixed = dot(jnp.concatenate(weights, axis=0), v_s[region(g * group), :])
+        merged = []
+        for i in range(group):
+            parts = [mixed[(i * AH + h) * WIN_Q : (i * AH + h + 1) * WIN_Q] for h in range(AH)]
+            values, total = parts[0][:, :width], parts[0][:, width:]
+            for h in range(1, AH):
+                values = jnp.where(heads[h], parts[h][:, :width], values)
+                total = jnp.where(heads[h], parts[h][:, width:], total)
+            merged.append((values / total).astype(BF16))
         local = g * atoms_group
         at = pl.multiple_of(step * size + local, atoms_group)
         own = atoms_ref[pl.ds(at, atoms_group), :].astype(F32)
-        result = own + dot(mix_s[local : local + atoms_group, :], proj_ref[...])
+        result = own + dot(jnp.concatenate(merged, axis=0), proj_ref[...])
         out_ref[local : local + atoms_group, :] = result.astype(BF16)
 
+    groups = blocks // group
     ahead = score(0)
     behind = None
-    for n in range(blocks):
+    for g in range(groups):
         scores = ahead
-        if n + 1 < blocks:
-            ahead = score(n + 1)
-        if n:
-            mix(n - 1, behind)
-        behind = soften(n, scores)
-        if n % group == 0 and n:
-            project_out(n // group - 1)
-    mix(blocks - 1, behind)
-    project_out(blocks // group - 1)
+        if g + 1 < groups:
+            ahead = score(g + 1)
+        if g:
+            mix(g - 1, behind)
+        behind = [soften(g * group + i, scores[i * span : (i + 1) * span]) for i in range(group)]
+    mix(groups - 1, behind)
 
     @pl.when(step == chunks - 1)
     def _():
@@ -190,7 +189,6 @@
                 pltpu.VMEM((rows + 2 * half, width), BF16),
                 pltpu.VMEM((width, rows + 2 * half), BF16),
                 pltpu.VMEM((rows + 2 * half, 2 * width), BF16),
-                pltpu.VMEM((size, width), BF16),
                 pltpu.VMEM((rows + 2 * half, width), BF16),
             ],
         ),
@@ -223,16 +221,16 @@
         ones.append(jnp.where(token == ids, 1.0, 0.0))
     hot = jnp.concatenate(ones, axis=1).astype(BF16)
     count = functools.reduce(jnp.add, ones)
-    part = dot(hot, hidden)
+    more = dot(hot, hidden)
 
     @pl.when(step == 0)
     def _():
-        sum_ref[...] = part
+        sum_ref[...] = more
         cnt_ref[...] = count
 
     @pl.when(step > 0)
     def _():
-        sum_ref[...] += part
+        sum_ref[...] += more
         cnt_ref[...] += count
 
 
@@ -310,7 +308,7 @@
     rows = halves[0].shape[0]
     return pl.pallas_call(
         functools.partial(query_kernel, 1.0 / math.sqrt(weight.shape[1] // TH)),
-        in_specs=[pl.BlockSpec(memory_space=pltpu.VMEM)] * 3 + [pl.BlockSpec(memory_space=pltpu.HBM)],
+        in_specs=[pl.BlockSpec(memory_space=pltpu.VMEM)] * 3 + [pl.BlockSpec(memory_space=pl.ANY)],
         out_shape=jax.ShapeDtypeStruct((rows, weight.shape[1]), BF16),
         scratch_shapes=[pltpu.VMEM(weight.shape, BF16), pltpu.SemaphoreType.DMA],
         compiler_params=params(VMEM_SMALL),
@@ -360,8 +358,8 @@
     return other + wide * (mixed - other), top + jnp.log(total)
 
 
-def attend_group(group, heads, width, half, q_ref, k_ref, v_ref, bias_hbm, scratch):
-    score_s, term_s, top_s, bias_s, mix_s, sems = scratch
+def attend_group(group, heads, width, half, q_ref, k_ref, v_ref, bias_ref, scratch):
+    score_s, term_s, top_s, mix_s = scratch
     rows = mix_s.shape[0]
     at = pl.multiple_of(half * rows, rows)
     pairs = heads // 2
@@ -392,7 +390,8 @@
 
     def soften(p, n):
         for r in range(n * tiles // chunks * ROW_TILE, (n + 1) * tiles // chunks * ROW_TILE, ROW_TILE):
-            bias = bias_s[2 * p + r // rows, r % rows : r % rows + ROW_TILE, :].astype(F32)
+            line = pl.multiple_of(at + r % rows, ROW_TILE)
+            bias = bias_ref[group * heads + 2 * p + r // rows, pl.ds(line, ROW_TILE), :].astype(F32)
             scores = score_s[p % 2][r : r + ROW_TILE, :] + bias
             top = jnp.max(scores, axis=-1, keepdims=True)
             term_s[p % 2][r : r + ROW_TILE, :] = jnp.exp(scores - top).astype(BF16)
@@ -420,16 +419,11 @@
         mix_s[:, window] = result
         return lse
 
-    copies = bias_copies(group, heads, half, bias_hbm, bias_s, sems)
     lse = jnp.zeros((rows, LANES), F32)
     stacked = stack(0)
     for n in range(chunks):
         score(0, n, stacked)
-    copies[0].wait()
     for p in range(pairs):
-        if p == 1:
-            for copy in copies[1:]:
-                copy.wait()
         mixed = None
         if p + 1 < pairs:
             stacked = stack(p + 1)
@@ -448,19 +442,6 @@
     return mix_s[...], lse
 
 
-def bias_copies(group, heads, half, bias_hbm, bias_s, sems):
-    rows = bias_s.shape[1]
-    at = pl.multiple_of(half * rows, rows)
-    return [
-        pltpu.make_async_copy(
-            bias_hbm.at[pl.ds(group * heads + 2 * p, 2), pl.ds(at, rows), :],
-            bias_s.at[pl.ds(2 * p, 2)],
-            sems.at[p],
-        )
-        for p in range(heads // 2)
-    ]
-
-
 def group_scratch(rows, keys, feats, heads):
     return [
         pltpu.VMEM((2 * rows, keys), F32),
@@ -469,20 +450,18 @@
         pltpu.VMEM((2 * rows, keys), BF16),
         pltpu.VMEM((2 * rows, LANES), F32),
         pltpu.VMEM((2 * rows, LANES), F32),
-        pltpu.VMEM((heads, rows, keys), BF16),
         pltpu.VMEM((rows, feats), F32),
-        pltpu.SemaphoreType.DMA((heads // 2,)),
         pltpu.VMEM((2, 2 * feats, feats), BF16),
         pltpu.SemaphoreType.DMA((2,)),
     ]
 
 
 def scratch_of(refs):
-    return refs[:2], refs[2:4], refs[4:6], refs[6], refs[7], refs[8]
+    return refs[:2], refs[2:4], refs[4:6], refs[6]
 
 
 def weight_copies(group, weight_hbm, refs):
-    weight_s, sems = refs[9:11]
+    weight_s, sems = refs[7:9]
     feats = weight_s.shape[2]
     return [
         pltpu.make_async_copy(
@@ -503,12 +482,10 @@
 
 
 def first_kernel(heads, width, half_ref, core_ref, q_ref, own_a, own_b, other_a, other_b, gain_ref, weight_hbm,
-                 bias_hbm, x_ref, k_ref, v_ref, msg_ref, *refs):
+                 bias_ref, x_ref, k_ref, v_ref, msg_ref, *refs):
     scratch = scratch_of(refs)
     weights = weight_copies(0, weight_hbm, refs)
     for copy in weights:
-        copy.start()
-    for copy in bias_copies(0, heads, half_ref[0], bias_hbm, scratch[3], scratch[5]):
         copy.start()
     rows = own_a.shape[0]
     core = core_ref[0]
@@ -516,28 +493,24 @@
     for place, parts in ((core, (own_a, own_b)), (1 - core, (other_a, other_b))):
         values = jnp.concatenate([part[...].astype(F32) for part in parts], axis=1)
         x_ref[pl.ds(pl.multiple_of(place * rows, rows), rows), :] = norm_rows(values, gain).astype(BF16)
-    project_keys(x_ref, refs[9], weights, k_ref, v_ref)
-    mixed, lse = attend_group(0, heads, width, half_ref[0], q_ref, k_ref, v_ref, bias_hbm, scratch)
+    project_keys(x_ref, refs[7], weights, k_ref, v_ref)
+    mixed, lse = attend_group(0, heads, width, half_ref[0], q_ref, k_ref, v_ref, bias_ref, scratch)
     msg_ref[...] = pack_message(mixed, lse, heads)
 
 
-def next_kernel(group, heads, width, half_ref, q_ref, x_ref, weight_hbm, bias_hbm, k_ref, v_ref, msg_ref, *refs):
+def next_kernel(group, heads, width, half_ref, q_ref, x_ref, weight_hbm, bias_ref, k_ref, v_ref, msg_ref, *refs):
     scratch = scratch_of(refs)
     weights = weight_copies(group, weight_hbm, refs)
     for copy in weights:
         copy.start()
-    for copy in bias_copies(group, heads, half_ref[0], bias_hbm, scratch[3], scratch[5]):
-        copy.start()
-    project_keys(x_ref, refs[9], weights, k_ref, v_ref)
-    mixed, lse = attend_group(group, heads, width, half_ref[0], q_ref, k_ref, v_ref, bias_hbm, scratch)
+    project_keys(x_ref, refs[7], weights, k_ref, v_ref)
+    mixed, lse = attend_group(group, heads, width, half_ref[0], q_ref, k_ref, v_ref, bias_ref, scratch)
     msg_ref[...] = pack_message(mixed, lse, heads)
 
 
-def keep_kernel(group, heads, width, half_ref, q_ref, k_ref, v_ref, near_ref, bias_hbm, o_ref, lse_ref, msg_ref, *refs):
+def keep_kernel(group, heads, width, half_ref, q_ref, k_ref, v_ref, near_ref, bias_ref, o_ref, lse_ref, msg_ref, *refs):
     scratch = scratch_of(refs)
-    for copy in bias_copies(group, heads, half_ref[0], bias_hbm, scratch[3], scratch[5]):
-        copy.start()
-    mixed, lse = attend_group(group, heads, width, half_ref[0], q_ref, k_ref, v_ref, bias_hbm, scratch)
+    mixed, lse = attend_group(group, heads, width, half_ref[0], q_ref, k_ref, v_ref, bias_ref, scratch)
     rows = mixed.shape[0]
     mixed, lse = merge_parts(mixed, lse, *unpack_message(near_ref[...], rows, heads), heads)
     o_ref[...] = mixed
@@ -564,12 +537,13 @@
             grid=(1,),
             in_specs=[pl.BlockSpec((tok_rows, feats), lambda i, *_: (0, group))]
             + [full(array.shape) for array in arrays]
-            + [pl.BlockSpec(memory_space=pltpu.HBM)] * (1 if weights is None else 2),
+            + [pl.BlockSpec(memory_space=pl.ANY)] * (0 if weights is None else 1)
+            + [pl.BlockSpec(memory_space=pltpu.VMEM)],
             out_specs=[full(shapes[out][0]) for out in outs],
             scratch_shapes=group_scratch(rows, keys, feats, heads),
         ),
         out_shape=[jax.ShapeDtypeStruct(*shapes[out]) for out in outs],
-        compiler_params=params(),
+        compiler_params=params(VMEM_SMALL),
         cost_estimate=pl.CostEstimate(flops=4 * 10**9, bytes_accessed=4 * 10**6, transcendentals=10**6),
         name=name,
     )(half, *scalars, q, *arrays, *([] if weights is None else [weights]), bias)
@@ -687,10 +661,11 @@
         atom_bias, tok2d, tok_rows, rows * n_pb,
     )
     behind = lax.ppermute(msg, "pb", up)
-    token_repr, own_keys, other_keys = [], [], []
+    token_repr = []
     for part in range(PARTS):
         sums, counts = pool(pos, atom_out, agg_weight, tok2d, tok_rows, part)
         token_repr.append(finish(behind, agg_weight, sums, counts, part))
+    late_bias, token_repr[0] = lax.optimization_barrier((pair_bias, token_repr[0]))
     own_keys, other_keys = key_parts(token_repr)
     queries = project_queries(token_repr, token_gain, token_q)
     parity = jnp.bitwise_and(plane ^ (plane >> 1), 1).astype(jnp.int32)
@@ -704,13 +679,13 @@
 
     x, k, v, msg = group_call(
         first_kernel, 0, send, (core.reshape(1),), queries, (*own_keys, *other_keys, token_gain), token_kv,
-        pair_bias, ("x", "k", "v", "msg"), "attend_first",
+        late_bias, ("x", "k", "v", "msg"), "attend_first",
     )
     held, near = [(k, v)], [lax.ppermute(msg, "ka", swap)]
     for g in range(1, GROUPS):
         k, v, msg = group_call(
             functools.partial(next_kernel, g), g, send, (), queries, (x,), token_kv,
-            pair_bias, ("k", "v", "msg"), "attend_next",
+            late_bias, ("k", "v", "msg"), "attend_next",
         )
         held.append((k, v))
         near.append(lax.ppermute(msg, "ka", swap))
@@ -718,7 +693,7 @@
     for g in range(GROUPS):
         o, lse, msg = group_call(
             functools.partial(keep_kernel, g), g, keep, (), queries, (*held[g], near[g]), None,
-            pair_bias, ("o", "lse", "msg"), "attend_keep",
+            late_bias, ("o", "lse", "msg"), "attend_keep",
         )
         sums.append((o, lse))
         gone.append(far(msg, bits[0]))

time: 118 us -> 113 us (0.958)
  Pallas kernels: 56.4 us -> 42.1 us
  local copies, waits for them, and re-layouts: 7.27 us -> 17.3 us
    pallas_call x4, Pallas kernels: 26.6 us -> 13.7 us  [group_call(): pl.pallas_call(functools.partial(kernel, heads, feats // heads), grid_spe...]
    unnamed x38 -> x26, local copies, waits for them, and re-layouts: 6.53 us -> 16.6 us
    pallas_call x1, Pallas kernels: 18.7 us -> 17.4 us  [atom_attention(): pl.pallas_call(functools.partial(atom_kernel, chunks, atom_total, tok_row...]
  transfers between devices with their start and end apart: 15 -> 15, of which waited for: 6 -> 7; matrix products, arithmetic and copies ran while one was open for 0% -> 0% of each run, Pallas kernels for 24% -> 16%
where the time goes in v1:
time: 113 us
  Pallas kernels  42.1 us (37%)
  starting transfers between devices  32.1 us (28%)
  waiting for transfers between devices  20.1 us (18%)
  local copies, waits for them, and re-layouts  17.3 us (15%)
    pallas_call x1, Pallas kernels, atom_attention(): pl.pallas_call(functools.partial(atom_kernel, chunks, atom_total, tok_row...  17.4 us
    unnamed x26, local copies, waits for them, and re-layouts  16.6 us
    pallas_call x4, Pallas kernels, group_call(): pl.pallas_call(functools.partial(kernel, heads, feats // heads), grid_spe...  13.7 us
    ppermute x4, starting transfers between devices, key_parts(): lax.ppermute(part, ('pb', 'ka'), pairs)  9.75 us
    ppermute x2, waiting for transfers between devices, far(): return lax.ppermute(msg, 'ka', [(i, i ^ 2 * bit - 1) for i in range(n_ka)])  7.4 us
    ppermute x2, starting transfers between devices, far(): return lax.ppermute(msg, 'ka', [(i, i ^ 2 * bit - 1) for i in range(n_ka)])  7.21 us
    ppermute x4, waiting for transfers between devices, key_parts(): lax.ppermute(part, ('pb', 'ka'), pairs)  6.55 us
    pallas_call x2, Pallas kernels, pool(): pl.pallas_call(functools.partial(pool_kernel, tok_rows), grid_spec=pltpu....  5.97 us
  transfers between devices with their start and end apart: 15, of which 7 were waited for; matrix products, arithmetic and copies ran while one was open for 0% of the time, Pallas kernels for 16%

profile of v1, /device:TPU:0, one launch (start us, length us, event | category | flops | bytes accessed | tf_op | source)
XLA Modules:
  0.0 112.8 jit_solution(15987543598381425829)
XLA Ops:
  0.6 0.7 fusion
  1.4 1.3 %collective-permute-start.1 = (bf16[64,128]{1,0:T(8,128)(2,1)S(1)}, bf16[64,128]{1,0:T(8,128)(2,1)S(1)}, u32[]{:S(2)}, u32[]{:S(2)}) collective-permute-start(bf16[64,128]{1,0:T(8,128)(2,1)S(1)} %get-tuple-element.44), channel_id=1, source_target_pairs={{4,0},{8,4},{12,8},{16,12},{20,16},{24,20},{28,24},{5,1},{9,5},{13... | collective-permute-start | bytes 49160 | tf_op jit(solution)/shard_map/ppermute | solution.py:658
  2.7 3.0 %collective-permute-start = (bf16[64,128]{1,0:T(8,128)(2,1)S(1)}, bf16[64,128]{1,0:T(8,128)(2,1)S(1)}, u32[]{:S(2)}, u32[]{:S(2)}) collective-permute-start(bf16[64,128]{1,0:T(8,128)(2,1)S(1)} %get-tuple-element.45), channel_id=1, source_target_pairs={{0,4},{4,8},{8,12},{12,16},{16,20},{20,24},{24,28},{1,5},{5,9},{9,... | collective-permute-start | bytes 49160 | tf_op jit(solution)/shard_map/ppermute | solution.py:657
  5.7 0.8 collective-permute-done.left_ref
  6.5 0.6 copy-done.12
  7.1 17.4 %atom_attention.1 = (bf16[3072,128]{1,0:T(8,128)(2,1)}, bf16[400,128]{1,0:T(8,128)(2,1)}) custom-call(s32[96]{0:T(128)} %shift_ref.1, s32[1]{0:T(128)} %bitcast.pos_ref, bf16[3072,128]{1,0:T(8,128)(2,1)} %atoms_ref.1, bf16[64,128]{1,0:T(8,128)(2,1)} %copy-done.12, bf16[64,128]{1,0:T(8,128)(2,1)} %copy-done.11, f32[128]{0:T(128)} %gain_ref.3, ...), custom_call_target="tpu_custom_call" | custom-call | flops 8000000000 | bytes 6000000 | tf_op jit(solution)/shard_map/atom_attention/pallas_call | solution.py:169
  24.5 4.5 %collective-permute-start.2 = (bf16[400,128]{1,0:T(8,128)(2,1)}, bf16[400,128]{1,0:T(8,128)(2,1)S(1)}, u32[]{:S(2)}, u32[]{:S(2)}) collective-permute-start(bf16[400,128]{1,0:T(8,128)(2,1)} %get-tuple-element.24), channel_id=1, source_target_pairs={{0,4},{4,8},{8,12},{12,16},{16,20},{20,24},{24,28},{1,5},{5,9},{9,... | collective-permute-start | bytes 307208 | tf_op jit(solution)/shard_map/ppermute | solution.py:663
  29.1 1.1 copy-done.10
  30.2 3.0 %pool.3 = (f32[384,384]{1,0:T(8,128)S(1)}, f32[384,128]{1,0:T(8,128)S(1)}) custom-call(s32[1]{0:T(128)} %bitcast.pos_ref, bf16[3072,128]{1,0:T(8,128)(2,1)S(1)} %copy-done.10, bf16[128,768]{1,0:T(8,128)(2,1)S(1)} %copy-done.2, s32[24,128]{1,0:T(8,128)S(1)} %bitcast.6), custom_call_target="tpu_custom_call" | custom-call | flops 2000000000 | bytes 2000000 | tf_op jit(solution)/shard_map/pool/pallas_call | solution.py:241
  33.8 4.3 %collective-permute-start.5 = (bf16[384,384]{1,0:T(8,128)(2,1)S(1)}, bf16[384,384]{1,0:T(8,128)(2,1)S(1)}, u32[]{:S(2)}, u32[]{:S(2)}) collective-permute-start(bf16[384,384]{1,0:T(8,128)(2,1)S(1)} %token_finish.3.b_ref), channel_id=1, source_target_pairs={{0,8},{9,1},{18,26},{27,19},{4,20},{13,29},{22,6},{31,15}} | collective-permute-start | bytes 884744 | tf_op jit(solution)/shard_map/ppermute | solution.py:629
  38.0 3.0 %pool.2 = (f32[384,384]{1,0:T(8,128)S(1)}, f32[384,128]{1,0:T(8,128)S(1)}) custom-call(s32[1]{0:T(128)} %bitcast.pos_ref, bf16[3072,128]{1,0:T(8,128)(2,1)S(1)} %copy-done.10, bf16[128,768]{1,0:T(8,128)(2,1)S(1)} %copy-done.2, s32[24,128]{1,0:T(8,128)S(1)} %bitcast.7), custom_call_target="tpu_custom_call" | custom-call | flops 2000000000 | bytes 2000000 | tf_op jit(solution)/shard_map/pool/pallas_call | solution.py:241
  41.7 1.3 %collective-permute-start.3 = (bf16[384,384]{1,0:T(8,128)(2,1)S(1)}, bf16[384,384]{1,0:T(8,128)(2,1)S(1)}, u32[]{:S(2)}, u32[]{:S(2)}) collective-permute-start(bf16[384,384]{1,0:T(8,128)(2,1)S(1)} %token_finish.2.a_ref), channel_id=1, source_target_pairs={{0,8},{9,1},{18,26},{27,19},{4,20},{13,29},{22,6},{31,15}} | collective-permute-start | bytes 884744 | tf_op jit(solution)/shard_map/ppermute | solution.py:629
  43.1 2.7 %collective-permute-start.6 = (bf16[384,384]{1,0:T(8,128)(2,1)S(1)}, bf16[384,384]{1,0:T(8,128)(2,1)S(1)}, u32[]{:S(2)}, u32[]{:S(2)}) collective-permute-start(bf16[384,384]{1,0:T(8,128)(2,1)S(1)} %broadcast_select_fusion), channel_id=1, source_target_pairs={{0,16},{8,24},{1,17},{9,25},{18,2},{26,10},{19,3},{27,11},{4,12},{... | collective-permute-start | bytes 884744 | tf_op jit(solution)/shard_map/ppermute | solution.py:629
  45.8 2.1 %collective-permute-done.3 = bf16[384,384]{1,0:T(8,128)(2,1)S(1)} collective-permute-done((bf16[384,384]{1,0:T(8,128)(2,1)S(1)}, bf16[384,384]{1,0:T(8,128)(2,1)S(1)}, u32[]{:S(2)}, u32[]{:S(2)}) %collective-permute-start.3) | collective-permute-done | bytes 294944 | tf_op jit(solution)/shard_map/ppermute | solution.py:629
  47.9 1.5 %collective-permute-start.4 = (bf16[384,384]{1,0:T(8,128)(2,1)S(1)}, bf16[384,384]{1,0:T(8,128)(2,1)S(1)}, u32[]{:S(2)}, u32[]{:S(2)}) collective-permute-start(bf16[384,384]{1,0:T(8,128)(2,1)S(1)} %broadcast_select_fusion.1), channel_id=1, source_target_pairs={{0,16},{8,24},{1,17},{9,25},{18,2},{26,10},{19,3},{27,11},{4,12},{... | collective-permute-start | bytes 884744 | tf_op jit(solution)/shard_map/ppermute | solution.py:629
  49.5 1.4 %collective-permute-done.6 = bf16[384,384]{1,0:T(8,128)(2,1)S(1)} collective-permute-done((bf16[384,384]{1,0:T(8,128)(2,1)S(1)}, bf16[384,384]{1,0:T(8,128)(2,1)S(1)}, u32[]{:S(2)}, u32[]{:S(2)}) %collective-permute-start.6) | collective-permute-done | bytes 294944 | tf_op jit(solution)/shard_map/ppermute | solution.py:629
  50.9 3.0 %collective-permute-done.4 = bf16[384,384]{1,0:T(8,128)(2,1)S(1)} collective-permute-done((bf16[384,384]{1,0:T(8,128)(2,1)S(1)}, bf16[384,384]{1,0:T(8,128)(2,1)S(1)}, u32[]{:S(2)}, u32[]{:S(2)}) %collective-permute-start.4) | collective-permute-done | bytes 294944 | tf_op jit(solution)/shard_map/ppermute | solution.py:629
  54.1 1.3 %queries.1.q_ref = bf16[384,768]{1,0:T(8,128)(2,1)S(1)} custom-call(bf16[384,384]{1,0:T(8,128)(2,1)S(1)} %token_finish.2.a_ref, bf16[384,384]{1,0:T(8,128)(2,1)S(1)} %token_finish.3.b_ref, f32[768]{0:T(1024)S(1)} %copy-done.3, bf16[768,768]{1,0:T(8,128)(2,1)S(1)} %copy-done.1), custom_call_target="tpu_custom_call" | custom-call | flops 500000000 | bytes 3000000 | tf_op jit(solution)/shard_map/queries/pallas_call | solution.py:309
  55.8 3.7 %copy-done.4 = bf16[16,384,768]{2,1,0:T(8,128)(2,1)S(1)} copy-done((bf16[16,384,768]{2,1,0:T(8,128)(2,1)S(1)}, bf16[16,384,768]{2,1,0:T(8,128)(2,1)}, u32[]{:S(2)}) %copy-start.4) | copy-done | bytes 9437208
  59.5 4.8 %attend_first.1 = (bf16[768,768]{1,0:T(8,128)(2,1)S(1)}, bf16[384,768]{1,0:T(8,128)(2,1)S(1)}, bf16[768,384]{1,0:T(8,128)(2,1)S(1)}, bf16[208,384]{1,0:T(8,128)(2,1)S(1)}) custom-call(s32[1]{0:T(128)} %bitcast.3.half_ref, s32[1]{0:T(128)} %bitcast.4.core_ref, bf16[384,768]{1,0:T(8,128)(2,1)S(1)} %queries.1.q_ref, ...), custom_call_target="tpu_custom_call" | custom-call | flops 4000000000 | bytes 4000000 | tf_op jit(solution)/shard_map/attend_first/pallas_call | solution.py:533
  64.3 5.1 %collective-permute-start.9 = (bf16[208,384]{1,0:T(8,128)(2,1)S(1)}, bf16[208,384]{1,0:T(8,128)(2,1)S(1)}, u32[]{:S(2)}, u32[]{:S(2)}) collective-permute-start(bf16[208,384]{1,0:T(8,128)(2,1)S(1)} %get-tuple-element.33), channel_id=1, source_target_pairs={{0,1},{1,0},{2,3},{3,2},{4,5},{5,4},{6,7},{7,6},{8,9},{9,8},{10,11... | collective-permute-start | bytes 479240 | tf_op jit(solution)/shard_map/ppermute | solution.py:684
  69.4 3.7 %copy-done.5 = bf16[16,384,768]{2,1,0:T(8,128)(2,1)S(1)} copy-done((bf16[16,384,768]{2,1,0:T(8,128)(2,1)S(1)}, bf16[16,384,768]{2,1,0:T(8,128)(2,1)}, u32[]{:S(2)}) %copy-start.5) | copy-done | bytes 9437208
  73.0 4.2 %attend_next.1 = (bf16[384,768]{1,0:T(8,128)(2,1)S(1)}, bf16[768,384]{1,0:T(8,128)(2,1)S(1)}, bf16[208,384]{1,0:T(8,128)(2,1)S(1)}) custom-call(s32[1]{0:T(128)} %bitcast.3.half_ref, bf16[384,768]{1,0:T(8,128)(2,1)S(1)} %queries.1.q_ref, bf16[768,768]{1,0:T(8,128)(2,1)S(1)} %get-tuple-element.37.x_ref, bf16[768,1536]{1,0:T(8,128)(2,1)S(1)} %copy-done.8, ...), custom_call_target="tpu_custom_call" | custom-call | flops 4000000000 | bytes 4000000 | tf_op jit(solution)/shard_map/attend_next/pallas_call | solution.py:533
  77.4 3.7 %copy-done.6 = bf16[16,384,768]{2,1,0:T(8,128)(2,1)S(1)} copy-done((bf16[16,384,768]{2,1,0:T(8,128)(2,1)S(1)}, bf16[16,384,768]{2,1,0:T(8,128)(2,1)}, u32[]{:S(2)}) %copy-start.6) | copy-done | bytes 9437208
  81.0 2.4 %attend_keep.2 = (f32[192,384]{1,0:T(8,128)S(1)}, f32[192,128]{1,0:T(8,128)S(1)}, bf16[208,384]{1,0:T(8,128)(2,1)S(1)}) custom-call(s32[1]{0:T(128)} %bitcast.2.half_ref, bf16[384,768]{1,0:T(8,128)(2,1)S(1)} %queries.1.q_ref, bf16[384,768]{1,0:T(8,128)(2,1)S(1)} %get-tuple-element.31.k_ref, bf16[768,384]{1,0:T(8,128)(2,1)S(1)} %get-tuple-element.32.v_ref, ...), custom_call_target="tpu_custom_call" | custom-call | flops 4000000000 | bytes 4000000 | tf_op jit(solution)/shard_map/attend_keep/pallas_call | solution.py:533
  83.4 7.1 %collective-permute-start.10 = (bf16[208,384]{1,0:T(8,128)(2,1)S(1)}, bf16[208,384]{1,0:T(8,128)(2,1)S(1)}, u32[]{:S(2)}, u32[]{:S(2)}) collective-permute-start(bf16[208,384]{1,0:T(8,128)(2,1)S(1)} %get-tuple-element.36), channel_id=1, source_target_pairs={{0,3},{1,2},{2,1},{3,0},{4,7},{5,6},{6,5},{7,4},{8,11},{9,10},{10,... | collective-permute-start | bytes 479240 | tf_op jit(solution)/shard_map/ppermute | solution.py:678
  90.6 3.7 %copy-done.7 = bf16[16,384,768]{2,1,0:T(8,128)(2,1)S(1)} copy-done((bf16[16,384,768]{2,1,0:T(8,128)(2,1)S(1)}, bf16[16,384,768]{2,1,0:T(8,128)(2,1)}, u32[]{:S(2)}) %copy-start.7) | copy-done | bytes 9437208
  94.3 2.3 %attend_keep.3 = (f32[192,384]{1,0:T(8,128)S(1)}, f32[192,128]{1,0:T(8,128)S(1)}, bf16[208,384]{1,0:T(8,128)(2,1)S(1)}) custom-call(s32[1]{0:T(128)} %bitcast.2.half_ref, bf16[384,768]{1,0:T(8,128)(2,1)S(1)} %queries.1.q_ref, bf16[384,768]{1,0:T(8,128)(2,1)S(1)} %get-tuple-element.38.k_ref, bf16[768,384]{1,0:T(8,128)(2,1)S(1)} %get-tuple-element.39.v_ref, ...), custom_call_target="tpu_custom_call" | custom-call | flops 4000000000 | bytes 4000000 | tf_op jit(solution)/shard_map/attend_keep/pallas_call | solution.py:533
  97.2 0.9 collective-permute-start.13
  98.1 7.4 %collective-permute-done.12.msg_ref = bf16[208,384]{1,0:T(8,128)(2,1)S(1)} collective-permute-done((bf16[208,384]{1,0:T(8,128)(2,1)S(1)}, bf16[208,384]{1,0:T(8,128)(2,1)S(1)}, u32[]{:S(2)}, u32[]{:S(2)}) %collective-permute-start.12) | collective-permute-done | bytes 159776 | tf_op jit(solution)/shard_map/ppermute | solution.py:678
  106.0 5.1 %collective-permute-done.14.other_b = bf16[192,384]{1,0:T(8,128)(2,1)S(1)} collective-permute-done((bf16[192,384]{1,0:T(8,128)(2,1)S(1)}, bf16[192,384]{1,0:T(8,128)(2,1)S(1)}, u32[]{:S(2)}, u32[]{:S(2)}) %collective-permute-start.14) | collective-permute-done | bytes 147488 | tf_op jit(solution)/shard_map/ppermute | solution.py:707
  111.2 1.6 %output_rows.1 = bf16[384,768]{1,0:T(8,128)(2,1)} custom-call(s32[1]{0:T(128)} %bitcast.2.half_ref, bf16[192,384]{1,0:T(8,128)(2,1)S(1)} %settle.2.own_a, bf16[192,384]{1,0:T(8,128)(2,1)S(1)} %settle.3.own_b, bf16[192,384]{1,0:T(8,128)(2,1)S(1)} %collective-permute-done.13.other_a, bf16[192,384]{1,0:T(8,128)(2,1)S(1)} %collective-permute-done.14.other_b, ...), custom_call_target="tpu_custom_call" | custom-call | tf_op jit(solution)/shard_map/output_rows/pallas_call | solution.py:595
  (42 shorter events, 3.0 us)
Async XLA Ops:
  1.4 4.3 %collective-permute-start.1 = (bf16[64,128]{1,0:T(8,128)(2,1)S(1)}, bf16[64,128]{1,0:T(8,128)(2,1)S(1)}, u32[]{:S(2)}, u32[]{:S(2)}) collective-permute-start(bf16[64,128]{1,0:T(8,128)(2,1)S(1)} %get-tuple-element.44), channel_id=1, source_target_pairs={{4,0},{8,4},{12,8},{16,12},{20,16},{24,20},{28,24},{5,1},{9,5},{13... | collective-permute-start | bytes 49160 | tf_op jit(solution)/shard_map/ppermute | solution.py:658
  2.7 3.9 %collective-permute-start = (bf16[64,128]{1,0:T(8,128)(2,1)S(1)}, bf16[64,128]{1,0:T(8,128)(2,1)S(1)}, u32[]{:S(2)}, u32[]{:S(2)}) collective-permute-start(bf16[64,128]{1,0:T(8,128)(2,1)S(1)} %get-tuple-element.45), channel_id=1, source_target_pairs={{0,4},{4,8},{8,12},{12,16},{16,20},{20,24},{24,28},{1,5},{5,9},{9,... | collective-permute-start | bytes 49160 | tf_op jit(solution)/shard_map/ppermute | solution.py:657
  5.7 0.8 copy-start.11
  6.5 0.6 copy-start.12
  7.1 21.9 %copy-start.2 = (bf16[128,768]{1,0:T(8,128)(2,1)S(1)}, bf16[128,768]{1,0:T(8,128)(2,1)}, u32[]{:S(2)}) copy-start(bf16[128,768]{1,0:T(8,128)(2,1)} %weight_ref.8) | copy-start | bytes 589828
  7.1 21.9 %copy-start.9 = (s32[3072]{0:T(1024)S(1)}, s32[3072]{0:T(1024)}, u32[]{:S(2)}) copy-start(s32[3072]{0:T(1024)} %param.19) | copy-start | bytes 36868
  24.5 8.6 %collective-permute-start.2 = (bf16[400,128]{1,0:T(8,128)(2,1)}, bf16[400,128]{1,0:T(8,128)(2,1)S(1)}, u32[]{:S(2)}, u32[]{:S(2)}) collective-permute-start(bf16[400,128]{1,0:T(8,128)(2,1)} %get-tuple-element.24), channel_id=1, source_target_pairs={{0,4},{4,8},{8,12},{12,16},{16,20},{20,24},{24,28},{1,5},{5,9},{9,... | collective-permute-start | bytes 307208 | tf_op jit(solution)/shard_map/ppermute | solution.py:663
  29.1 1.1 %copy-start.10 = (bf16[3072,128]{1,0:T(8,128)(2,1)S(1)}, bf16[3072,128]{1,0:T(8,128)(2,1)}, u32[]{:S(2)}) copy-start(bf16[3072,128]{1,0:T(8,128)(2,1)} %get-tuple-element.21.out_ref) | copy-start | bytes 2359300
  33.8 9.2 %collective-permute-start.5 = (bf16[384,384]{1,0:T(8,128)(2,1)S(1)}, bf16[384,384]{1,0:T(8,128)(2,1)S(1)}, u32[]{:S(2)}, u32[]{:S(2)}) collective-permute-start(bf16[384,384]{1,0:T(8,128)(2,1)S(1)} %token_finish.3.b_ref), channel_id=1, source_target_pairs={{0,8},{9,1},{18,26},{27,19},{4,20},{13,29},{22,6},{31,15}} | collective-permute-start | bytes 884744 | tf_op jit(solution)/shard_map/ppermute | solution.py:629
  41.1 13.1 %copy-start.1 = (bf16[768,768]{1,0:T(8,128)(2,1)S(1)}, bf16[768,768]{1,0:T(8,128)(2,1)}, u32[]{:S(2)}) copy-start(bf16[768,768]{1,0:T(8,128)(2,1)} %weight_hbm.3) | copy-start | bytes 3538948
  41.1 13.1 %copy-start.3 = (f32[768]{0:T(1024)S(1)}, f32[768]{0:T(1024)}, u32[]{:S(2)}) copy-start(f32[768]{0:T(1024)} %gain_ref.5) | copy-start | bytes 9220
  41.7 6.2 %collective-permute-start.3 = (bf16[384,384]{1,0:T(8,128)(2,1)S(1)}, bf16[384,384]{1,0:T(8,128)(2,1)S(1)}, u32[]{:S(2)}, u32[]{:S(2)}) collective-permute-start(bf16[384,384]{1,0:T(8,128)(2,1)S(1)} %token_finish.2.a_ref), channel_id=1, source_target_pairs={{0,8},{9,1},{18,26},{27,19},{4,20},{13,29},{22,6},{31,15}} | collective-permute-start | bytes 884744 | tf_op jit(solution)/shard_map/ppermute | solution.py:629
  43.1 7.8 %collective-permute-start.6 = (bf16[384,384]{1,0:T(8,128)(2,1)S(1)}, bf16[384,384]{1,0:T(8,128)(2,1)S(1)}, u32[]{:S(2)}, u32[]{:S(2)}) collective-permute-start(bf16[384,384]{1,0:T(8,128)(2,1)S(1)} %broadcast_select_fusion), channel_id=1, source_target_pairs={{0,16},{8,24},{1,17},{9,25},{18,2},{26,10},{19,3},{27,11},{4,12},{... | collective-permute-start | bytes 884744 | tf_op jit(solution)/shard_map/ppermute | solution.py:629
  47.9 6.1 %collective-permute-start.4 = (bf16[384,384]{1,0:T(8,128)(2,1)S(1)}, bf16[384,384]{1,0:T(8,128)(2,1)S(1)}, u32[]{:S(2)}, u32[]{:S(2)}) collective-permute-start(bf16[384,384]{1,0:T(8,128)(2,1)S(1)} %broadcast_select_fusion.1), channel_id=1, source_target_pairs={{0,16},{8,24},{1,17},{9,25},{18,2},{26,10},{19,3},{27,11},{4,12},{... | collective-permute-start | bytes 884744 | tf_op jit(solution)/shard_map/ppermute | solution.py:629
  50.9 4.6 %collective-permute-start.8 = (bf16[384,384]{1,0:T(8,128)(2,1)S(1)}, bf16[384,384]{1,0:T(8,128)(2,1)S(1)}, u32[]{:S(2)}, u32[]{:S(2)}) collective-permute-start(bf16[384,384]{1,0:T(8,128)(2,1)S(1)} %broadcast_select_fusion.2.own_b), channel_id=1, source_target_pairs={{0,4},{4,0},{8,12},{12,8},{16,20},{20,16},{24,28},{28,24},{1,5},{5... | collective-permute-start | bytes 884744 | tf_op jit(solution)/shard_map/ppermute | solution.py:630
  54.0 1.6 %collective-permute-start.7 = (bf16[384,384]{1,0:T(8,128)(2,1)S(1)}, bf16[384,384]{1,0:T(8,128)(2,1)S(1)}, u32[]{:S(2)}, u32[]{:S(2)}) collective-permute-start(bf16[384,384]{1,0:T(8,128)(2,1)S(1)} %broadcast_select_fusion.3.own_a), channel_id=1, source_target_pairs={{0,4},{4,0},{8,12},{12,8},{16,20},{20,16},{24,28},{28,24},{1,5},{5... | collective-permute-start | bytes 884744 | tf_op jit(solution)/shard_map/ppermute | solution.py:630
  54.1 1.7 %copy-start.8 = (bf16[768,1536]{1,0:T(8,128)(2,1)S(1)}, bf16[768,1536]{1,0:T(8,128)(2,1)}, u32[]{:S(2)}) copy-start(bf16[768,1536]{1,0:T(8,128)(2,1)} %weight_hbm.5) | copy-start | bytes 7077892
  55.8 3.7 %copy-start.4 = (bf16[16,384,768]{2,1,0:T(8,128)(2,1)S(1)}, bf16[16,384,768]{2,1,0:T(8,128)(2,1)}, u32[]{:S(2)}) copy-start(bf16[16,384,768]{2,1,0:T(8,128)(2,1)} %bias_ref.5) | copy-start | bytes 28311556
  64.3 13.1 %collective-permute-start.9 = (bf16[208,384]{1,0:T(8,128)(2,1)S(1)}, bf16[208,384]{1,0:T(8,128)(2,1)S(1)}, u32[]{:S(2)}, u32[]{:S(2)}) collective-permute-start(bf16[208,384]{1,0:T(8,128)(2,1)S(1)} %get-tuple-element.33), channel_id=1, source_target_pairs={{0,1},{1,0},{2,3},{3,2},{4,5},{5,4},{6,7},{7,6},{8,9},{9,8},{10,11... | collective-permute-start | bytes 479240 | tf_op jit(solution)/shard_map/ppermute | solution.py:684
  69.4 3.7 %copy-start.5 = (bf16[16,384,768]{2,1,0:T(8,128)(2,1)S(1)}, bf16[16,384,768]{2,1,0:T(8,128)(2,1)}, u32[]{:S(2)}) copy-start(bf16[16,384,768]{2,1,0:T(8,128)(2,1)} %bias_ref.5) | copy-start | bytes 28311556
  77.3 13.3 %collective-permute-start.11 = (bf16[208,384]{1,0:T(8,128)(2,1)S(1)}, bf16[208,384]{1,0:T(8,128)(2,1)S(1)}, u32[]{:S(2)}, u32[]{:S(2)}) collective-permute-start(bf16[208,384]{1,0:T(8,128)(2,1)S(1)} %get-tuple-element.40), channel_id=1, source_target_pairs={{0,1},{1,0},{2,3},{3,2},{4,5},{5,4},{6,7},{7,6},{8,9},{9,8},{10,11... | collective-permute-start | bytes 479240 | tf_op jit(solution)/shard_map/ppermute | solution.py:691
  77.4 3.7 %copy-start.6 = (bf16[16,384,768]{2,1,0:T(8,128)(2,1)S(1)}, bf16[16,384,768]{2,1,0:T(8,128)(2,1)}, u32[]{:S(2)}) copy-start(bf16[16,384,768]{2,1,0:T(8,128)(2,1)} %bias_ref.5) | copy-start | bytes 28311556
  83.4 13.2 %collective-permute-start.10 = (bf16[208,384]{1,0:T(8,128)(2,1)S(1)}, bf16[208,384]{1,0:T(8,128)(2,1)S(1)}, u32[]{:S(2)}, u32[]{:S(2)}) collective-permute-start(bf16[208,384]{1,0:T(8,128)(2,1)S(1)} %get-tuple-element.36), channel_id=1, source_target_pairs={{0,3},{1,2},{2,1},{3,0},{4,7},{5,6},{6,5},{7,4},{8,11},{9,10},{10,... | collective-permute-start | bytes 479240 | tf_op jit(solution)/shard_map/ppermute | solution.py:678
  90.6 3.7 %copy-start.7 = (bf16[16,384,768]{2,1,0:T(8,128)(2,1)S(1)}, bf16[16,384,768]{2,1,0:T(8,128)(2,1)}, u32[]{:S(2)}) copy-start(bf16[16,384,768]{2,1,0:T(8,128)(2,1)} %bias_ref.5) | copy-start | bytes 28311556
  94.2 16.9 %copy-start = (bf16[768,768]{1,0:T(8,128)(2,1)S(1)}, bf16[768,768]{1,0:T(8,128)(2,1)}, u32[]{:S(2)}) copy-start(bf16[768,768]{1,0:T(8,128)(2,1)} %weight_ref.9) | copy-start | bytes 3538948
  96.6 8.9 %collective-permute-start.12 = (bf16[208,384]{1,0:T(8,128)(2,1)S(1)}, bf16[208,384]{1,0:T(8,128)(2,1)S(1)}, u32[]{:S(2)}, u32[]{:S(2)}) collective-permute-start(bf16[208,384]{1,0:T(8,128)(2,1)S(1)} %get-tuple-element.43), channel_id=1, source_target_pairs={{0,3},{1,2},{2,1},{3,0},{4,7},{5,6},{6,5},{7,4},{8,11},{9,10},{10,... | collective-permute-start | bytes 479240 | tf_op jit(solution)/shard_map/ppermute | solution.py:678
  97.2 8.9 %collective-permute-start.13 = (bf16[192,384]{1,0:T(8,128)(2,1)S(1)}, bf16[192,384]{1,0:T(8,128)(2,1)S(1)}, u32[]{:S(2)}, u32[]{:S(2)}) collective-permute-start(bf16[192,384]{1,0:T(8,128)(2,1)S(1)} %settle.2.own_a), channel_id=1, source_target_pairs={{0,1},{1,0},{2,3},{3,2},{4,5},{5,4},{6,7},{7,6},{8,9},{9,8},{10,11... | collective-permute-start | bytes 442376 | tf_op jit(solution)/shard_map/ppermute | solution.py:707
  106.0 5.2 %collective-permute-start.14 = (bf16[192,384]{1,0:T(8,128)(2,1)S(1)}, bf16[192,384]{1,0:T(8,128)(2,1)S(1)}, u32[]{:S(2)}, u32[]{:S(2)}) collective-permute-start(bf16[192,384]{1,0:T(8,128)(2,1)S(1)} %settle.3.own_b), channel_id=1, source_target_pairs={{0,1},{1,0},{2,3},{3,2},{4,5},{5,4},{6,7},{7,6},{8,9},{9,8},{10,11... | collective-permute-start | bytes 442376 | tf_op jit(solution)/shard_map/ppermute | solution.py:707

commit v2 on v1

--- a/solution.py
+++ b/solution.py
@@ -54,6 +54,7 @@
     bias_ref,
     tok_ref,
     out_ref,
+    near_ref,
     msg_ref,
     q_s,
     k_s,
@@ -138,6 +139,7 @@
         own = atoms_ref[pl.ds(at, atoms_group), :].astype(F32)
         result = own + dot(jnp.concatenate(merged, axis=0), proj_ref[...])
         out_ref[local : local + atoms_group, :] = result.astype(BF16)
+        near_ref[local : local + atoms_group, :] = result.astype(BF16)
 
     groups = blocks // group
     ahead = score(0)
@@ -183,6 +185,7 @@
             ],
             out_specs=[
                 pl.BlockSpec((size, width), lambda i, *_: (i, 0)),
+                pl.BlockSpec((size, width), lambda i, *_: (i, 0)),
                 full((SHIFT_MAX + 16, width)),
             ],
             scratch_shapes=[
@@ -193,6 +196,7 @@
             ],
         ),
         out_shape=[
+            jax.ShapeDtypeStruct((rows, width), BF16),
             jax.ShapeDtypeStruct((rows, width), BF16),
             jax.ShapeDtypeStruct((SHIFT_MAX + 16, width), BF16),
         ],
@@ -390,8 +394,7 @@
 
     def soften(p, n):
         for r in range(n * tiles // chunks * ROW_TILE, (n + 1) * tiles // chunks * ROW_TILE, ROW_TILE):
-            line = pl.multiple_of(at + r % rows, ROW_TILE)
-            bias = bias_ref[group * heads + 2 * p + r // rows, pl.ds(line, ROW_TILE), :].astype(F32)
+            bias = bias_ref[group * heads + 2 * p + r // rows, r % rows : r % rows + ROW_TILE, :].astype(F32)
             scores = score_s[p % 2][r : r + ROW_TILE, :] + bias
             top = jnp.max(scores, axis=-1, keepdims=True)
             term_s[p % 2][r : r + ROW_TILE, :] = jnp.exp(scores - top).astype(BF16)
@@ -627,7 +630,7 @@
             fresh = (jnp.bitwise_and(away, ~(known + order[r])) == 0) & (jnp.bitwise_and(away, order[r]) != 0)
             gets = gets | (fresh & (core == c))
         held = [jnp.where(gets, lax.ppermute(part, ("pb", "ka"), pairs), part) for part in held]
-    return held, [lax.ppermute(part, "pb", [(p, p ^ 1) for p in range(n_pb)]) for part in held]
+    return held
 
 
 def body(
@@ -656,21 +659,30 @@
     tok2d = token_of_atom.reshape(rows // LANES, LANES)
     left = lax.ppermute(atoms[rows - half :], "pb", up)
     right = lax.ppermute(atoms[:half], "pb", down)
-    atom_out, msg = atom_attention(
+    atom_out, near_out, msg = atom_attention(
         window_shift, pos, atoms, left, right, atom_gain, atom_qkv, atom_proj,
         atom_bias, tok2d, tok_rows, rows * n_pb,
     )
     behind = lax.ppermute(msg, "pb", up)
     token_repr = []
     for part in range(PARTS):
-        sums, counts = pool(pos, atom_out, agg_weight, tok2d, tok_rows, part)
+        sums, counts = pool(pos, near_out, agg_weight, tok2d, tok_rows, part)
         token_repr.append(finish(behind, agg_weight, sums, counts, part))
     late_bias, token_repr[0] = lax.optimization_barrier((pair_bias, token_repr[0]))
-    own_keys, other_keys = key_parts(token_repr)
-    queries = project_queries(token_repr, token_gain, token_q)
     parity = jnp.bitwise_and(plane ^ (plane >> 1), 1).astype(jnp.int32)
     core = lax.rem(shard, n_pb // n_ka).astype(jnp.int32)
     keep, send = parity.reshape(1), (1 - parity).reshape(1)
+    share = tok_rows // 2
+    send_bias = lax.dynamic_slice_in_dim(late_bias, (1 - parity) * share, share, axis=1)
+    queries = project_queries(token_repr, token_gain, token_q)
+    own_keys = key_parts(token_repr)
+    own_keys[0], queries, send_bias = lax.optimization_barrier((own_keys[0], queries, send_bias))
+    cores = [(p, p ^ 1) for p in range(n_pb)]
+    other_keys = [lax.ppermute(own_keys[0], "pb", cores)]
+    late_bias, own_keys[1] = lax.optimization_barrier((late_bias, own_keys[1]))
+    other_keys.append(lax.ppermute(own_keys[1], "pb", cores))
+    late_bias, send_bias = lax.optimization_barrier((late_bias, send_bias))
+    keep_bias = lax.dynamic_slice_in_dim(late_bias, parity * share, share, axis=1)
     swap = [(i, i ^ 1) for i in range(n_ka)]
     bits = bits_of(n_ka)[1:]
 
@@ -679,13 +691,13 @@
 
     x, k, v, msg = group_call(
         first_kernel, 0, send, (core.reshape(1),), queries, (*own_keys, *other_keys, token_gain), token_kv,
-        late_bias, ("x", "k", "v", "msg"), "attend_first",
+        send_bias, ("x", "k", "v", "msg"), "attend_first",
     )
     held, near = [(k, v)], [lax.ppermute(msg, "ka", swap)]
     for g in range(1, GROUPS):
         k, v, msg = group_call(
             functools.partial(next_kernel, g), g, send, (), queries, (x,), token_kv,
-            late_bias, ("k", "v", "msg"), "attend_next",
+            send_bias, ("k", "v", "msg"), "attend_next",
         )
         held.append((k, v))
         near.append(lax.ppermute(msg, "ka", swap))
@@ -693,7 +705,7 @@
     for g in range(GROUPS):
         o, lse, msg = group_call(
             functools.partial(keep_kernel, g), g, keep, (), queries, (*held[g], near[g]), None,
-            late_bias, ("o", "lse", "msg"), "attend_keep",
+            keep_bias, ("o", "lse", "msg"), "attend_keep",
         )
         sums.append((o, lse))
         gone.append(far(msg, bits[0]))

time: 113 us -> 110 us (0.973)
  waiting for transfers between devices: 20.1 us -> 17.6 us
    unnamed x26 -> x24, local copies, waits for them, and re-layouts: 16.6 us -> 8.09 us
    ppermute x2, starting transfers between devices: 1.01 us -> 9.3 us  [body(): other_mix.append(lax.ppermute(own_mix[g], 'ka', swap))]
    dynamic_slice x0 -> x2, local copies, waits for them, and re-layouts: none -> 7.55 us  [the longest x1 4.91 us: body(): lax.dynamic_slice_in_dim(late_bias, (1 - parity) * share, share, axis=1)]
    ppermute x2, waiting for transfers between devices: 7.4 us -> 0.94 us  [far(): return lax.ppermute(msg, 'ka', [(i, i ^ 2 * bit - 1) for i in range(n_ka)])]
    ppermute x1, starting transfers between devices: 5.11 us -> 0.76 us  [body(): held, near = ([(k, v)], [lax.ppermute(msg, 'ka', swap)])]
    ppermute x1, waiting for transfers between devices: 0.01 us -> 3.86 us  [body(): right = lax.ppermute(atoms[:half], 'pb', down)]
    ppermute x2, starting transfers between devices: 7.21 us -> 3.95 us  [far(): return lax.ppermute(msg, 'ka', [(i, i ^ 2 * bit - 1) for i in range(n_ka)])]
    ppermute x1, waiting for transfers between devices: 0.01 us -> 1.41 us  [body(): near.append(lax.ppermute(msg, 'ka', swap))]
  transfers between devices with their start and end apart: 15 -> 15, of which waited for: 7 -> 8; matrix products, arithmetic and copies ran while one was open for 0% -> 7% of each run, Pallas kernels for 16% -> 12%
where the time goes in v2:
time: 110 us
  Pallas kernels  41.9 us (38%)
  starting transfers between devices  32.6 us (30%)
  waiting for transfers between devices  17.6 us (16%)
  local copies, waits for them, and re-layouts  16.4 us (15%)
    pallas_call x1, Pallas kernels, atom_attention(): pl.pallas_call(functools.partial(atom_kernel, chunks, atom_total, tok_row...  17.5 us
    pallas_call x4, Pallas kernels, group_call(): pl.pallas_call(functools.partial(kernel, heads, feats // heads), grid_spe...  13.4 us
    ppermute x2, starting transfers between devices, body(): other_mix.append(lax.ppermute(own_mix[g], 'ka', swap))  9.3 us
    ppermute x4, starting transfers between devices, key_parts(): lax.ppermute(part, ('pb', 'ka'), pairs)  8.55 us
    unnamed x24, local copies, waits for them, and re-layouts  8.09 us
    pallas_call x2, Pallas kernels, pool(): pl.pallas_call(functools.partial(pool_kernel, tok_rows), grid_spec=pltpu....  6.04 us
    ppermute x4, waiting for transfers between devices, key_parts(): lax.ppermute(part, ('pb', 'ka'), pairs)  5.87 us
    dynamic_slice x1, local copies, waits for them, and re-layouts, body(): lax.dynamic_slice_in_dim(late_bias, (1 - parity) * share, share, axis=1)  4.91 us
  transfers between devices with their start and end apart: 15, of which 8 were waited for; matrix products, arithmetic and copies ran while one was open for 7% of the time, Pallas kernels for 12%

profile of v2, /device:TPU:0, one launch (start us, length us, event | category | flops | bytes accessed | tf_op | source)
XLA Modules:
  0.0 109.6 jit_solution(11705320954770303573)
XLA Ops:
  1.4 2.3 %collective-permute-start = (bf16[64,128]{1,0:T(8,128)(2,1)S(1)}, bf16[64,128]{1,0:T(8,128)(2,1)S(1)}, u32[]{:S(2)}, u32[]{:S(2)}) collective-permute-start(bf16[64,128]{1,0:T(8,128)(2,1)S(1)} %get-tuple-element.61), channel_id=1, source_target_pairs={{0,4},{4,8},{8,12},{12,16},{16,20},{20,24},{24,28},{1,5},{5,9},{9,... | collective-permute-start | bytes 49160 | tf_op jit(solution)/shard_map/ppermute | solution.py:660
  3.7 1.3 %collective-permute-start.1 = (bf16[64,128]{1,0:T(8,128)(2,1)S(1)}, bf16[64,128]{1,0:T(8,128)(2,1)S(1)}, u32[]{:S(2)}, u32[]{:S(2)}) collective-permute-start(bf16[64,128]{1,0:T(8,128)(2,1)S(1)} %get-tuple-element.60), channel_id=1, source_target_pairs={{4,0},{8,4},{12,8},{16,12},{20,16},{24,20},{28,24},{5,1},{9,5},{13... | collective-permute-start | bytes 49160 | tf_op jit(solution)/shard_map/ppermute | solution.py:661
  5.0 3.9 %collective-permute-done.1.right_ref = bf16[64,128]{1,0:T(8,128)(2,1)S(1)} collective-permute-done((bf16[64,128]{1,0:T(8,128)(2,1)S(1)}, bf16[64,128]{1,0:T(8,128)(2,1)S(1)}, u32[]{:S(2)}, u32[]{:S(2)}) %collective-permute-start.1) | collective-permute-done | bytes 16416 | tf_op jit(solution)/shard_map/ppermute | solution.py:661
  9.5 17.5 %atom_attention.1 = (bf16[3072,128]{1,0:T(8,128)(2,1)}, bf16[3072,128]{1,0:T(8,128)(2,1)}, bf16[400,128]{1,0:T(8,128)(2,1)}) custom-call(s32[96]{0:T(128)} %shift_ref.1, s32[1]{0:T(128)} %bitcast.pos_ref, bf16[3072,128]{1,0:T(8,128)(2,1)} %atoms_ref.1, bf16[64,128]{1,0:T(8,128)(2,1)} %copy-done.10, bf16[64,128]{1,0:T(8,128)(2,1)} %copy-done.11, ...), custom_call_target="tpu_custom_call" | custom-call | flops 8000000000 | bytes 6000000 | tf_op jit(solution)/shard_map/atom_attention/pallas_call | solution.py:171
  27.0 4.4 %collective-permute-start.2 = (bf16[400,128]{1,0:T(8,128)(2,1)}, bf16[400,128]{1,0:T(8,128)(2,1)S(1)}, u32[]{:S(2)}, u32[]{:S(2)}) collective-permute-start(bf16[400,128]{1,0:T(8,128)(2,1)} %get-tuple-element.32), channel_id=1, source_target_pairs={{0,4},{4,8},{8,12},{12,16},{16,20},{20,24},{24,28},{1,5},{5,9},{9,... | collective-permute-start | bytes 307208 | tf_op jit(solution)/shard_map/ppermute | solution.py:666
  31.5 1.1 %copy-done.9 = bf16[3072,128]{1,0:T(8,128)(2,1)S(1)} copy-done((bf16[3072,128]{1,0:T(8,128)(2,1)S(1)}, bf16[3072,128]{1,0:T(8,128)(2,1)}, u32[]{:S(2)}) %copy-start.9) | copy-done | bytes 786456
  32.6 3.0 %pool.3 = (f32[384,384]{1,0:T(8,128)S(1)}, f32[384,128]{1,0:T(8,128)S(1)}) custom-call(s32[1]{0:T(128)} %bitcast.pos_ref, bf16[3072,128]{1,0:T(8,128)(2,1)S(1)} %copy-done.9, bf16[128,768]{1,0:T(8,128)(2,1)S(1)} %copy-done.4, s32[24,128]{1,0:T(8,128)S(1)} %bitcast.6), custom_call_target="tpu_custom_call" | custom-call | flops 2000000000 | bytes 2000000 | tf_op jit(solution)/shard_map/pool/pallas_call | solution.py:245
  36.2 4.3 %collective-permute-start.5 = (bf16[384,384]{1,0:T(8,128)(2,1)S(1)}, bf16[384,384]{1,0:T(8,128)(2,1)S(1)}, u32[]{:S(2)}, u32[]{:S(2)}) collective-permute-start(bf16[384,384]{1,0:T(8,128)(2,1)S(1)} %token_finish.3.b_ref), channel_id=1, source_target_pairs={{0,8},{9,1},{18,26},{27,19},{4,20},{13,29},{22,6},{31,15}} | collective-permute-start | bytes 884744 | tf_op jit(solution)/shard_map/ppermute | solution.py:632
  40.5 3.0 %pool.2 = (f32[384,384]{1,0:T(8,128)S(1)}, f32[384,128]{1,0:T(8,128)S(1)}) custom-call(s32[1]{0:T(128)} %bitcast.pos_ref, bf16[3072,128]{1,0:T(8,128)(2,1)S(1)} %copy-done.9, bf16[128,768]{1,0:T(8,128)(2,1)S(1)} %copy-done.4, s32[24,128]{1,0:T(8,128)S(1)} %bitcast.7), custom_call_target="tpu_custom_call" | custom-call | flops 2000000000 | bytes 2000000 | tf_op jit(solution)/shard_map/pool/pallas_call | solution.py:245
  44.1 1.3 %collective-permute-start.3 = (bf16[384,384]{1,0:T(8,128)(2,1)S(1)}, bf16[384,384]{1,0:T(8,128)(2,1)S(1)}, u32[]{:S(2)}, u32[]{:S(2)}) collective-permute-start(bf16[384,384]{1,0:T(8,128)(2,1)S(1)} %token_finish.2.a_ref), channel_id=1, source_target_pairs={{0,8},{9,1},{18,26},{27,19},{4,20},{13,29},{22,6},{31,15}} | collective-permute-start | bytes 884744 | tf_op jit(solution)/shard_map/ppermute | solution.py:632
  45.6 1.3 %collective-permute-start.6 = (bf16[384,384]{1,0:T(8,128)(2,1)S(1)}, bf16[384,384]{1,0:T(8,128)(2,1)S(1)}, u32[]{:S(2)}, u32[]{:S(2)}) collective-permute-start(bf16[384,384]{1,0:T(8,128)(2,1)S(1)} %broadcast_select_fusion), channel_id=1, source_target_pairs={{0,16},{8,24},{1,17},{9,25},{18,2},{26,10},{19,3},{27,11},{4,12},{... | collective-permute-start | bytes 884744 | tf_op jit(solution)/shard_map/ppermute | solution.py:632
  46.9 5.9 %collective-permute-done.3 = bf16[384,384]{1,0:T(8,128)(2,1)S(1)} collective-permute-done((bf16[384,384]{1,0:T(8,128)(2,1)S(1)}, bf16[384,384]{1,0:T(8,128)(2,1)S(1)}, u32[]{:S(2)}, u32[]{:S(2)}) %collective-permute-start.3) | collective-permute-done | bytes 294944 | tf_op jit(solution)/shard_map/ppermute | solution.py:632
  52.8 1.6 %collective-permute-start.4 = (bf16[384,384]{1,0:T(8,128)(2,1)S(1)}, bf16[384,384]{1,0:T(8,128)(2,1)S(1)}, u32[]{:S(2)}, u32[]{:S(2)}) collective-permute-start(bf16[384,384]{1,0:T(8,128)(2,1)S(1)} %broadcast_select_fusion.1), channel_id=1, source_target_pairs={{0,16},{8,24},{1,17},{9,25},{18,2},{26,10},{19,3},{27,11},{4,12},{... | collective-permute-start | bytes 884744 | tf_op jit(solution)/shard_map/ppermute | solution.py:632
  54.4 4.9 %constant_dynamic-slice_fusion.1.bias_ref = bf16[16,192,768]{2,1,0:T(8,128)(2,1)} fusion(bf16[16,384,768]{2,1,0:T(8,128)(2,1)} %param.25, s32[]{:T(128)S(6)} %select_n.38), kind=kLoop, calls=%fused_computation.5 | loop fusion | bytes 9437188 | tf_op jit(solution)/shard_map/dynamic_slice | solution.py:676
  59.3 1.3 %queries.1.q_ref = bf16[384,768]{1,0:T(8,128)(2,1)S(1)} custom-call(bf16[384,384]{1,0:T(8,128)(2,1)S(1)} %token_finish.2.a_ref, bf16[384,384]{1,0:T(8,128)(2,1)S(1)} %token_finish.3.b_ref, f32[768]{0:T(1024)S(1)} %copy-done.5, bf16[768,768]{1,0:T(8,128)(2,1)S(1)} %copy-done.3), custom_call_target="tpu_custom_call" | custom-call | flops 500000000 | bytes 3000000 | tf_op jit(solution)/shard_map/queries/pallas_call | solution.py:313
  61.3 1.1 collective-permute-done.8.other_b
  62.8 2.3 %copy-done = bf16[16,192,768]{2,1,0:T(8,128)(2,1)S(1)} copy-done((bf16[16,192,768]{2,1,0:T(8,128)(2,1)S(1)}, bf16[16,192,768]{2,1,0:T(8,128)(2,1)}, u32[]{:S(2)}) %copy-start) | copy-done | bytes 4718616
  65.1 1.7 %copy-done.6 = bf16[768,1536]{1,0:T(8,128)(2,1)S(1)} copy-done((bf16[768,1536]{1,0:T(8,128)(2,1)S(1)}, bf16[768,1536]{1,0:T(8,128)(2,1)}, u32[]{:S(2)}) %copy-start.6) | copy-done | bytes 2359320
  66.8 4.7 %attend_first.1 = (bf16[768,768]{1,0:T(8,128)(2,1)S(1)}, bf16[384,768]{1,0:T(8,128)(2,1)S(1)}, bf16[768,384]{1,0:T(8,128)(2,1)S(1)}, bf16[208,384]{1,0:T(8,128)(2,1)S(1)}) custom-call(s32[1]{0:T(128)} %bitcast.3.half_ref, s32[1]{0:T(128)} %bitcast.4.core_ref, bf16[384,768]{1,0:T(8,128)(2,1)S(1)} %queries.1.q_ref, ...), custom_call_target="tpu_custom_call" | custom-call | flops 4000000000 | bytes 4000000 | tf_op jit(solution)/shard_map/attend_first/pallas_call | solution.py:536
  71.5 2.3 %copy-done.1 = bf16[16,192,768]{2,1,0:T(8,128)(2,1)S(1)} copy-done((bf16[16,192,768]{2,1,0:T(8,128)(2,1)S(1)}, bf16[16,192,768]{2,1,0:T(8,128)(2,1)}, u32[]{:S(2)}) %copy-start.1) | copy-done | bytes 4718616
  73.8 4.1 %attend_next.1 = (bf16[384,768]{1,0:T(8,128)(2,1)S(1)}, bf16[768,384]{1,0:T(8,128)(2,1)S(1)}, bf16[208,384]{1,0:T(8,128)(2,1)S(1)}) custom-call(s32[1]{0:T(128)} %bitcast.3.half_ref, bf16[384,768]{1,0:T(8,128)(2,1)S(1)} %queries.1.q_ref, bf16[768,768]{1,0:T(8,128)(2,1)S(1)} %get-tuple-element.53.x_ref, bf16[768,1536]{1,0:T(8,128)(2,1)S(1)} %copy-done.7, ...), custom_call_target="tpu_custom_call" | custom-call | flops 4000000000 | bytes 4000000 | tf_op jit(solution)/shard_map/attend_next/pallas_call | solution.py:536
  77.9 1.4 %collective-permute-start.11 = (bf16[208,384]{1,0:T(8,128)(2,1)S(1)}, bf16[208,384]{1,0:T(8,128)(2,1)S(1)}, u32[]{:S(2)}, u32[]{:S(2)}) collective-permute-start(bf16[208,384]{1,0:T(8,128)(2,1)S(1)} %get-tuple-element.56), channel_id=1, source_target_pairs={{0,1},{1,0},{2,3},{3,2},{4,5},{5,4},{6,7},{7,6},{8,9},{9,8},{10,11... | collective-permute-start | bytes 479240 | tf_op jit(solution)/shard_map/ppermute | solution.py:703
  79.3 2.6 %constant_dynamic-slice_fusion.bias_ref = bf16[16,192,768]{2,1,0:T(8,128)(2,1)S(1)} fusion(bf16[16,384,768]{2,1,0:T(8,128)(2,1)} %param.25, s32[]{:T(128)S(6)} %select_n.41), kind=kLoop, calls=%fused_computation.4 | loop fusion | bytes 9437188 | tf_op jit(solution)/shard_map/dynamic_slice | solution.py:685
  82.7 1.4 %collective-permute-done.11.near_ref = bf16[208,384]{1,0:T(8,128)(2,1)S(1)} collective-permute-done((bf16[208,384]{1,0:T(8,128)(2,1)S(1)}, bf16[208,384]{1,0:T(8,128)(2,1)S(1)}, u32[]{:S(2)}, u32[]{:S(2)}) %collective-permute-start.11) | collective-permute-done | bytes 159776 | tf_op jit(solution)/shard_map/ppermute | solution.py:703
  84.1 2.3 %attend_keep.3 = (f32[192,384]{1,0:T(8,128)S(1)}, f32[192,128]{1,0:T(8,128)S(1)}, bf16[208,384]{1,0:T(8,128)(2,1)S(1)}) custom-call(s32[1]{0:T(128)} %bitcast.2.half_ref, bf16[384,768]{1,0:T(8,128)(2,1)S(1)} %queries.1.q_ref, bf16[384,768]{1,0:T(8,128)(2,1)S(1)} %get-tuple-element.54.k_ref, bf16[768,384]{1,0:T(8,128)(2,1)S(1)} %get-tuple-element.55.v_ref, ...), custom_call_target="tpu_custom_call" | custom-call | flops 4000000000 | bytes 4000000 | tf_op jit(solution)/shard_map/attend_keep/pallas_call | solution.py:536
  86.4 3.4 %collective-permute-start.12 = (bf16[208,384]{1,0:T(8,128)(2,1)S(1)}, bf16[208,384]{1,0:T(8,128)(2,1)S(1)}, u32[]{:S(2)}, u32[]{:S(2)}) collective-permute-start(bf16[208,384]{1,0:T(8,128)(2,1)S(1)} %get-tuple-element.59), channel_id=1, source_target_pairs={{0,3},{1,2},{2,1},{3,0},{4,7},{5,6},{6,5},{7,4},{8,11},{9,10},{10,... | collective-permute-start | bytes 479240 | tf_op jit(solution)/shard_map/ppermute | solution.py:690
  89.9 2.4 %attend_keep.2 = (f32[192,384]{1,0:T(8,128)S(1)}, f32[192,128]{1,0:T(8,128)S(1)}, bf16[208,384]{1,0:T(8,128)(2,1)S(1)}) custom-call(s32[1]{0:T(128)} %bitcast.2.half_ref, bf16[384,768]{1,0:T(8,128)(2,1)S(1)} %queries.1.q_ref, bf16[384,768]{1,0:T(8,128)(2,1)S(1)} %get-tuple-element.46.k_ref, bf16[768,384]{1,0:T(8,128)(2,1)S(1)} %get-tuple-element.47.v_ref, ...), custom_call_target="tpu_custom_call" | custom-call | flops 4000000000 | bytes 4000000 | tf_op jit(solution)/shard_map/attend_keep/pallas_call | solution.py:536
  94.2 7.5 %collective-permute-start.14 = (bf16[192,384]{1,0:T(8,128)(2,1)S(1)}, bf16[192,384]{1,0:T(8,128)(2,1)S(1)}, u32[]{:S(2)}, u32[]{:S(2)}) collective-permute-start(bf16[192,384]{1,0:T(8,128)(2,1)S(1)} %settle.3.own_b), channel_id=1, source_target_pairs={{0,1},{1,0},{2,3},{3,2},{4,5},{5,4},{6,7},{7,6},{8,9},{9,8},{10,11... | collective-permute-start | bytes 442376 | tf_op jit(solution)/shard_map/ppermute | solution.py:719
  102.2 1.8 %collective-permute-start.13 = (bf16[192,384]{1,0:T(8,128)(2,1)S(1)}, bf16[192,384]{1,0:T(8,128)(2,1)S(1)}, u32[]{:S(2)}, u32[]{:S(2)}) collective-permute-start(bf16[192,384]{1,0:T(8,128)(2,1)S(1)} %settle.2.own_a), channel_id=1, source_target_pairs={{0,1},{1,0},{2,3},{3,2},{4,5},{5,4},{6,7},{7,6},{8,9},{9,8},{10,11... | collective-permute-start | bytes 442376 | tf_op jit(solution)/shard_map/ppermute | solution.py:719
  103.9 2.1 %collective-permute-done.14.other_b = bf16[192,384]{1,0:T(8,128)(2,1)S(1)} collective-permute-done((bf16[192,384]{1,0:T(8,128)(2,1)S(1)}, bf16[192,384]{1,0:T(8,128)(2,1)S(1)}, u32[]{:S(2)}, u32[]{:S(2)}) %collective-permute-start.14) | collective-permute-done | bytes 147488 | tf_op jit(solution)/shard_map/ppermute | solution.py:719
  106.0 2.0 %collective-permute-done.13.other_a = bf16[192,384]{1,0:T(8,128)(2,1)S(1)} collective-permute-done((bf16[192,384]{1,0:T(8,128)(2,1)S(1)}, bf16[192,384]{1,0:T(8,128)(2,1)S(1)}, u32[]{:S(2)}, u32[]{:S(2)}) %collective-permute-start.13) | collective-permute-done | bytes 147488 | tf_op jit(solution)/shard_map/ppermute | solution.py:719
  108.0 1.6 %output_rows.1 = bf16[384,768]{1,0:T(8,128)(2,1)} custom-call(s32[1]{0:T(128)} %bitcast.2.half_ref, bf16[192,384]{1,0:T(8,128)(2,1)S(1)} %settle.2.own_a, bf16[192,384]{1,0:T(8,128)(2,1)S(1)} %settle.3.own_b, bf16[192,384]{1,0:T(8,128)(2,1)S(1)} %collective-permute-done.13.other_a, bf16[192,384]{1,0:T(8,128)(2,1)S(1)} %collective-permute-done.14.other_b, ...), custom_call_target="tpu_custom_call" | custom-call | tf_op jit(solution)/shard_map/output_rows/pallas_call | solution.py:598
  (42 shorter events, 6.8 us)
Async XLA Ops:
  1.4 3.7 %collective-permute-start = (bf16[64,128]{1,0:T(8,128)(2,1)S(1)}, bf16[64,128]{1,0:T(8,128)(2,1)S(1)}, u32[]{:S(2)}, u32[]{:S(2)}) collective-permute-start(bf16[64,128]{1,0:T(8,128)(2,1)S(1)} %get-tuple-element.61), channel_id=1, source_target_pairs={{0,4},{4,8},{8,12},{12,16},{16,20},{20,24},{24,28},{1,5},{5,9},{9,... | collective-permute-start | bytes 49160 | tf_op jit(solution)/shard_map/ppermute | solution.py:660
  3.7 5.2 %collective-permute-start.1 = (bf16[64,128]{1,0:T(8,128)(2,1)S(1)}, bf16[64,128]{1,0:T(8,128)(2,1)S(1)}, u32[]{:S(2)}, u32[]{:S(2)}) collective-permute-start(bf16[64,128]{1,0:T(8,128)(2,1)S(1)} %get-tuple-element.60), channel_id=1, source_target_pairs={{4,0},{8,4},{12,8},{16,12},{20,16},{24,20},{28,24},{5,1},{9,5},{13... | collective-permute-start | bytes 49160 | tf_op jit(solution)/shard_map/ppermute | solution.py:661
  5.0 3.9 %copy-start.10 = (bf16[64,128]{1,0:T(8,128)(2,1)}, bf16[64,128]{1,0:T(8,128)(2,1)S(1)}, u32[]{:S(2)}) copy-start(bf16[64,128]{1,0:T(8,128)(2,1)S(1)} %collective-permute-done.left_ref) | copy-start | bytes 49156
  8.9 0.6 copy-start.11
  9.5 21.9 %copy-start.4 = (bf16[128,768]{1,0:T(8,128)(2,1)S(1)}, bf16[128,768]{1,0:T(8,128)(2,1)}, u32[]{:S(2)}) copy-start(bf16[128,768]{1,0:T(8,128)(2,1)} %weight_ref.8) | copy-start | bytes 589828
  9.5 21.9 %copy-start.8 = (s32[3072]{0:T(1024)S(1)}, s32[3072]{0:T(1024)}, u32[]{:S(2)}) copy-start(s32[3072]{0:T(1024)} %param.19) | copy-start | bytes 36868
  27.0 8.6 %collective-permute-start.2 = (bf16[400,128]{1,0:T(8,128)(2,1)}, bf16[400,128]{1,0:T(8,128)(2,1)S(1)}, u32[]{:S(2)}, u32[]{:S(2)}) collective-permute-start(bf16[400,128]{1,0:T(8,128)(2,1)} %get-tuple-element.32), channel_id=1, source_target_pairs={{0,4},{4,8},{8,12},{12,16},{16,20},{20,24},{24,28},{1,5},{5,9},{9,... | collective-permute-start | bytes 307208 | tf_op jit(solution)/shard_map/ppermute | solution.py:666
  31.4 1.1 %copy-start.9 = (bf16[3072,128]{1,0:T(8,128)(2,1)S(1)}, bf16[3072,128]{1,0:T(8,128)(2,1)}, u32[]{:S(2)}) copy-start(bf16[3072,128]{1,0:T(8,128)(2,1)} %get-tuple-element.33.out_ref) | copy-start | bytes 2359300
  36.2 9.3 %collective-permute-start.5 = (bf16[384,384]{1,0:T(8,128)(2,1)S(1)}, bf16[384,384]{1,0:T(8,128)(2,1)S(1)}, u32[]{:S(2)}, u32[]{:S(2)}) collective-permute-start(bf16[384,384]{1,0:T(8,128)(2,1)S(1)} %token_finish.3.b_ref), channel_id=1, source_target_pairs={{0,8},{9,1},{18,26},{27,19},{4,20},{13,29},{22,6},{31,15}} | collective-permute-start | bytes 884744 | tf_op jit(solution)/shard_map/ppermute | solution.py:632
  44.1 8.6 %collective-permute-start.3 = (bf16[384,384]{1,0:T(8,128)(2,1)S(1)}, bf16[384,384]{1,0:T(8,128)(2,1)S(1)}, u32[]{:S(2)}, u32[]{:S(2)}) collective-permute-start(bf16[384,384]{1,0:T(8,128)(2,1)S(1)} %token_finish.2.a_ref), channel_id=1, source_target_pairs={{0,8},{9,1},{18,26},{27,19},{4,20},{13,29},{22,6},{31,15}} | collective-permute-start | bytes 884744 | tf_op jit(solution)/shard_map/ppermute | solution.py:632
  45.6 15.1 %collective-permute-start.6 = (bf16[384,384]{1,0:T(8,128)(2,1)S(1)}, bf16[384,384]{1,0:T(8,128)(2,1)S(1)}, u32[]{:S(2)}, u32[]{:S(2)}) collective-permute-start(bf16[384,384]{1,0:T(8,128)(2,1)S(1)} %broadcast_select_fusion), channel_id=1, source_target_pairs={{0,16},{8,24},{1,17},{9,25},{18,2},{26,10},{19,3},{27,11},{4,12},{... | collective-permute-start | bytes 884744 | tf_op jit(solution)/shard_map/ppermute | solution.py:632
  52.8 6.6 %copy-start.3 = (bf16[768,768]{1,0:T(8,128)(2,1)S(1)}, bf16[768,768]{1,0:T(8,128)(2,1)}, u32[]{:S(2)}) copy-start(bf16[768,768]{1,0:T(8,128)(2,1)} %weight_hbm.3) | copy-start | bytes 3538948
  52.8 6.6 %copy-start.5 = (f32[768]{0:T(1024)S(1)}, f32[768]{0:T(1024)}, u32[]{:S(2)}) copy-start(f32[768]{0:T(1024)} %gain_ref.5) | copy-start | bytes 9220
  52.8 7.9 %collective-permute-start.4 = (bf16[384,384]{1,0:T(8,128)(2,1)S(1)}, bf16[384,384]{1,0:T(8,128)(2,1)S(1)}, u32[]{:S(2)}, u32[]{:S(2)}) collective-permute-start(bf16[384,384]{1,0:T(8,128)(2,1)S(1)} %broadcast_select_fusion.1), channel_id=1, source_target_pairs={{0,16},{8,24},{1,17},{9,25},{18,2},{26,10},{19,3},{27,11},{4,12},{... | collective-permute-start | bytes 884744 | tf_op jit(solution)/shard_map/ppermute | solution.py:632
  60.7 1.6 %collective-permute-start.8 = (bf16[384,384]{1,0:T(8,128)(2,1)S(1)}, bf16[384,384]{1,0:T(8,128)(2,1)S(1)}, u32[]{:S(2)}, u32[]{:S(2)}) collective-permute-start(bf16[384,384]{1,0:T(8,128)(2,1)S(1)} %broadcast_select_fusion.2.own_b), channel_id=1, source_target_pairs={{0,4},{4,0},{8,12},{12,8},{16,20},{20,16},{24,28},{28,24},{1,5},{5... | collective-permute-start | bytes 884744 | tf_op jit(solution)/shard_map/ppermute | solution.py:683
  60.8 2.0 %collective-permute-start.7 = (bf16[384,384]{1,0:T(8,128)(2,1)S(1)}, bf16[384,384]{1,0:T(8,128)(2,1)S(1)}, u32[]{:S(2)}, u32[]{:S(2)}) collective-permute-start(bf16[384,384]{1,0:T(8,128)(2,1)S(1)} %broadcast_select_fusion.3.own_a), channel_id=1, source_target_pairs={{0,4},{4,0},{8,12},{12,8},{16,20},{20,16},{24,28},{28,24},{1,5},{5... | collective-permute-start | bytes 884744 | tf_op jit(solution)/shard_map/ppermute | solution.py:681
  62.8 2.3 %copy-start = (bf16[16,192,768]{2,1,0:T(8,128)(2,1)S(1)}, bf16[16,192,768]{2,1,0:T(8,128)(2,1)}, u32[]{:S(2)}) copy-start(bf16[16,192,768]{2,1,0:T(8,128)(2,1)} %constant_dynamic-slice_fusion.1.bias_ref) | copy-start | bytes 14155780
  65.1 1.7 %copy-start.6 = (bf16[768,1536]{1,0:T(8,128)(2,1)S(1)}, bf16[768,1536]{1,0:T(8,128)(2,1)}, u32[]{:S(2)}) copy-start(bf16[768,1536]{1,0:T(8,128)(2,1)} %weight_hbm.5) | copy-start | bytes 7077892
  66.8 4.7 %copy-start.7 = (bf16[768,1536]{1,0:T(8,128)(2,1)S(1)}, bf16[768,1536]{1,0:T(8,128)(2,1)}, u32[]{:S(2)}) copy-start(bf16[768,1536]{1,0:T(8,128)(2,1)} %weight_hbm.5) | copy-start | bytes 7077892
  71.5 2.3 %copy-start.1 = (bf16[16,192,768]{2,1,0:T(8,128)(2,1)S(1)}, bf16[16,192,768]{2,1,0:T(8,128)(2,1)}, u32[]{:S(2)}) copy-start(bf16[16,192,768]{2,1,0:T(8,128)(2,1)} %constant_dynamic-slice_fusion.1.bias_ref) | copy-start | bytes 14155780
  77.9 6.2 %collective-permute-start.11 = (bf16[208,384]{1,0:T(8,128)(2,1)S(1)}, bf16[208,384]{1,0:T(8,128)(2,1)S(1)}, u32[]{:S(2)}, u32[]{:S(2)}) collective-permute-start(bf16[208,384]{1,0:T(8,128)(2,1)S(1)} %get-tuple-element.56), channel_id=1, source_target_pairs={{0,1},{1,0},{2,3},{3,2},{4,5},{5,4},{6,7},{7,6},{8,9},{9,8},{10,11... | collective-permute-start | bytes 479240 | tf_op jit(solution)/shard_map/ppermute | solution.py:703
  81.9 7.9 %collective-permute-start.9 = (bf16[208,384]{1,0:T(8,128)(2,1)S(1)}, bf16[208,384]{1,0:T(8,128)(2,1)S(1)}, u32[]{:S(2)}, u32[]{:S(2)}) collective-permute-start(bf16[208,384]{1,0:T(8,128)(2,1)S(1)} %get-tuple-element.48), channel_id=1, source_target_pairs={{0,1},{1,0},{2,3},{3,2},{4,5},{5,4},{6,7},{7,6},{8,9},{9,8},{10,11... | collective-permute-start | bytes 479240 | tf_op jit(solution)/shard_map/ppermute | solution.py:696
  86.4 7.3 %collective-permute-start.12 = (bf16[208,384]{1,0:T(8,128)(2,1)S(1)}, bf16[208,384]{1,0:T(8,128)(2,1)S(1)}, u32[]{:S(2)}, u32[]{:S(2)}) collective-permute-start(bf16[208,384]{1,0:T(8,128)(2,1)S(1)} %get-tuple-element.59), channel_id=1, source_target_pairs={{0,3},{1,2},{2,1},{3,0},{4,7},{5,6},{6,5},{7,4},{8,11},{9,10},{10,... | collective-permute-start | bytes 479240 | tf_op jit(solution)/shard_map/ppermute | solution.py:690
  89.9 18.1 %copy-start.2 = (bf16[768,768]{1,0:T(8,128)(2,1)S(1)}, bf16[768,768]{1,0:T(8,128)(2,1)}, u32[]{:S(2)}) copy-start(bf16[768,768]{1,0:T(8,128)(2,1)} %weight_ref.9) | copy-start | bytes 3538948
  92.3 9.4 %collective-permute-start.10 = (bf16[208,384]{1,0:T(8,128)(2,1)S(1)}, bf16[208,384]{1,0:T(8,128)(2,1)S(1)}, u32[]{:S(2)}, u32[]{:S(2)}) collective-permute-start(bf16[208,384]{1,0:T(8,128)(2,1)S(1)} %get-tuple-element.52), channel_id=1, source_target_pairs={{0,3},{1,2},{2,1},{3,0},{4,7},{5,6},{6,5},{7,4},{8,11},{9,10},{10,... | collective-permute-start | bytes 479240 | tf_op jit(solution)/shard_map/ppermute | solution.py:690
  94.2 11.8 %collective-permute-start.14 = (bf16[192,384]{1,0:T(8,128)(2,1)S(1)}, bf16[192,384]{1,0:T(8,128)(2,1)S(1)}, u32[]{:S(2)}, u32[]{:S(2)}) collective-permute-start(bf16[192,384]{1,0:T(8,128)(2,1)S(1)} %settle.3.own_b), channel_id=1, source_target_pairs={{0,1},{1,0},{2,3},{3,2},{4,5},{5,4},{6,7},{7,6},{8,9},{9,8},{10,11... | collective-permute-start | bytes 442376 | tf_op jit(solution)/shard_map/ppermute | solution.py:719
  102.2 5.8 %collective-permute-start.13 = (bf16[192,384]{1,0:T(8,128)(2,1)S(1)}, bf16[192,384]{1,0:T(8,128)(2,1)S(1)}, u32[]{:S(2)}, u32[]{:S(2)}) collective-permute-start(bf16[192,384]{1,0:T(8,128)(2,1)S(1)} %settle.2.own_a), channel_id=1, source_target_pairs={{0,1},{1,0},{2,3},{3,2},{4,5},{5,4},{6,7},{7,6},{8,9},{9,8},{10,11... | collective-permute-start | bytes 442376 | tf_op jit(solution)/shard_map/ppermute | solution.py:719

commit v3 on v1

--- a/solution.py
+++ b/solution.py
@@ -295,26 +295,29 @@
     )(msg, weight, sums, counts)
 
 
-def query_kernel(scale, a_ref, b_ref, gain_ref, weight_hbm, out_ref, weight_s, sem):
-    copy = pltpu.make_async_copy(weight_hbm, weight_s, sem)
-    copy.start()
+def query_kernel(scale, a_ref, b_ref, gain_ref, weight_ref, bias_ref, kv_ref, out_ref, bias_out, kv_out):
+    del bias_ref, kv_ref, bias_out, kv_out
     rows = jnp.concatenate([a_ref[...].astype(F32), b_ref[...].astype(F32)], axis=1)
     normed = norm_rows(rows, gain_ref[...].reshape(1, -1)).astype(BF16)
-    copy.wait()
-    out_ref[...] = (dot(normed, weight_s[...]) * scale).astype(BF16)
-
-
-def project_queries(halves, gain, weight):
+    out_ref[...] = (dot(normed, weight_ref[...]) * scale).astype(BF16)
+
+
+def project_queries(halves, gain, weight, bias, kv):
     rows = halves[0].shape[0]
     return pl.pallas_call(
         functools.partial(query_kernel, 1.0 / math.sqrt(weight.shape[1] // TH)),
-        in_specs=[pl.BlockSpec(memory_space=pltpu.VMEM)] * 3 + [pl.BlockSpec(memory_space=pl.ANY)],
-        out_shape=jax.ShapeDtypeStruct((rows, weight.shape[1]), BF16),
-        scratch_shapes=[pltpu.VMEM(weight.shape, BF16), pltpu.SemaphoreType.DMA],
+        in_specs=[pl.BlockSpec(memory_space=pltpu.VMEM)] * 6,
+        out_specs=[pl.BlockSpec(memory_space=pltpu.VMEM)] * 3,
+        out_shape=[
+            jax.ShapeDtypeStruct((rows, weight.shape[1]), BF16),
+            jax.ShapeDtypeStruct(bias.shape, bias.dtype),
+            jax.ShapeDtypeStruct(kv.shape, kv.dtype),
+        ],
+        input_output_aliases={4: 1, 5: 2},
         compiler_params=params(VMEM_SMALL),
         cost_estimate=pl.CostEstimate(flops=5 * 10**8, bytes_accessed=3 * 10**6, transcendentals=0),
         name="queries",
-    )(*halves, gain, weight)
+    )(*halves, gain, weight, bias, kv)
 
 
 GROUPS = 2
@@ -451,8 +454,6 @@
         pltpu.VMEM((2 * rows, LANES), F32),
         pltpu.VMEM((2 * rows, LANES), F32),
         pltpu.VMEM((rows, feats), F32),
-        pltpu.VMEM((2, 2 * feats, feats), BF16),
-        pltpu.SemaphoreType.DMA((2,)),
     ]
 
 
@@ -460,55 +461,38 @@
     return refs[:2], refs[2:4], refs[4:6], refs[6]
 
 
-def weight_copies(group, weight_hbm, refs):
-    weight_s, sems = refs[7:9]
-    feats = weight_s.shape[2]
-    return [
-        pltpu.make_async_copy(
-            weight_hbm.at[:, pl.ds((part * GROUPS + group) * feats, feats)], weight_s.at[part], sems.at[part]
-        )
-        for part in range(2)
-    ]
-
-
-def project_keys(x_ref, weight_s, copies, k_ref, v_ref):
+def project_keys(group, x_ref, weight_ref, k_ref, v_ref):
     tile = x_ref.shape[0] // 2
-    copies[0].wait()
+    feats = v_ref.shape[1]
     for r in range(0, x_ref.shape[0], tile):
-        k_ref[:, r : r + tile] = dot(x_ref[r : r + tile, :], weight_s[0]).T.astype(BF16)
-    copies[1].wait()
-    for r in range(0, x_ref.shape[0], tile):
-        v_ref[r : r + tile, :] = dot(x_ref[r : r + tile, :], weight_s[1]).astype(BF16)
-
-
-def first_kernel(heads, width, half_ref, core_ref, q_ref, own_a, own_b, other_a, other_b, gain_ref, weight_hbm,
-                 bias_ref, x_ref, k_ref, v_ref, msg_ref, *refs):
+        rows = x_ref[r : r + tile, :]
+        k_ref[:, r : r + tile] = dot(rows, weight_ref[:, group * feats : (group + 1) * feats]).T.astype(BF16)
+        at = (GROUPS + group) * feats
+        v_ref[r : r + tile, :] = dot(rows, weight_ref[:, at : at + feats]).astype(BF16)
+
+
+def first_kernel(heads, width, half_ref, core_ref, q_ref, own_a, own_b, other_a, other_b, gain_ref, weight_ref,
+                 bias_ref, x_ref, k_ref, v_ref, msg_ref, kv_out, bias_out, *refs):
     scratch = scratch_of(refs)
-    weights = weight_copies(0, weight_hbm, refs)
-    for copy in weights:
-        copy.start()
     rows = own_a.shape[0]
     core = core_ref[0]
     gain = gain_ref[...].reshape(1, -1)
     for place, parts in ((core, (own_a, own_b)), (1 - core, (other_a, other_b))):
         values = jnp.concatenate([part[...].astype(F32) for part in parts], axis=1)
         x_ref[pl.ds(pl.multiple_of(place * rows, rows), rows), :] = norm_rows(values, gain).astype(BF16)
-    project_keys(x_ref, refs[7], weights, k_ref, v_ref)
+    project_keys(0, x_ref, weight_ref, k_ref, v_ref)
     mixed, lse = attend_group(0, heads, width, half_ref[0], q_ref, k_ref, v_ref, bias_ref, scratch)
     msg_ref[...] = pack_message(mixed, lse, heads)
 
 
-def next_kernel(group, heads, width, half_ref, q_ref, x_ref, weight_hbm, bias_ref, k_ref, v_ref, msg_ref, *refs):
+def next_kernel(group, heads, width, half_ref, q_ref, x_ref, weight_ref, bias_ref, k_ref, v_ref, msg_ref, kv_out, bias_out, *refs):
     scratch = scratch_of(refs)
-    weights = weight_copies(group, weight_hbm, refs)
-    for copy in weights:
-        copy.start()
-    project_keys(x_ref, refs[7], weights, k_ref, v_ref)
+    project_keys(group, x_ref, weight_ref, k_ref, v_ref)
     mixed, lse = attend_group(group, heads, width, half_ref[0], q_ref, k_ref, v_ref, bias_ref, scratch)
     msg_ref[...] = pack_message(mixed, lse, heads)
 
 
-def keep_kernel(group, heads, width, half_ref, q_ref, k_ref, v_ref, near_ref, bias_ref, o_ref, lse_ref, msg_ref, *refs):
+def keep_kernel(group, heads, width, half_ref, q_ref, k_ref, v_ref, near_ref, bias_ref, o_ref, lse_ref, msg_ref, bias_out, *refs):
     scratch = scratch_of(refs)
     mixed, lse = attend_group(group, heads, width, half_ref[0], q_ref, k_ref, v_ref, bias_ref, scratch)
     rows = mixed.shape[0]
@@ -530,6 +514,8 @@
         "lse": ((rows, LANES), F32),
         "msg": ((rows + 2 * heads, feats), BF16),
     }
+    held = ([] if weights is None else [weights]) + [bias]
+    before = 2 + len(scalars) + len(arrays)
     return pl.pallas_call(
         functools.partial(kernel, heads, feats // heads),
         grid_spec=pltpu.PrefetchScalarGridSpec(
@@ -537,16 +523,18 @@
             grid=(1,),
             in_specs=[pl.BlockSpec((tok_rows, feats), lambda i, *_: (0, group))]
             + [full(array.shape) for array in arrays]
-            + [pl.BlockSpec(memory_space=pl.ANY)] * (0 if weights is None else 1)
-            + [pl.BlockSpec(memory_space=pltpu.VMEM)],
-            out_specs=[full(shapes[out][0]) for out in outs],
+            + [pl.BlockSpec(memory_space=pltpu.VMEM)] * len(held),
+            out_specs=[full(shapes[out][0]) for out in outs]
+            + [pl.BlockSpec(memory_space=pltpu.VMEM)] * len(held),
             scratch_shapes=group_scratch(rows, keys, feats, heads),
         ),
-        out_shape=[jax.ShapeDtypeStruct(*shapes[out]) for out in outs],
+        out_shape=[jax.ShapeDtypeStruct(*shapes[out]) for out in outs]
+        + [jax.ShapeDtypeStruct(array.shape, array.dtype) for array in held],
+        input_output_aliases={before + i: len(outs) + i for i in range(len(held))},
         compiler_params=params(VMEM_SMALL),
         cost_estimate=pl.CostEstimate(flops=4 * 10**9, bytes_accessed=4 * 10**6, transcendentals=10**6),
         name=name,
-    )(half, *scalars, q, *arrays, *([] if weights is None else [weights]), bias)
+    )(half, *scalars, q, *arrays, *held)
 
 
 def merge_kernel(heads, o_ref, lse_ref, msg_ref, out_ref, sum_ref, back_ref):
@@ -627,7 +615,7 @@
             fresh = (jnp.bitwise_and(away, ~(known + order[r])) == 0) & (jnp.bitwise_and(away, order[r]) != 0)
             gets = gets | (fresh & (core == c))
         held = [jnp.where(gets, lax.ppermute(part, ("pb", "ka"), pairs), part) for part in held]
-    return held, [lax.ppermute(part, "pb", [(p, p ^ 1) for p in range(n_pb)]) for part in held]
+    return held
 
 
 def body(
@@ -665,35 +653,37 @@
     for part in range(PARTS):
         sums, counts = pool(pos, atom_out, agg_weight, tok2d, tok_rows, part)
         token_repr.append(finish(behind, agg_weight, sums, counts, part))
-    late_bias, token_repr[0] = lax.optimization_barrier((pair_bias, token_repr[0]))
-    own_keys, other_keys = key_parts(token_repr)
-    queries = project_queries(token_repr, token_gain, token_q)
     parity = jnp.bitwise_and(plane ^ (plane >> 1), 1).astype(jnp.int32)
     core = lax.rem(shard, n_pb // n_ka).astype(jnp.int32)
     keep, send = parity.reshape(1), (1 - parity).reshape(1)
+    late_bias, late_kv, token_repr[0] = lax.optimization_barrier((pair_bias, token_kv, token_repr[0]))
+    queries, bias, kv = project_queries(token_repr, token_gain, token_q, late_bias, late_kv)
+    own_keys = key_parts(token_repr)
+    own_keys[0], queries = lax.optimization_barrier((own_keys[0], queries))
+    other_keys = [lax.ppermute(part, "pb", [(p, p ^ 1) for p in range(n_pb)]) for part in own_keys]
     swap = [(i, i ^ 1) for i in range(n_ka)]
     bits = bits_of(n_ka)[1:]
 
     def far(msg, bit):
         return lax.ppermute(msg, "ka", [(i, i ^ (2 * bit - 1)) for i in range(n_ka)])
 
-    x, k, v, msg = group_call(
-        first_kernel, 0, send, (core.reshape(1),), queries, (*own_keys, *other_keys, token_gain), token_kv,
-        late_bias, ("x", "k", "v", "msg"), "attend_first",
+    x, k, v, msg, kv, bias = group_call(
+        first_kernel, 0, send, (core.reshape(1),), queries, (*own_keys, *other_keys, token_gain), kv,
+        bias, ("x", "k", "v", "msg"), "attend_first",
     )
     held, near = [(k, v)], [lax.ppermute(msg, "ka", swap)]
     for g in range(1, GROUPS):
-        k, v, msg = group_call(
-            functools.partial(next_kernel, g), g, send, (), queries, (x,), token_kv,
-            late_bias, ("k", "v", "msg"), "attend_next",
+        k, v, msg, kv, bias = group_call(
+            functools.partial(next_kernel, g), g, send, (), queries, (x,), kv,
+            bias, ("k", "v", "msg"), "attend_next",
         )
         held.append((k, v))
         near.append(lax.ppermute(msg, "ka", swap))
     sums, gone = [], []
     for g in range(GROUPS):
-        o, lse, msg = group_call(
+        o, lse, msg, bias = group_call(
             functools.partial(keep_kernel, g), g, keep, (), queries, (*held[g], near[g]), None,
-            late_bias, ("o", "lse", "msg"), "attend_keep",
+            bias, ("o", "lse", "msg"), "attend_keep",
         )
         sums.append((o, lse))
         gone.append(far(msg, bits[0]))

time: 113 us -> 128 us (1.13)
  the two profiles are of different devices: /device:TPU:0 before, /device:TPU:20 now
where the time goes in v3:
time: 128 us; the launch traced here: 127 us
  Pallas kernels  41.9 us (33%)
  local copies, waits for them, and re-layouts  33.8 us (26%)
  waiting for transfers between devices  28.8 us (22%)
  starting transfers between devices  20 us (16%)
  other arithmetic  2.1 us (2%)
    unnamed x36, local copies, waits for them, and re-layouts  23.2 us
    pallas_call x1, Pallas kernels, atom_attention(): pl.pallas_call(functools.partial(atom_kernel, chunks, atom_total, tok_row...  17.4 us
    pallas_call x4, Pallas kernels, group_call(): pl.pallas_call(functools.partial(kernel, heads, feats // heads), grid_spe...  13.9 us
    optimization_barrier x2, local copies, waits for them, and re-layouts, body(): lax.optimization_barrier((pair_bias, token_kv, token_repr[0]))  9.82 us
    ppermute x2, waiting for transfers between devices, far(): return lax.ppermute(msg, 'ka', [(i, i ^ 2 * bit - 1) for i in range(n_ka)])  8.64 us
    ppermute x4, starting transfers between devices, key_parts(): lax.ppermute(part, ('pb', 'ka'), pairs)  7.37 us
    pallas_call x2, Pallas kernels, pool(): pl.pallas_call(functools.partial(pool_kernel, tok_rows), grid_spec=pltpu....  6.01 us
    ppermute x2, waiting for transfers between devices, body(): other_mix.append(lax.ppermute(own_mix[g], 'ka', swap))  5.74 us
  transfers between devices with their start and end apart: 15, of which 10 were waited for; matrix products, arithmetic and copies ran while one was open for 2% of the time, Pallas kernels for 13%

profile of v3, /device:TPU:20, one launch (start us, length us, event | category | flops | bytes accessed | tf_op | source)
XLA Modules:
  0.0 127.5 jit_solution(1651817368233112845)
XLA Ops:
  0.6 1.7 %copy.33.kv_ref = bf16[768,1536]{1,0:T(8,128)(2,1)S(1)} copy(bf16[768,1536]{1,0:T(8,128)(2,1)} %param.23) | data formatting | bytes 4718592 | tf_op jit(solution)/shard_map/optimization_barrier | solution.py:659
  2.3 8.2 %copy.34.bias_ref = bf16[16,384,768]{2,1,0:T(8,128)(2,1)} copy(bf16[16,384,768]{2,1,0:T(8,128)(2,1)} %param.25) | data formatting | bytes 18874368 | tf_op jit(solution)/shard_map/optimization_barrier | solution.py:659
  11.2 2.8 %collective-permute-start.1 = (bf16[64,128]{1,0:T(8,128)(2,1)S(1)}, bf16[64,128]{1,0:T(8,128)(2,1)S(1)}, u32[]{:S(2)}, u32[]{:S(2)}) collective-permute-start(bf16[64,128]{1,0:T(8,128)(2,1)S(1)} %get-tuple-element.64), channel_id=1, source_target_pairs={{4,0},{8,4},{12,8},{16,12},{20,16},{24,20},{28,24},{5,1},{9,5},{13... | collective-permute-start | bytes 49160 | tf_op jit(solution)/shard_map/ppermute | solution.py:646
  14.0 1.9 %collective-permute-start = (bf16[64,128]{1,0:T(8,128)(2,1)S(1)}, bf16[64,128]{1,0:T(8,128)(2,1)S(1)}, u32[]{:S(2)}, u32[]{:S(2)}) collective-permute-start(bf16[64,128]{1,0:T(8,128)(2,1)S(1)} %get-tuple-element.65), channel_id=1, source_target_pairs={{0,4},{4,8},{8,12},{12,16},{16,20},{20,24},{24,28},{1,5},{5,9},{9,... | collective-permute-start | bytes 49160 | tf_op jit(solution)/shard_map/ppermute | solution.py:645
  15.9 4.0 %collective-permute-done.left_ref = bf16[64,128]{1,0:T(8,128)(2,1)S(1)} collective-permute-done((bf16[64,128]{1,0:T(8,128)(2,1)S(1)}, bf16[64,128]{1,0:T(8,128)(2,1)S(1)}, u32[]{:S(2)}, u32[]{:S(2)}) %collective-permute-start) | collective-permute-done | bytes 16416 | tf_op jit(solution)/shard_map/ppermute | solution.py:645
  20.5 17.4 %atom_attention.1 = (bf16[3072,128]{1,0:T(8,128)(2,1)}, bf16[400,128]{1,0:T(8,128)(2,1)}) custom-call(s32[96]{0:T(128)} %shift_ref.1, s32[1]{0:T(128)} %bitcast.pos_ref, bf16[3072,128]{1,0:T(8,128)(2,1)} %atoms_ref.1, bf16[64,128]{1,0:T(8,128)(2,1)} %copy-done.17, bf16[64,128]{1,0:T(8,128)(2,1)} %copy-done.16, f32[128]{0:T(128)} %gain_ref.3, ...), custom_call_target="tpu_custom_call" | custom-call | flops 8000000000 | bytes 6000000 | tf_op jit(solution)/shard_map/atom_attention/pallas_call | solution.py:169
  38.0 1.9 %collective-permute-start.2 = (bf16[400,128]{1,0:T(8,128)(2,1)}, bf16[400,128]{1,0:T(8,128)(2,1)S(1)}, u32[]{:S(2)}, u32[]{:S(2)}) collective-permute-start(bf16[400,128]{1,0:T(8,128)(2,1)} %get-tuple-element.34), channel_id=1, source_target_pairs={{0,4},{4,8},{8,12},{12,16},{16,20},{20,24},{24,28},{1,5},{5,9},{9,... | collective-permute-start | bytes 307208 | tf_op jit(solution)/shard_map/ppermute | solution.py:651
  41.0 3.0 %pool.3 = (f32[384,384]{1,0:T(8,128)S(1)}, f32[384,128]{1,0:T(8,128)S(1)}) custom-call(s32[1]{0:T(128)} %bitcast.pos_ref, bf16[3072,128]{1,0:T(8,128)(2,1)S(1)} %copy-done.13, bf16[128,768]{1,0:T(8,128)(2,1)S(1)} %copy-done.7, s32[24,128]{1,0:T(8,128)S(1)} %bitcast.6), custom_call_target="tpu_custom_call" | custom-call | flops 2000000000 | bytes 2000000 | tf_op jit(solution)/shard_map/pool/pallas_call | solution.py:241
  45.6 1.3 %collective-permute-start.5 = (bf16[384,384]{1,0:T(8,128)(2,1)S(1)}, bf16[384,384]{1,0:T(8,128)(2,1)S(1)}, u32[]{:S(2)}, u32[]{:S(2)}) collective-permute-start(bf16[384,384]{1,0:T(8,128)(2,1)S(1)} %token_finish.3.b_ref), channel_id=1, source_target_pairs={{0,8},{9,1},{18,26},{27,19},{4,20},{13,29},{22,6},{31,15}} | collective-permute-start | bytes 884744 | tf_op jit(solution)/shard_map/ppermute | solution.py:617
  46.9 3.0 %pool.2 = (f32[384,384]{1,0:T(8,128)S(1)}, f32[384,128]{1,0:T(8,128)S(1)}) custom-call(s32[1]{0:T(128)} %bitcast.pos_ref, bf16[3072,128]{1,0:T(8,128)(2,1)S(1)} %copy-done.13, bf16[128,768]{1,0:T(8,128)(2,1)S(1)} %copy-done.7, s32[24,128]{1,0:T(8,128)S(1)} %bitcast.7), custom_call_target="tpu_custom_call" | custom-call | flops 2000000000 | bytes 2000000 | tf_op jit(solution)/shard_map/pool/pallas_call | solution.py:241
  50.6 2.0 %collective-permute-start.3 = (bf16[384,384]{1,0:T(8,128)(2,1)S(1)}, bf16[384,384]{1,0:T(8,128)(2,1)}, u32[]{:S(2)}, u32[]{:S(2)}) collective-permute-start(bf16[384,384]{1,0:T(8,128)(2,1)S(1)} %token_finish.2.a_ref), channel_id=1, source_target_pairs={{0,8},{9,1},{18,26},{27,19},{4,20},{13,29},{22,6},{31,15}} | collective-permute-start | bytes 884744 | tf_op jit(solution)/shard_map/ppermute | solution.py:617
  52.6 2.0 %collective-permute-start.6 = (bf16[384,384]{1,0:T(8,128)(2,1)S(1)}, bf16[384,384]{1,0:T(8,128)(2,1)}, u32[]{:S(2)}, u32[]{:S(2)}) collective-permute-start(bf16[384,384]{1,0:T(8,128)(2,1)S(1)} %broadcast_select_fusion), channel_id=1, source_target_pairs={{0,16},{8,24},{1,17},{9,25},{18,2},{26,10},{19,3},{27,11},{4,12},{... | collective-permute-start | bytes 884744 | tf_op jit(solution)/shard_map/ppermute | solution.py:617
  54.7 3.5 %collective-permute-done.3 = bf16[384,384]{1,0:T(8,128)(2,1)} collective-permute-done((bf16[384,384]{1,0:T(8,128)(2,1)S(1)}, bf16[384,384]{1,0:T(8,128)(2,1)}, u32[]{:S(2)}, u32[]{:S(2)}) %collective-permute-start.3) | collective-permute-done | bytes 294944 | tf_op jit(solution)/shard_map/ppermute | solution.py:617
  58.2 2.0 %collective-permute-start.4 = (bf16[384,384]{1,0:T(8,128)(2,1)S(1)}, bf16[384,384]{1,0:T(8,128)(2,1)}, u32[]{:S(2)}, u32[]{:S(2)}) collective-permute-start(bf16[384,384]{1,0:T(8,128)(2,1)S(1)} %broadcast_select_fusion.1), channel_id=1, source_target_pairs={{0,16},{8,24},{1,17},{9,25},{18,2},{26,10},{19,3},{27,11},{4,12},{... | collective-permute-start | bytes 884744 | tf_op jit(solution)/shard_map/ppermute | solution.py:617
  60.3 3.7 %copy-done = bf16[16,384,768]{2,1,0:T(8,128)(2,1)S(1)} copy-done((bf16[16,384,768]{2,1,0:T(8,128)(2,1)S(1)}, bf16[16,384,768]{2,1,0:T(8,128)(2,1)}, u32[]{:S(2)}) %copy-start) | copy-done | bytes 9437208
  63.9 1.3 copy-done.5
  66.1 3.6 %copy-done.1 = bf16[16,384,768]{2,1,0:T(8,128)(2,1)} copy-done((bf16[16,384,768]{2,1,0:T(8,128)(2,1)}, bf16[16,384,768]{2,1,0:T(8,128)(2,1)S(1)}, u32[]{:S(2)}) %copy-start.1) | copy-done | bytes 9437208
  73.4 1.2 collective-permute-done.7.other_a
  74.6 3.7 %copy-done.2 = bf16[16,384,768]{2,1,0:T(8,128)(2,1)S(1)} copy-done((bf16[16,384,768]{2,1,0:T(8,128)(2,1)S(1)}, bf16[16,384,768]{2,1,0:T(8,128)(2,1)}, u32[]{:S(2)}) %copy-start.2) | copy-done | bytes 9437208
  79.3 5.6 %attend_first.1 = (bf16[768,768]{1,0:T(8,128)(2,1)S(1)}, bf16[384,768]{1,0:T(8,128)(2,1)S(1)}, bf16[768,384]{1,0:T(8,128)(2,1)S(1)}, bf16[208,384]{1,0:T(8,128)(...) custom-call(s32[1]{0:T(128)} %bitcast.3.half_ref, ...), custom_call_target="tpu_custom_call", output_to_operand_aliasing={{4}: (8, {}), {5}: (9, {})} | custom-call | flops 4000000000 | bytes 4000000 | tf_op jit(solution)/shard_map/attend_first/pallas_call | solution.py:519
  84.9 3.7 %copy-done.3 = bf16[16,384,768]{2,1,0:T(8,128)(2,1)} copy-done((bf16[16,384,768]{2,1,0:T(8,128)(2,1)}, bf16[16,384,768]{2,1,0:T(8,128)(2,1)S(1)}, u32[]{:S(2)}) %copy-start.3) | copy-done | bytes 9437208
  88.5 5.1 %collective-permute-start.9 = (bf16[208,384]{1,0:T(8,128)(2,1)S(1)}, bf16[208,384]{1,0:T(8,128)(2,1)S(1)}, u32[]{:S(2)}, u32[]{:S(2)}) collective-permute-start(bf16[208,384]{1,0:T(8,128)(2,1)S(1)} %get-tuple-element.49), channel_id=1, source_target_pairs={{0,1},{1,0},{2,3},{3,2},{4,5},{5,4},{6,7},{7,6},{8,9},{9,8},{10,11... | collective-permute-start | bytes 479240 | tf_op jit(solution)/shard_map/ppermute | solution.py:674
  93.6 3.7 %copy-done.4 = bf16[16,384,768]{2,1,0:T(8,128)(2,1)S(1)} copy-done((bf16[16,384,768]{2,1,0:T(8,128)(2,1)S(1)}, bf16[16,384,768]{2,1,0:T(8,128)(2,1)}, u32[]{:S(2)}) %copy-start.4) | copy-done | bytes 9437208
  97.3 3.5 %attend_next.1 = (bf16[384,768]{1,0:T(8,128)(2,1)S(1)}, bf16[768,384]{1,0:T(8,128)(2,1)S(1)}, bf16[208,384]{1,0:T(8,128)(2,1)S(1)}, bf16[768,1536]{1,0:T(8,128)(2,1)S(1)}, bf16[16,384,768]{2,1,0:T(8,128)(2,1)S(1)}) custom-call(s32[1]{0:T(128)} %bitcast.3.half_ref, bf16[384,768]{1,0:T(8,128)(2,1)S(1)} %copy-done.11, ...), custom_call_target="tpu_custom_call", output_to_operand_aliasing={{3}: (3, {}), {4}: (4, {})} | custom-call | flops 4000000000 | bytes 4000000 | tf_op jit(solution)/shard_map/attend_next/pallas_call | solution.py:519
  100.9 2.3 %attend_keep.2 = (f32[192,384]{1,0:T(8,128)S(1)}, f32[192,128]{1,0:T(8,128)S(1)}, bf16[208,384]{1,0:T(8,128)(2,1)S(1)}, bf16[16,384,768]{2,1,0:T(8,128)(2,1)S(1)}) custom-call(s32[1]{0:T(128)} %bitcast.2.half_ref, bf16[384,768]{1,0:T(8,128)(2,1)S(1)} %copy-done.11, bf16[384,768]{1,0:T(8,128)(2,1)S(1)} %get-tuple-element.47.k_ref, ...), custom_call_target="tpu_custom_call", output_to_operand_aliasing={{3}: (5, {})} | custom-call | flops 4000000000 | bytes 4000000 | tf_op jit(solution)/shard_map/attend_keep/pallas_call | solution.py:519
  103.3 4.6 %collective-permute-done.11.near_ref = bf16[208,384]{1,0:T(8,128)(2,1)S(1)} collective-permute-done((bf16[208,384]{1,0:T(8,128)(2,1)S(1)}, bf16[208,384]{1,0:T(8,128)(2,1)S(1)}, u32[]{:S(2)}, u32[]{:S(2)}) %collective-permute-start.11) | collective-permute-done | bytes 159776 | tf_op jit(solution)/shard_map/ppermute | solution.py:681
  107.8 2.5 %attend_keep.3 = (f32[192,384]{1,0:T(8,128)S(1)}, f32[192,128]{1,0:T(8,128)S(1)}, bf16[208,384]{1,0:T(8,128)(2,1)S(1)}, bf16[16,384,768]{2,1,0:T(8,128)(2,1)S(1)}) custom-call(s32[1]{0:T(128)} %bitcast.2.half_ref, bf16[384,768]{1,0:T(8,128)(2,1)S(1)} %copy-done.11, bf16[384,768]{1,0:T(8,128)(2,1)S(1)} %get-tuple-element.57.k_ref, ...), custom_call_target="tpu_custom_call", output_to_operand_aliasing={{3}: (5, {})} | custom-call | flops 4000000000 | bytes 4000000 | tf_op jit(solution)/shard_map/attend_keep/pallas_call | solution.py:519
  110.4 6.6 %collective-permute-done.10.msg_ref = bf16[208,384]{1,0:T(8,128)(2,1)S(1)} collective-permute-done((bf16[208,384]{1,0:T(8,128)(2,1)S(1)}, bf16[208,384]{1,0:T(8,128)(2,1)S(1)}, u32[]{:S(2)}, u32[]{:S(2)}) %collective-permute-start.10) | collective-permute-done | bytes 159776 | tf_op jit(solution)/shard_map/ppermute | solution.py:668
  117.6 2.0 %collective-permute-done.12.msg_ref = bf16[208,384]{1,0:T(8,128)(2,1)S(1)} collective-permute-done((bf16[208,384]{1,0:T(8,128)(2,1)S(1)}, bf16[208,384]{1,0:T(8,128)(2,1)S(1)}, u32[]{:S(2)}, u32[]{:S(2)}) %collective-permute-start.12) | collective-permute-done | bytes 159776 | tf_op jit(solution)/shard_map/ppermute | solution.py:668
  120.1 3.4 %collective-permute-done.13.other_a = bf16[192,384]{1,0:T(8,128)(2,1)S(1)} collective-permute-done((bf16[192,384]{1,0:T(8,128)(2,1)S(1)}, bf16[192,384]{1,0:T(8,128)(2,1)S(1)}, u32[]{:S(2)}, u32[]{:S(2)}) %collective-permute-start.13) | collective-permute-done | bytes 147488 | tf_op jit(solution)/shard_map/ppermute | solution.py:697
  123.5 2.4 %collective-permute-done.14.other_b = bf16[192,384]{1,0:T(8,128)(2,1)S(1)} collective-permute-done((bf16[192,384]{1,0:T(8,128)(2,1)S(1)}, bf16[192,384]{1,0:T(8,128)(2,1)S(1)}, u32[]{:S(2)}, u32[]{:S(2)}) %collective-permute-start.14) | collective-permute-done | bytes 147488 | tf_op jit(solution)/shard_map/ppermute | solution.py:697
  125.9 1.6 %output_rows.1 = bf16[384,768]{1,0:T(8,128)(2,1)} custom-call(s32[1]{0:T(128)} %bitcast.2.half_ref, bf16[192,384]{1,0:T(8,128)(2,1)S(1)} %settle.2.own_a, bf16[192,384]{1,0:T(8,128)(2,1)S(1)} %settle.3.own_b, bf16[192,384]{1,0:T(8,128)(2,1)S(1)} %collective-permute-done.13.other_a, bf16[192,384]{1,0:T(8,128)(2,1)S(1)} %collective-permute-done.14.other_b, ...), custom_call_target="tpu_custom_call" | custom-call | tf_op jit(solution)/shard_map/output_rows/pallas_call | solution.py:583
  (54 shorter events, 11.5 us)
Async XLA Ops:
  11.2 4.7 %collective-permute-start.1 = (bf16[64,128]{1,0:T(8,128)(2,1)S(1)}, bf16[64,128]{1,0:T(8,128)(2,1)S(1)}, u32[]{:S(2)}, u32[]{:S(2)}) collective-permute-start(bf16[64,128]{1,0:T(8,128)(2,1)S(1)} %get-tuple-element.64), channel_id=1, source_target_pairs={{4,0},{8,4},{12,8},{16,12},{20,16},{24,20},{28,24},{5,1},{9,5},{13... | collective-permute-start | bytes 49160 | tf_op jit(solution)/shard_map/ppermute | solution.py:646
  14.0 6.0 %collective-permute-start = (bf16[64,128]{1,0:T(8,128)(2,1)S(1)}, bf16[64,128]{1,0:T(8,128)(2,1)S(1)}, u32[]{:S(2)}, u32[]{:S(2)}) collective-permute-start(bf16[64,128]{1,0:T(8,128)(2,1)S(1)} %get-tuple-element.65), channel_id=1, source_target_pairs={{0,4},{4,8},{8,12},{12,16},{16,20},{20,24},{24,28},{1,5},{5,9},{9,... | collective-permute-start | bytes 49160 | tf_op jit(solution)/shard_map/ppermute | solution.py:645
  15.9 4.0 %copy-start.16 = (bf16[64,128]{1,0:T(8,128)(2,1)}, bf16[64,128]{1,0:T(8,128)(2,1)S(1)}, u32[]{:S(2)}) copy-start(bf16[64,128]{1,0:T(8,128)(2,1)S(1)} %collective-permute-done.1.right_ref) | copy-start | bytes 49156
  20.5 19.4 %copy-start.7 = (bf16[128,768]{1,0:T(8,128)(2,1)S(1)}, bf16[128,768]{1,0:T(8,128)(2,1)}, u32[]{:S(2)}) copy-start(bf16[128,768]{1,0:T(8,128)(2,1)} %weight_ref.9) | copy-start | bytes 589828
  20.5 19.4 %copy-start.12 = (s32[3072]{0:T(1024)S(1)}, s32[3072]{0:T(1024)}, u32[]{:S(2)}) copy-start(s32[3072]{0:T(1024)} %param.19) | copy-start | bytes 36868
  38.0 7.1 %collective-permute-start.2 = (bf16[400,128]{1,0:T(8,128)(2,1)}, bf16[400,128]{1,0:T(8,128)(2,1)S(1)}, u32[]{:S(2)}, u32[]{:S(2)}) collective-permute-start(bf16[400,128]{1,0:T(8,128)(2,1)} %get-tuple-element.34), channel_id=1, source_target_pairs={{0,4},{4,8},{8,12},{12,16},{16,20},{20,24},{24,28},{1,5},{5,9},{9,... | collective-permute-start | bytes 307208 | tf_op jit(solution)/shard_map/ppermute | solution.py:651
  39.9 1.1 copy-start.13
  45.6 7.0 %collective-permute-start.5 = (bf16[384,384]{1,0:T(8,128)(2,1)S(1)}, bf16[384,384]{1,0:T(8,128)(2,1)S(1)}, u32[]{:S(2)}, u32[]{:S(2)}) collective-permute-start(bf16[384,384]{1,0:T(8,128)(2,1)S(1)} %token_finish.3.b_ref), channel_id=1, source_target_pairs={{0,8},{9,1},{18,26},{27,19},{4,20},{13,29},{22,6},{31,15}} | collective-permute-start | bytes 884744 | tf_op jit(solution)/shard_map/ppermute | solution.py:617
  50.0 10.3 %copy-start.8 = (f32[768]{0:T(1024)S(1)}, f32[768]{0:T(1024)}, u32[]{:S(2)}) copy-start(f32[768]{0:T(1024)} %gain_ref.5) | copy-start | bytes 9220
  50.6 7.6 %collective-permute-start.3 = (bf16[384,384]{1,0:T(8,128)(2,1)S(1)}, bf16[384,384]{1,0:T(8,128)(2,1)}, u32[]{:S(2)}, u32[]{:S(2)}) collective-permute-start(bf16[384,384]{1,0:T(8,128)(2,1)S(1)} %token_finish.2.a_ref), channel_id=1, source_target_pairs={{0,8},{9,1},{18,26},{27,19},{4,20},{13,29},{22,6},{31,15}} | collective-permute-start | bytes 884744 | tf_op jit(solution)/shard_map/ppermute | solution.py:617
  52.6 13.5 %copy-start.15 = (bf16[384,384]{1,0:T(8,128)(2,1)}, bf16[384,384]{1,0:T(8,128)(2,1)S(1)}, u32[]{:S(2)}) copy-start(bf16[384,384]{1,0:T(8,128)(2,1)S(1)} %broadcast_select_fusion) | copy-start | bytes 884740
  52.6 17.9 %collective-permute-start.6 = (bf16[384,384]{1,0:T(8,128)(2,1)S(1)}, bf16[384,384]{1,0:T(8,128)(2,1)}, u32[]{:S(2)}, u32[]{:S(2)}) collective-permute-start(bf16[384,384]{1,0:T(8,128)(2,1)S(1)} %broadcast_select_fusion), channel_id=1, source_target_pairs={{0,16},{8,24},{1,17},{9,25},{18,2},{26,10},{19,3},{27,11},{4,12},{... | collective-permute-start | bytes 884744 | tf_op jit(solution)/shard_map/ppermute | solution.py:617
  58.2 7.9 %copy-start.14 = (bf16[384,384]{1,0:T(8,128)(2,1)}, bf16[384,384]{1,0:T(8,128)(2,1)S(1)}, u32[]{:S(2)}) copy-start(bf16[384,384]{1,0:T(8,128)(2,1)S(1)} %broadcast_select_fusion.1) | copy-start | bytes 884740
  58.2 13.4 %collective-permute-start.4 = (bf16[384,384]{1,0:T(8,128)(2,1)S(1)}, bf16[384,384]{1,0:T(8,128)(2,1)}, u32[]{:S(2)}, u32[]{:S(2)}) collective-permute-start(bf16[384,384]{1,0:T(8,128)(2,1)S(1)} %broadcast_select_fusion.1), channel_id=1, source_target_pairs={{0,16},{8,24},{1,17},{9,25},{18,2},{26,10},{19,3},{27,11},{4,12},{... | collective-permute-start | bytes 884744 | tf_op jit(solution)/shard_map/ppermute | solution.py:617
  60.3 3.7 %copy-start = (bf16[16,384,768]{2,1,0:T(8,128)(2,1)S(1)}, bf16[16,384,768]{2,1,0:T(8,128)(2,1)}, u32[]{:S(2)}) copy-start(bf16[16,384,768]{2,1,0:T(8,128)(2,1)} %copy.34.bias_ref) | copy-start | bytes 28311556
  63.9 1.3 copy-start.5
  66.1 3.6 %copy-start.1 = (bf16[16,384,768]{2,1,0:T(8,128)(2,1)}, bf16[16,384,768]{2,1,0:T(8,128)(2,1)S(1)}, u32[]{:S(2)}) copy-start(bf16[16,384,768]{2,1,0:T(8,128)(2,1)S(1)} %get-tuple-element.46.bias_ref) | copy-start | bytes 28311556
  69.7 0.8 copy-start.9
  71.6 1.8 %collective-permute-start.8 = (bf16[384,384]{1,0:T(8,128)(2,1)S(1)}, bf16[384,384]{1,0:T(8,128)(2,1)}, u32[]{:S(2)}, u32[]{:S(2)}) collective-permute-start(bf16[384,384]{1,0:T(8,128)(2,1)S(1)} %broadcast_select_fusion.2.own_b), channel_id=1, source_target_pairs={{0,4},{4,0},{8,12},{12,8},{16,20},{20,16},{24,28},{28,24},{1,5},{5... | collective-permute-start | bytes 884744 | tf_op jit(solution)/shard_map/ppermute | solution.py:663
  72.7 1.9 %collective-permute-start.7 = (bf16[384,384]{1,0:T(8,128)(2,1)S(1)}, bf16[384,384]{1,0:T(8,128)(2,1)}, u32[]{:S(2)}, u32[]{:S(2)}) collective-permute-start(bf16[384,384]{1,0:T(8,128)(2,1)S(1)} %broadcast_select_fusion.3.own_a), channel_id=1, source_target_pairs={{0,4},{4,0},{8,12},{12,8},{16,20},{20,16},{24,28},{28,24},{1,5},{5... | collective-permute-start | bytes 884744 | tf_op jit(solution)/shard_map/ppermute | solution.py:663
  74.6 3.7 %copy-start.2 = (bf16[16,384,768]{2,1,0:T(8,128)(2,1)S(1)}, bf16[16,384,768]{2,1,0:T(8,128)(2,1)}, u32[]{:S(2)}) copy-start(bf16[16,384,768]{2,1,0:T(8,128)(2,1)} %copy-done.1) | copy-start | bytes 28311556
  78.2 1.1 copy-start.10
  79.3 14.3 %copy-start.11 = (bf16[384,768]{1,0:T(8,128)(2,1)S(1)}, bf16[384,768]{1,0:T(8,128)(2,1)}, u32[]{:S(2)}) copy-start(bf16[384,768]{1,0:T(8,128)(2,1)} %copy-done.9) | copy-start | bytes 1769476
  84.9 3.7 %copy-start.3 = (bf16[16,384,768]{2,1,0:T(8,128)(2,1)}, bf16[16,384,768]{2,1,0:T(8,128)(2,1)S(1)}, u32[]{:S(2)}) copy-start(bf16[16,384,768]{2,1,0:T(8,128)(2,1)S(1)} %get-tuple-element.52.bias_ref) | copy-start | bytes 28311556
  88.5 12.4 %collective-permute-start.9 = (bf16[208,384]{1,0:T(8,128)(2,1)S(1)}, bf16[208,384]{1,0:T(8,128)(2,1)S(1)}, u32[]{:S(2)}, u32[]{:S(2)}) collective-permute-start(bf16[208,384]{1,0:T(8,128)(2,1)S(1)} %get-tuple-element.49), channel_id=1, source_target_pairs={{0,1},{1,0},{2,3},{3,2},{4,5},{5,4},{6,7},{7,6},{8,9},{9,8},{10,11... | collective-permute-start | bytes 479240 | tf_op jit(solution)/shard_map/ppermute | solution.py:674
  93.6 3.7 %copy-start.4 = (bf16[16,384,768]{2,1,0:T(8,128)(2,1)S(1)}, bf16[16,384,768]{2,1,0:T(8,128)(2,1)}, u32[]{:S(2)}) copy-start(bf16[16,384,768]{2,1,0:T(8,128)(2,1)} %copy-done.3) | copy-start | bytes 28311556
  100.8 7.0 %collective-permute-start.11 = (bf16[208,384]{1,0:T(8,128)(2,1)S(1)}, bf16[208,384]{1,0:T(8,128)(2,1)S(1)}, u32[]{:S(2)}, u32[]{:S(2)}) collective-permute-start(bf16[208,384]{1,0:T(8,128)(2,1)S(1)} %get-tuple-element.59), channel_id=1, source_target_pairs={{0,1},{1,0},{2,3},{3,2},{4,5},{5,4},{6,7},{7,6},{8,9},{9,8},{10,11... | collective-permute-start | bytes 479240 | tf_op jit(solution)/shard_map/ppermute | solution.py:681
  103.2 13.9 %collective-permute-start.10 = (bf16[208,384]{1,0:T(8,128)(2,1)S(1)}, bf16[208,384]{1,0:T(8,128)(2,1)S(1)}, u32[]{:S(2)}, u32[]{:S(2)}) collective-permute-start(bf16[208,384]{1,0:T(8,128)(2,1)S(1)} %get-tuple-element.56), channel_id=1, source_target_pairs={{0,3},{1,2},{2,1},{3,0},{4,7},{5,6},{6,5},{7,4},{8,11},{9,10},{10,... | collective-permute-start | bytes 479240 | tf_op jit(solution)/shard_map/ppermute | solution.py:668
  107.8 18.1 %copy-start.6 = (bf16[768,768]{1,0:T(8,128)(2,1)S(1)}, bf16[768,768]{1,0:T(8,128)(2,1)}, u32[]{:S(2)}) copy-start(bf16[768,768]{1,0:T(8,128)(2,1)} %weight_ref.11) | copy-start | bytes 3538948
  110.3 9.3 %collective-permute-start.12 = (bf16[208,384]{1,0:T(8,128)(2,1)S(1)}, bf16[208,384]{1,0:T(8,128)(2,1)S(1)}, u32[]{:S(2)}, u32[]{:S(2)}) collective-permute-start(bf16[208,384]{1,0:T(8,128)(2,1)S(1)} %get-tuple-element.63), channel_id=1, source_target_pairs={{0,3},{1,2},{2,1},{3,0},{4,7},{5,6},{6,5},{7,4},{8,11},{9,10},{10,... | collective-permute-start | bytes 479240 | tf_op jit(solution)/shard_map/ppermute | solution.py:668
  117.5 6.0 %collective-permute-start.13 = (bf16[192,384]{1,0:T(8,128)(2,1)S(1)}, bf16[192,384]{1,0:T(8,128)(2,1)S(1)}, u32[]{:S(2)}, u32[]{:S(2)}) collective-permute-start(bf16[192,384]{1,0:T(8,128)(2,1)S(1)} %settle.2.own_a), channel_id=1, source_target_pairs={{0,1},{1,0},{2,3},{3,2},{4,5},{5,4},{6,7},{7,6},{8,9},{9,8},{10,11... | collective-permute-start | bytes 442376 | tf_op jit(solution)/shard_map/ppermute | solution.py:697
  120.1 5.8 %collective-permute-start.14 = (bf16[192,384]{1,0:T(8,128)(2,1)S(1)}, bf16[192,384]{1,0:T(8,128)(2,1)S(1)}, u32[]{:S(2)}, u32[]{:S(2)}) collective-permute-start(bf16[192,384]{1,0:T(8,128)(2,1)S(1)} %settle.3.own_b), channel_id=1, source_target_pairs={{0,1},{1,0},{2,3},{3,2},{4,5},{5,4},{6,7},{7,6},{8,9},{9,8},{10,11... | collective-permute-start | bytes 442376 | tf_op jit(solution)/shard_map/ppermute | solution.py:697
  (1 other events, 0.6 us)

commit v4 on v2

--- a/solution.py
+++ b/solution.py
@@ -54,7 +54,6 @@
     bias_ref,
     tok_ref,
     out_ref,
-    near_ref,
     msg_ref,
     q_s,
     k_s,
@@ -139,7 +138,6 @@
         own = atoms_ref[pl.ds(at, atoms_group), :].astype(F32)
         result = own + dot(jnp.concatenate(merged, axis=0), proj_ref[...])
         out_ref[local : local + atoms_group, :] = result.astype(BF16)
-        near_ref[local : local + atoms_group, :] = result.astype(BF16)
 
     groups = blocks // group
     ahead = score(0)
@@ -185,7 +183,6 @@
             ],
             out_specs=[
                 pl.BlockSpec((size, width), lambda i, *_: (i, 0)),
-                pl.BlockSpec((size, width), lambda i, *_: (i, 0)),
                 full((SHIFT_MAX + 16, width)),
             ],
             scratch_shapes=[
@@ -196,7 +193,6 @@
             ],
         ),
         out_shape=[
-            jax.ShapeDtypeStruct((rows, width), BF16),
             jax.ShapeDtypeStruct((rows, width), BF16),
             jax.ShapeDtypeStruct((SHIFT_MAX + 16, width), BF16),
         ],
@@ -659,30 +655,25 @@
     tok2d = token_of_atom.reshape(rows // LANES, LANES)
     left = lax.ppermute(atoms[rows - half :], "pb", up)
     right = lax.ppermute(atoms[:half], "pb", down)
-    atom_out, near_out, msg = atom_attention(
+    atom_out, msg = atom_attention(
         window_shift, pos, atoms, left, right, atom_gain, atom_qkv, atom_proj,
         atom_bias, tok2d, tok_rows, rows * n_pb,
     )
     behind = lax.ppermute(msg, "pb", up)
     token_repr = []
     for part in range(PARTS):
-        sums, counts = pool(pos, near_out, agg_weight, tok2d, tok_rows, part)
+        sums, counts = pool(pos, atom_out, agg_weight, tok2d, tok_rows, part)
         token_repr.append(finish(behind, agg_weight, sums, counts, part))
-    late_bias, token_repr[0] = lax.optimization_barrier((pair_bias, token_repr[0]))
     parity = jnp.bitwise_and(plane ^ (plane >> 1), 1).astype(jnp.int32)
     core = lax.rem(shard, n_pb // n_ka).astype(jnp.int32)
     keep, send = parity.reshape(1), (1 - parity).reshape(1)
     share = tok_rows // 2
-    send_bias = lax.dynamic_slice_in_dim(late_bias, (1 - parity) * share, share, axis=1)
     queries = project_queries(token_repr, token_gain, token_q)
     own_keys = key_parts(token_repr)
-    own_keys[0], queries, send_bias = lax.optimization_barrier((own_keys[0], queries, send_bias))
-    cores = [(p, p ^ 1) for p in range(n_pb)]
-    other_keys = [lax.ppermute(own_keys[0], "pb", cores)]
-    late_bias, own_keys[1] = lax.optimization_barrier((late_bias, own_keys[1]))
-    other_keys.append(lax.ppermute(own_keys[1], "pb", cores))
-    late_bias, send_bias = lax.optimization_barrier((late_bias, send_bias))
-    keep_bias = lax.dynamic_slice_in_dim(late_bias, parity * share, share, axis=1)
+    own_keys[0], queries = lax.optimization_barrier((own_keys[0], queries))
+    other_keys = [lax.ppermute(part, "pb", [(p, p ^ 1) for p in range(n_pb)]) for part in own_keys]
+    bias, *own_keys = lax.optimization_barrier((pair_bias, *own_keys))
+    send_bias = lax.dynamic_slice_in_dim(bias, (1 - parity) * share, share, axis=1)
     swap = [(i, i ^ 1) for i in range(n_ka)]
     bits = bits_of(n_ka)[1:]
 
@@ -694,6 +685,8 @@
         send_bias, ("x", "k", "v", "msg"), "attend_first",
     )
     held, near = [(k, v)], [lax.ppermute(msg, "ka", swap)]
+    bias, x = lax.optimization_barrier((bias, x))
+    keep_bias = lax.dynamic_slice_in_dim(bias, parity * share, share, axis=1)
     for g in range(1, GROUPS):
         k, v, msg = group_call(
             functools.partial(next_kernel, g), g, send, (), queries, (x,), token_kv,

time: 110 us -> 105 us (0.955)
  local copies, waits for them, and re-layouts: 16.4 us -> 5.89 us
  waiting for transfers between devices: 17.6 us -> 21.9 us
    unnamed x24, local copies, waits for them, and re-layouts: 8.09 us -> 2.02 us
    dynamic_slice x2, local copies, waits for them, and re-layouts: 7.55 us -> 3.13 us  [the longest x1 2.8 us: body(): lax.dynamic_slice_in_dim(bias, (1 - parity) * share, share, axis=1)]
    ppermute x1, waiting for transfers between devices: 1.41 us -> 4.59 us  [body(): near.append(lax.ppermute(msg, 'ka', swap))]
    ppermute x4, waiting for transfers between devices: 5.87 us -> 8.52 us  [key_parts(): lax.ppermute(part, ('pb', 'ka'), pairs)]
    ppermute x2, waiting for transfers between devices: 1.49 us -> 0.01 us  [body(): lax.ppermute(part, 'pb', [(p, p ^ 1) for p in range(n_pb)])]
    ppermute x2, starting transfers between devices: 3.95 us -> 5.26 us  [far(): return lax.ppermute(msg, 'ka', [(i, i ^ 2 * bit - 1) for i in range(n_ka)])]
  transfers between devices with their start and end apart: 15 -> 15, of which waited for: 8 -> 7; matrix products, arithmetic and copies ran while one was open for 7% -> 3% of each run, Pallas kernels for 12% -> 13%
where the time goes in v4:
time: 105 us; the launch traced here: 104 us
  Pallas kernels  42.1 us (40%)
  starting transfers between devices  32.9 us (31%)
  waiting for transfers between devices  21.9 us (21%)
  local copies, waits for them, and re-layouts  5.89 us (6%)
    pallas_call x1, Pallas kernels, atom_attention(): pl.pallas_call(functools.partial(atom_kernel, chunks, atom_total, tok_row...  17.4 us
    pallas_call x4, Pallas kernels, group_call(): pl.pallas_call(functools.partial(kernel, heads, feats // heads), grid_spe...  13.8 us
    ppermute x4, starting transfers between devices, key_parts(): lax.ppermute(part, ('pb', 'ka'), pairs)  8.55 us
    ppermute x4, waiting for transfers between devices, key_parts(): lax.ppermute(part, ('pb', 'ka'), pairs)  8.52 us
    ppermute x2, starting transfers between devices, body(): other_mix.append(lax.ppermute(own_mix[g], 'ka', swap))  8.46 us
    pallas_call x2, Pallas kernels, pool(): pl.pallas_call(functools.partial(pool_kernel, tok_rows), grid_spec=pltpu....  6 us
    ppermute x2, starting transfers between devices, far(): return lax.ppermute(msg, 'ka', [(i, i ^ 2 * bit - 1) for i in range(n_ka)])  5.26 us
    ppermute x1, waiting for transfers between devices, body(): near.append(lax.ppermute(msg, 'ka', swap))  4.59 us
  transfers between devices with their start and end apart: 15, of which 7 were waited for; matrix products, arithmetic and copies ran while one was open for 3% of the time, Pallas kernels for 13%

profile of v4, /device:TPU:0, one launch (start us, length us, event | category | flops | bytes accessed | tf_op | source)
XLA Modules:
  0.0 104.0 jit_solution(8772873442628155131)
XLA Ops:
  0.6 0.7 fusion
  1.4 2.3 %collective-permute-start = (bf16[64,128]{1,0:T(8,128)(2,1)S(1)}, bf16[64,128]{1,0:T(8,128)(2,1)S(1)}, u32[]{:S(2)}, u32[]{:S(2)}) collective-permute-start(bf16[64,128]{1,0:T(8,128)(2,1)S(1)} %get-tuple-element.55), channel_id=1, source_target_pairs={{0,4},{4,8},{8,12},{12,16},{16,20},{20,24},{24,28},{1,5},{5,9},{9,... | collective-permute-start | bytes 49160 | tf_op jit(solution)/shard_map/ppermute | solution.py:656
  3.7 1.3 %collective-permute-start.1 = (bf16[64,128]{1,0:T(8,128)(2,1)S(1)}, bf16[64,128]{1,0:T(8,128)(2,1)S(1)}, u32[]{:S(2)}, u32[]{:S(2)}) collective-permute-start(bf16[64,128]{1,0:T(8,128)(2,1)S(1)} %get-tuple-element.54), channel_id=1, source_target_pairs={{4,0},{8,4},{12,8},{16,12},{20,16},{24,20},{28,24},{5,1},{9,5},{13... | collective-permute-start | bytes 49160 | tf_op jit(solution)/shard_map/ppermute | solution.py:657
  5.0 3.9 %collective-permute-done.1.right_ref = bf16[64,128]{1,0:T(8,128)(2,1)S(1)} collective-permute-done((bf16[64,128]{1,0:T(8,128)(2,1)S(1)}, bf16[64,128]{1,0:T(8,128)(2,1)S(1)}, u32[]{:S(2)}, u32[]{:S(2)}) %collective-permute-start.1) | collective-permute-done | bytes 16416 | tf_op jit(solution)/shard_map/ppermute | solution.py:657
  8.9 0.6 copy-done.8
  9.5 17.4 %atom_attention.1 = (bf16[3072,128]{1,0:T(8,128)(2,1)}, bf16[400,128]{1,0:T(8,128)(2,1)}) custom-call(s32[96]{0:T(128)} %shift_ref.1, s32[1]{0:T(128)} %bitcast.pos_ref, bf16[3072,128]{1,0:T(8,128)(2,1)} %atoms_ref.1, bf16[64,128]{1,0:T(8,128)(2,1)} %copy-done.7, bf16[64,128]{1,0:T(8,128)(2,1)} %copy-done.8, f32[128]{0:T(128)} %gain_ref.3, ...), custom_call_target="tpu_custom_call" | custom-call | flops 8000000000 | bytes 6000000 | tf_op jit(solution)/shard_map/atom_attention/pallas_call | solution.py:169
  26.9 4.4 %collective-permute-start.2 = (bf16[400,128]{1,0:T(8,128)(2,1)}, bf16[400,128]{1,0:T(8,128)(2,1)S(1)}, u32[]{:S(2)}, u32[]{:S(2)}) collective-permute-start(bf16[400,128]{1,0:T(8,128)(2,1)} %get-tuple-element.29), channel_id=1, source_target_pairs={{0,4},{4,8},{8,12},{12,16},{16,20},{20,24},{24,28},{1,5},{5,9},{9,... | collective-permute-start | bytes 307208 | tf_op jit(solution)/shard_map/ppermute | solution.py:662
  31.4 1.1 %copy-done.6 = bf16[3072,128]{1,0:T(8,128)(2,1)S(1)} copy-done((bf16[3072,128]{1,0:T(8,128)(2,1)S(1)}, bf16[3072,128]{1,0:T(8,128)(2,1)}, u32[]{:S(2)}) %copy-start.6) | copy-done | bytes 786456
  32.5 3.0 %pool.2 = (f32[384,384]{1,0:T(8,128)S(1)}, f32[384,128]{1,0:T(8,128)S(1)}) custom-call(s32[1]{0:T(128)} %bitcast.pos_ref, bf16[3072,128]{1,0:T(8,128)(2,1)S(1)} %copy-done.6, bf16[128,768]{1,0:T(8,128)(2,1)S(1)} %copy-done.2, s32[24,128]{1,0:T(8,128)S(1)} %bitcast.6), custom_call_target="tpu_custom_call" | custom-call | flops 2000000000 | bytes 2000000 | tf_op jit(solution)/shard_map/pool/pallas_call | solution.py:241
  36.1 4.4 %collective-permute-start.3 = (bf16[384,384]{1,0:T(8,128)(2,1)S(1)}, bf16[384,384]{1,0:T(8,128)(2,1)S(1)}, u32[]{:S(2)}, u32[]{:S(2)}) collective-permute-start(bf16[384,384]{1,0:T(8,128)(2,1)S(1)} %token_finish.2.a_ref), channel_id=1, source_target_pairs={{0,8},{9,1},{18,26},{27,19},{4,20},{13,29},{22,6},{31,15}} | collective-permute-start | bytes 884744 | tf_op jit(solution)/shard_map/ppermute | solution.py:628
  40.5 3.0 %pool.3 = (f32[384,384]{1,0:T(8,128)S(1)}, f32[384,128]{1,0:T(8,128)S(1)}) custom-call(s32[1]{0:T(128)} %bitcast.pos_ref, bf16[3072,128]{1,0:T(8,128)(2,1)S(1)} %copy-done.6, bf16[128,768]{1,0:T(8,128)(2,1)S(1)} %copy-done.2, s32[24,128]{1,0:T(8,128)S(1)} %bitcast.7), custom_call_target="tpu_custom_call" | custom-call | flops 2000000000 | bytes 2000000 | tf_op jit(solution)/shard_map/pool/pallas_call | solution.py:241
  44.1 1.3 %collective-permute-start.5 = (bf16[384,384]{1,0:T(8,128)(2,1)S(1)}, bf16[384,384]{1,0:T(8,128)(2,1)S(1)}, u32[]{:S(2)}, u32[]{:S(2)}) collective-permute-start(bf16[384,384]{1,0:T(8,128)(2,1)S(1)} %token_finish.3.b_ref), channel_id=1, source_target_pairs={{0,8},{9,1},{18,26},{27,19},{4,20},{13,29},{22,6},{31,15}} | collective-permute-start | bytes 884744 | tf_op jit(solution)/shard_map/ppermute | solution.py:628
  45.5 1.3 %collective-permute-start.4 = (bf16[384,384]{1,0:T(8,128)(2,1)S(1)}, bf16[384,384]{1,0:T(8,128)(2,1)S(1)}, u32[]{:S(2)}, u32[]{:S(2)}) collective-permute-start(bf16[384,384]{1,0:T(8,128)(2,1)S(1)} %broadcast_select_fusion.1), channel_id=1, source_target_pairs={{0,16},{8,24},{1,17},{9,25},{18,2},{26,10},{19,3},{27,11},{4,12},{... | collective-permute-start | bytes 884744 | tf_op jit(solution)/shard_map/ppermute | solution.py:628
  46.9 5.9 %collective-permute-done.5 = bf16[384,384]{1,0:T(8,128)(2,1)S(1)} collective-permute-done((bf16[384,384]{1,0:T(8,128)(2,1)S(1)}, bf16[384,384]{1,0:T(8,128)(2,1)S(1)}, u32[]{:S(2)}, u32[]{:S(2)}) %collective-permute-start.5) | collective-permute-done | bytes 294944 | tf_op jit(solution)/shard_map/ppermute | solution.py:628
  52.8 1.5 %collective-permute-start.6 = (bf16[384,384]{1,0:T(8,128)(2,1)S(1)}, bf16[384,384]{1,0:T(8,128)(2,1)S(1)}, u32[]{:S(2)}, u32[]{:S(2)}) collective-permute-start(bf16[384,384]{1,0:T(8,128)(2,1)S(1)} %broadcast_select_fusion), channel_id=1, source_target_pairs={{0,16},{8,24},{1,17},{9,25},{18,2},{26,10},{19,3},{27,11},{4,12},{... | collective-permute-start | bytes 884744 | tf_op jit(solution)/shard_map/ppermute | solution.py:628
  54.3 1.3 %queries.1.q_ref = bf16[384,768]{1,0:T(8,128)(2,1)S(1)} custom-call(bf16[384,384]{1,0:T(8,128)(2,1)S(1)} %token_finish.2.a_ref, bf16[384,384]{1,0:T(8,128)(2,1)S(1)} %token_finish.3.b_ref, f32[768]{0:T(1024)S(1)} %copy-done.3, bf16[768,768]{1,0:T(8,128)(2,1)S(1)} %copy-done.1), custom_call_target="tpu_custom_call" | custom-call | flops 500000000 | bytes 3000000 | tf_op jit(solution)/shard_map/queries/pallas_call | solution.py:309
  55.6 2.6 %collective-permute-done.6 = bf16[384,384]{1,0:T(8,128)(2,1)S(1)} collective-permute-done((bf16[384,384]{1,0:T(8,128)(2,1)S(1)}, bf16[384,384]{1,0:T(8,128)(2,1)S(1)}, u32[]{:S(2)}, u32[]{:S(2)}) %collective-permute-start.6) | collective-permute-done | bytes 294944 | tf_op jit(solution)/shard_map/ppermute | solution.py:628
  58.9 2.8 %constant_dynamic-slice_fusion.1.bias_ref = bf16[16,192,768]{2,1,0:T(8,128)(2,1)S(1)} fusion(bf16[16,384,768]{2,1,0:T(8,128)(2,1)} %param.25, s32[]{:T(128)S(6)} %select_n.40), kind=kLoop, calls=%fused_computation.5 | loop fusion | bytes 9437188 | tf_op jit(solution)/shard_map/dynamic_slice | solution.py:676
  62.0 4.7 %attend_first.1 = (bf16[768,768]{1,0:T(8,128)(2,1)S(1)}, bf16[384,768]{1,0:T(8,128)(2,1)S(1)}, bf16[768,384]{1,0:T(8,128)(2,1)S(1)}, bf16[208,384]{1,0:T(8,128)(2,1)S(1)}) custom-call(s32[1]{0:T(128)} %bitcast.3.half_ref, s32[1]{0:T(128)} %bitcast.4.core_ref, bf16[384,768]{1,0:T(8,128)(2,1)S(1)} %queries.1.q_ref, ...), custom_call_target="tpu_custom_call" | custom-call | flops 4000000000 | bytes 4000000 | tf_op jit(solution)/shard_map/attend_first/pallas_call | solution.py:532
  66.7 4.2 %attend_next.1 = (bf16[384,768]{1,0:T(8,128)(2,1)S(1)}, bf16[768,384]{1,0:T(8,128)(2,1)S(1)}, bf16[208,384]{1,0:T(8,128)(2,1)S(1)}) custom-call(s32[1]{0:T(128)} %bitcast.3.half_ref, bf16[384,768]{1,0:T(8,128)(2,1)S(1)} %queries.1.q_ref, bf16[768,768]{1,0:T(8,128)(2,1)S(1)} %get-tuple-element.47.x_ref, bf16[768,1536]{1,0:T(8,128)(2,1)S(1)} %copy-done.4, ...), custom_call_target="tpu_custom_call" | custom-call | flops 4000000000 | bytes 4000000 | tf_op jit(solution)/shard_map/attend_next/pallas_call | solution.py:532
  70.9 1.4 %collective-permute-start.11 = (bf16[208,384]{1,0:T(8,128)(2,1)S(1)}, bf16[208,384]{1,0:T(8,128)(2,1)S(1)}, u32[]{:S(2)}, u32[]{:S(2)}) collective-permute-start(bf16[208,384]{1,0:T(8,128)(2,1)S(1)} %get-tuple-element.50), channel_id=1, source_target_pairs={{0,1},{1,0},{2,3},{3,2},{4,5},{5,4},{6,7},{7,6},{8,9},{9,8},{10,11... | collective-permute-start | bytes 479240 | tf_op jit(solution)/shard_map/ppermute | solution.py:696
  72.3 0.7 collective-permute-start.9
  73.3 4.6 %collective-permute-done.11.near_ref = bf16[208,384]{1,0:T(8,128)(2,1)S(1)} collective-permute-done((bf16[208,384]{1,0:T(8,128)(2,1)S(1)}, bf16[208,384]{1,0:T(8,128)(2,1)S(1)}, u32[]{:S(2)}, u32[]{:S(2)}) %collective-permute-start.11) | collective-permute-done | bytes 159776 | tf_op jit(solution)/shard_map/ppermute | solution.py:696
  77.9 2.5 %attend_keep.3 = (f32[192,384]{1,0:T(8,128)S(1)}, f32[192,128]{1,0:T(8,128)S(1)}, bf16[208,384]{1,0:T(8,128)(2,1)S(1)}) custom-call(s32[1]{0:T(128)} %bitcast.2.half_ref, bf16[384,768]{1,0:T(8,128)(2,1)S(1)} %queries.1.q_ref, bf16[384,768]{1,0:T(8,128)(2,1)S(1)} %get-tuple-element.48.k_ref, bf16[768,384]{1,0:T(8,128)(2,1)S(1)} %get-tuple-element.49.v_ref, ...), custom_call_target="tpu_custom_call" | custom-call | flops 4000000000 | bytes 4000000 | tf_op jit(solution)/shard_map/attend_keep/pallas_call | solution.py:532
  80.4 5.2 %collective-permute-start.12 = (bf16[208,384]{1,0:T(8,128)(2,1)S(1)}, bf16[208,384]{1,0:T(8,128)(2,1)S(1)}, u32[]{:S(2)}, u32[]{:S(2)}) collective-permute-start(bf16[208,384]{1,0:T(8,128)(2,1)S(1)} %get-tuple-element.53), channel_id=1, source_target_pairs={{0,3},{1,2},{2,1},{3,0},{4,7},{5,6},{6,5},{7,4},{8,11},{9,10},{10,... | collective-permute-start | bytes 479240 | tf_op jit(solution)/shard_map/ppermute | solution.py:681
  85.5 2.5 %attend_keep.2 = (f32[192,384]{1,0:T(8,128)S(1)}, f32[192,128]{1,0:T(8,128)S(1)}, bf16[208,384]{1,0:T(8,128)(2,1)S(1)}) custom-call(s32[1]{0:T(128)} %bitcast.2.half_ref, bf16[384,768]{1,0:T(8,128)(2,1)S(1)} %queries.1.q_ref, bf16[384,768]{1,0:T(8,128)(2,1)S(1)} %get-tuple-element.39.k_ref, bf16[768,384]{1,0:T(8,128)(2,1)S(1)} %get-tuple-element.40.v_ref, ...), custom_call_target="tpu_custom_call" | custom-call | flops 4000000000 | bytes 4000000 | tf_op jit(solution)/shard_map/attend_keep/pallas_call | solution.py:532
  88.1 1.2 %collective-permute-done.12.msg_ref = bf16[208,384]{1,0:T(8,128)(2,1)S(1)} collective-permute-done((bf16[208,384]{1,0:T(8,128)(2,1)S(1)}, bf16[208,384]{1,0:T(8,128)(2,1)S(1)}, u32[]{:S(2)}, u32[]{:S(2)}) %collective-permute-start.12) | collective-permute-done | bytes 159776 | tf_op jit(solution)/shard_map/ppermute | solution.py:681
  89.7 6.4 %collective-permute-start.14 = (bf16[192,384]{1,0:T(8,128)(2,1)S(1)}, bf16[192,384]{1,0:T(8,128)(2,1)S(1)}, u32[]{:S(2)}, u32[]{:S(2)}) collective-permute-start(bf16[192,384]{1,0:T(8,128)(2,1)S(1)} %settle.3.own_b), channel_id=1, source_target_pairs={{0,1},{1,0},{2,3},{3,2},{4,5},{5,4},{6,7},{7,6},{8,9},{9,8},{10,11... | collective-permute-start | bytes 442376 | tf_op jit(solution)/shard_map/ppermute | solution.py:712
  96.6 2.0 %collective-permute-start.13 = (bf16[192,384]{1,0:T(8,128)(2,1)S(1)}, bf16[192,384]{1,0:T(8,128)(2,1)S(1)}, u32[]{:S(2)}, u32[]{:S(2)}) collective-permute-start(bf16[192,384]{1,0:T(8,128)(2,1)S(1)} %settle.2.own_a), channel_id=1, source_target_pairs={{0,1},{1,0},{2,3},{3,2},{4,5},{5,4},{6,7},{7,6},{8,9},{9,8},{10,11... | collective-permute-start | bytes 442376 | tf_op jit(solution)/shard_map/ppermute | solution.py:712
  98.7 1.3 %collective-permute-done.14.other_b = bf16[192,384]{1,0:T(8,128)(2,1)S(1)} collective-permute-done((bf16[192,384]{1,0:T(8,128)(2,1)S(1)}, bf16[192,384]{1,0:T(8,128)(2,1)S(1)}, u32[]{:S(2)}, u32[]{:S(2)}) %collective-permute-start.14) | collective-permute-done | bytes 147488 | tf_op jit(solution)/shard_map/ppermute | solution.py:712
  99.9 2.5 %collective-permute-done.13.other_a = bf16[192,384]{1,0:T(8,128)(2,1)S(1)} collective-permute-done((bf16[192,384]{1,0:T(8,128)(2,1)S(1)}, bf16[192,384]{1,0:T(8,128)(2,1)S(1)}, u32[]{:S(2)}, u32[]{:S(2)}) %collective-permute-start.13) | collective-permute-done | bytes 147488 | tf_op jit(solution)/shard_map/ppermute | solution.py:712
  102.4 1.6 %output_rows.1 = bf16[384,768]{1,0:T(8,128)(2,1)} custom-call(s32[1]{0:T(128)} %bitcast.2.half_ref, bf16[192,384]{1,0:T(8,128)(2,1)S(1)} %settle.2.own_a, bf16[192,384]{1,0:T(8,128)(2,1)S(1)} %settle.3.own_b, bf16[192,384]{1,0:T(8,128)(2,1)S(1)} %collective-permute-done.13.other_a, bf16[192,384]{1,0:T(8,128)(2,1)S(1)} %collective-permute-done.14.other_b, ...), custom_call_target="tpu_custom_call" | custom-call | tf_op jit(solution)/shard_map/output_rows/pallas_call | solution.py:594
  (43 shorter events, 3.5 us)
Async XLA Ops:
  1.4 3.7 %collective-permute-start = (bf16[64,128]{1,0:T(8,128)(2,1)S(1)}, bf16[64,128]{1,0:T(8,128)(2,1)S(1)}, u32[]{:S(2)}, u32[]{:S(2)}) collective-permute-start(bf16[64,128]{1,0:T(8,128)(2,1)S(1)} %get-tuple-element.55), channel_id=1, source_target_pairs={{0,4},{4,8},{8,12},{12,16},{16,20},{20,24},{24,28},{1,5},{5,9},{9,... | collective-permute-start | bytes 49160 | tf_op jit(solution)/shard_map/ppermute | solution.py:656
  3.7 5.2 %collective-permute-start.1 = (bf16[64,128]{1,0:T(8,128)(2,1)S(1)}, bf16[64,128]{1,0:T(8,128)(2,1)S(1)}, u32[]{:S(2)}, u32[]{:S(2)}) collective-permute-start(bf16[64,128]{1,0:T(8,128)(2,1)S(1)} %get-tuple-element.54), channel_id=1, source_target_pairs={{4,0},{8,4},{12,8},{16,12},{20,16},{24,20},{28,24},{5,1},{9,5},{13... | collective-permute-start | bytes 49160 | tf_op jit(solution)/shard_map/ppermute | solution.py:657
  5.0 3.9 %copy-start.7 = (bf16[64,128]{1,0:T(8,128)(2,1)}, bf16[64,128]{1,0:T(8,128)(2,1)S(1)}, u32[]{:S(2)}) copy-start(bf16[64,128]{1,0:T(8,128)(2,1)S(1)} %collective-permute-done.left_ref) | copy-start | bytes 49156
  8.9 0.6 copy-start.8
  9.5 21.8 %copy-start.2 = (bf16[128,768]{1,0:T(8,128)(2,1)S(1)}, bf16[128,768]{1,0:T(8,128)(2,1)}, u32[]{:S(2)}) copy-start(bf16[128,768]{1,0:T(8,128)(2,1)} %weight_ref.8) | copy-start | bytes 589828
  9.5 21.8 %copy-start.5 = (s32[3072]{0:T(1024)S(1)}, s32[3072]{0:T(1024)}, u32[]{:S(2)}) copy-start(s32[3072]{0:T(1024)} %param.19) | copy-start | bytes 36868
  26.9 8.5 %collective-permute-start.2 = (bf16[400,128]{1,0:T(8,128)(2,1)}, bf16[400,128]{1,0:T(8,128)(2,1)S(1)}, u32[]{:S(2)}, u32[]{:S(2)}) collective-permute-start(bf16[400,128]{1,0:T(8,128)(2,1)} %get-tuple-element.29), channel_id=1, source_target_pairs={{0,4},{4,8},{8,12},{12,16},{16,20},{20,24},{24,28},{1,5},{5,9},{9,... | collective-permute-start | bytes 307208 | tf_op jit(solution)/shard_map/ppermute | solution.py:662
  31.3 1.1 %copy-start.6 = (bf16[3072,128]{1,0:T(8,128)(2,1)S(1)}, bf16[3072,128]{1,0:T(8,128)(2,1)}, u32[]{:S(2)}) copy-start(bf16[3072,128]{1,0:T(8,128)(2,1)} %get-tuple-element.26.out_ref) | copy-start | bytes 2359300
  36.1 18.2 %copy-start.1 = (bf16[768,768]{1,0:T(8,128)(2,1)S(1)}, bf16[768,768]{1,0:T(8,128)(2,1)}, u32[]{:S(2)}) copy-start(bf16[768,768]{1,0:T(8,128)(2,1)} %weight_hbm.3) | copy-start | bytes 3538948
  36.1 18.2 %copy-start.3 = (f32[768]{0:T(1024)S(1)}, f32[768]{0:T(1024)}, u32[]{:S(2)}) copy-start(f32[768]{0:T(1024)} %gain_ref.5) | copy-start | bytes 9220
  36.1 9.4 %collective-permute-start.3 = (bf16[384,384]{1,0:T(8,128)(2,1)S(1)}, bf16[384,384]{1,0:T(8,128)(2,1)S(1)}, u32[]{:S(2)}, u32[]{:S(2)}) collective-permute-start(bf16[384,384]{1,0:T(8,128)(2,1)S(1)} %token_finish.2.a_ref), channel_id=1, source_target_pairs={{0,8},{9,1},{18,26},{27,19},{4,20},{13,29},{22,6},{31,15}} | collective-permute-start | bytes 884744 | tf_op jit(solution)/shard_map/ppermute | solution.py:628
  44.1 8.6 %collective-permute-start.5 = (bf16[384,384]{1,0:T(8,128)(2,1)S(1)}, bf16[384,384]{1,0:T(8,128)(2,1)S(1)}, u32[]{:S(2)}, u32[]{:S(2)}) collective-permute-start(bf16[384,384]{1,0:T(8,128)(2,1)S(1)} %token_finish.3.b_ref), channel_id=1, source_target_pairs={{0,8},{9,1},{18,26},{27,19},{4,20},{13,29},{22,6},{31,15}} | collective-permute-start | bytes 884744 | tf_op jit(solution)/shard_map/ppermute | solution.py:628
  45.5 10.0 %collective-permute-start.4 = (bf16[384,384]{1,0:T(8,128)(2,1)S(1)}, bf16[384,384]{1,0:T(8,128)(2,1)S(1)}, u32[]{:S(2)}, u32[]{:S(2)}) collective-permute-start(bf16[384,384]{1,0:T(8,128)(2,1)S(1)} %broadcast_select_fusion.1), channel_id=1, source_target_pairs={{0,16},{8,24},{1,17},{9,25},{18,2},{26,10},{19,3},{27,11},{4,12},{... | collective-permute-start | bytes 884744 | tf_op jit(solution)/shard_map/ppermute | solution.py:628
  52.8 5.5 %collective-permute-start.6 = (bf16[384,384]{1,0:T(8,128)(2,1)S(1)}, bf16[384,384]{1,0:T(8,128)(2,1)S(1)}, u32[]{:S(2)}, u32[]{:S(2)}) collective-permute-start(bf16[384,384]{1,0:T(8,128)(2,1)S(1)} %broadcast_select_fusion), channel_id=1, source_target_pairs={{0,16},{8,24},{1,17},{9,25},{18,2},{26,10},{19,3},{27,11},{4,12},{... | collective-permute-start | bytes 884744 | tf_op jit(solution)/shard_map/ppermute | solution.py:628
  58.3 3.4 %collective-permute-start.8 = (bf16[384,384]{1,0:T(8,128)(2,1)S(1)}, bf16[384,384]{1,0:T(8,128)(2,1)S(1)}, u32[]{:S(2)}, u32[]{:S(2)}) collective-permute-start(bf16[384,384]{1,0:T(8,128)(2,1)S(1)} %broadcast_select_fusion.2.own_b), channel_id=1, source_target_pairs={{0,4},{4,0},{8,12},{12,8},{16,20},{20,16},{24,28},{28,24},{1,5},{5... | collective-permute-start | bytes 884744 | tf_op jit(solution)/shard_map/ppermute | solution.py:674
  58.4 3.3 %collective-permute-start.7 = (bf16[384,384]{1,0:T(8,128)(2,1)S(1)}, bf16[384,384]{1,0:T(8,128)(2,1)S(1)}, u32[]{:S(2)}, u32[]{:S(2)}) collective-permute-start(bf16[384,384]{1,0:T(8,128)(2,1)S(1)} %broadcast_select_fusion.3.own_a), channel_id=1, source_target_pairs={{0,4},{4,0},{8,12},{12,8},{16,20},{20,16},{24,28},{28,24},{1,5},{5... | collective-permute-start | bytes 884744 | tf_op jit(solution)/shard_map/ppermute | solution.py:674
  58.9 3.1 %copy-start.4 = (bf16[768,1536]{1,0:T(8,128)(2,1)S(1)}, bf16[768,1536]{1,0:T(8,128)(2,1)}, u32[]{:S(2)}) copy-start(bf16[768,1536]{1,0:T(8,128)(2,1)} %weight_hbm.5) | copy-start | bytes 7077892
  62.0 11.0 %slice-start = ((s8[9437184]{0:T(1024)(128)(4,1)}), s8[4194304]{0:T(1024)(128)(4,1)S(1)}, s32[]{:S(2)}) async-start(s8[9437184]{0:T(1024)(128)(4,1)} %bitcast.8), calls=%async_computation | async-start | bytes 8388608
  62.0 11.0 %slice-start.1 = ((s8[9437184]{0:T(1024)(128)(4,1)}), s8[4194304]{0:T(1024)(128)(4,1)S(1)}, s32[]{:S(2)}) async-start(s8[9437184]{0:T(1024)(128)(4,1)} %bitcast.8), calls=%async_computation.1 | async-start | bytes 8388608
  66.7 6.3 %slice-start.2 = ((s8[9437184]{0:T(1024)(128)(4,1)}), s8[1048576]{0:T(1024)(128)(4,1)S(1)}, s32[]{:S(2)}) async-start(s8[9437184]{0:T(1024)(128)(4,1)} %bitcast.8), calls=%async_computation.2 | async-start | bytes 2097152
  70.9 7.0 %collective-permute-start.11 = (bf16[208,384]{1,0:T(8,128)(2,1)S(1)}, bf16[208,384]{1,0:T(8,128)(2,1)S(1)}, u32[]{:S(2)}, u32[]{:S(2)}) collective-permute-start(bf16[208,384]{1,0:T(8,128)(2,1)S(1)} %get-tuple-element.50), channel_id=1, source_target_pairs={{0,1},{1,0},{2,3},{3,2},{4,5},{5,4},{6,7},{7,6},{8,9},{9,8},{10,11... | collective-permute-start | bytes 479240 | tf_op jit(solution)/shard_map/ppermute | solution.py:696
  72.3 13.3 %collective-permute-start.9 = (bf16[208,384]{1,0:T(8,128)(2,1)S(1)}, bf16[208,384]{1,0:T(8,128)(2,1)S(1)}, u32[]{:S(2)}, u32[]{:S(2)}) collective-permute-start(bf16[208,384]{1,0:T(8,128)(2,1)S(1)} %get-tuple-element.41), channel_id=1, source_target_pairs={{0,1},{1,0},{2,3},{3,2},{4,5},{5,4},{6,7},{7,6},{8,9},{9,8},{10,11... | collective-permute-start | bytes 479240 | tf_op jit(solution)/shard_map/ppermute | solution.py:687
  80.4 8.9 %collective-permute-start.12 = (bf16[208,384]{1,0:T(8,128)(2,1)S(1)}, bf16[208,384]{1,0:T(8,128)(2,1)S(1)}, u32[]{:S(2)}, u32[]{:S(2)}) collective-permute-start(bf16[208,384]{1,0:T(8,128)(2,1)S(1)} %get-tuple-element.53), channel_id=1, source_target_pairs={{0,3},{1,2},{2,1},{3,0},{4,7},{5,6},{6,5},{7,4},{8,11},{9,10},{10,... | collective-permute-start | bytes 479240 | tf_op jit(solution)/shard_map/ppermute | solution.py:681
  85.5 16.9 %copy-start = (bf16[768,768]{1,0:T(8,128)(2,1)S(1)}, bf16[768,768]{1,0:T(8,128)(2,1)}, u32[]{:S(2)}) copy-start(bf16[768,768]{1,0:T(8,128)(2,1)} %weight_ref.9) | copy-start | bytes 3538948
  88.0 8.1 %collective-permute-start.10 = (bf16[208,384]{1,0:T(8,128)(2,1)S(1)}, bf16[208,384]{1,0:T(8,128)(2,1)S(1)}, u32[]{:S(2)}, u32[]{:S(2)}) collective-permute-start(bf16[208,384]{1,0:T(8,128)(2,1)S(1)} %get-tuple-element.46), channel_id=1, source_target_pairs={{0,3},{1,2},{2,1},{3,0},{4,7},{5,6},{6,5},{7,4},{8,11},{9,10},{10,... | collective-permute-start | bytes 479240 | tf_op jit(solution)/shard_map/ppermute | solution.py:681
  89.7 10.2 %collective-permute-start.14 = (bf16[192,384]{1,0:T(8,128)(2,1)S(1)}, bf16[192,384]{1,0:T(8,128)(2,1)S(1)}, u32[]{:S(2)}, u32[]{:S(2)}) collective-permute-start(bf16[192,384]{1,0:T(8,128)(2,1)S(1)} %settle.3.own_b), channel_id=1, source_target_pairs={{0,1},{1,0},{2,3},{3,2},{4,5},{5,4},{6,7},{7,6},{8,9},{9,8},{10,11... | collective-permute-start | bytes 442376 | tf_op jit(solution)/shard_map/ppermute | solution.py:712
  96.6 5.8 %collective-permute-start.13 = (bf16[192,384]{1,0:T(8,128)(2,1)S(1)}, bf16[192,384]{1,0:T(8,128)(2,1)S(1)}, u32[]{:S(2)}, u32[]{:S(2)}) collective-permute-start(bf16[192,384]{1,0:T(8,128)(2,1)S(1)} %settle.2.own_a), channel_id=1, source_target_pairs={{0,1},{1,0},{2,3},{3,2},{4,5},{5,4},{6,7},{7,6},{8,9},{9,8},{10,11... | collective-permute-start | bytes 442376 | tf_op jit(solution)/shard_map/ppermute | solution.py:712

commit v5 on v4

--- a/solution.py
+++ b/solution.py
@@ -700,6 +700,7 @@
             functools.partial(keep_kernel, g), g, keep, (), queries, (*held[g], near[g]), None,
             keep_bias, ("o", "lse", "msg"), "attend_keep",
         )
+        queries, msg = lax.optimization_barrier((queries, msg))
         sums.append((o, lse))
         gone.append(far(msg, bits[0]))
     own_mix, other_mix = [], []

time: 105 us -> 111 us (1.057)
  waiting for transfers between devices: 21.9 us -> 27.8 us
    ppermute x1, waiting for transfers between devices: 0.01 us -> 7.14 us  [body(): held, near = ([(k, v)], [lax.ppermute(msg, 'ka', swap)])]
    ppermute x1, waiting for transfers between devices: 4.59 us -> 0.01 us  [body(): near.append(lax.ppermute(msg, 'ka', swap))]
    ppermute x2, waiting for transfers between devices: 1.18 us -> 4.48 us  [far(): return lax.ppermute(msg, 'ka', [(i, i ^ 2 * bit - 1) for i in range(n_ka)])]
  transfers between devices with their start and end apart: 15 -> 15, of which waited for: 7 -> 7; matrix products, arithmetic and copies ran while one was open for 3% -> 3% of each run, Pallas kernels for 13% -> 10%
where the time goes in v5:
time: 111 us; the launch traced here: 110 us
  Pallas kernels  42.2 us (38%)
  starting transfers between devices  33 us (30%)
  waiting for transfers between devices  27.8 us (25%)
  local copies, waits for them, and re-layouts  5.89 us (5%)
    pallas_call x1, Pallas kernels, atom_attention(): pl.pallas_call(functools.partial(atom_kernel, chunks, atom_total, tok_row...  17.4 us
    pallas_call x4, Pallas kernels, group_call(): pl.pallas_call(functools.partial(kernel, heads, feats // heads), grid_spe...  13.8 us
    ppermute x4, starting transfers between devices, key_parts(): lax.ppermute(part, ('pb', 'ka'), pairs)  8.55 us
    ppermute x2, starting transfers between devices, body(): other_mix.append(lax.ppermute(own_mix[g], 'ka', swap))  8.54 us
    ppermute x4, waiting for transfers between devices, key_parts(): lax.ppermute(part, ('pb', 'ka'), pairs)  8.52 us
    ppermute x1, waiting for transfers between devices, body(): held, near = ([(k, v)], [lax.ppermute(msg, 'ka', swap)])  7.14 us
    pallas_call x2, Pallas kernels, pool(): pl.pallas_call(functools.partial(pool_kernel, tok_rows), grid_spec=pltpu....  6 us
    ppermute x2, starting transfers between devices, far(): return lax.ppermute(msg, 'ka', [(i, i ^ 2 * bit - 1) for i in range(n_ka)])  5.22 us
  transfers between devices with their start and end apart: 15, of which 7 were waited for; matrix products, arithmetic and copies ran while one was open for 3% of the time, Pallas kernels for 10%

profile of v5, /device:TPU:0, one launch (start us, length us, event | category | flops | bytes accessed | tf_op | source)
XLA Modules:
  0.0 110.1 jit_solution(7376665771341750725)
XLA Ops:
  0.6 0.7 fusion
  1.4 2.3 %collective-permute-start = (bf16[64,128]{1,0:T(8,128)(2,1)S(1)}, bf16[64,128]{1,0:T(8,128)(2,1)S(1)}, u32[]{:S(2)}, u32[]{:S(2)}) collective-permute-start(bf16[64,128]{1,0:T(8,128)(2,1)S(1)} %get-tuple-element.61), channel_id=1, source_target_pairs={{0,4},{4,8},{8,12},{12,16},{16,20},{20,24},{24,28},{1,5},{5,9},{9,... | collective-permute-start | bytes 49160 | tf_op jit(solution)/shard_map/ppermute | solution.py:656
  3.7 1.3 %collective-permute-start.1 = (bf16[64,128]{1,0:T(8,128)(2,1)S(1)}, bf16[64,128]{1,0:T(8,128)(2,1)S(1)}, u32[]{:S(2)}, u32[]{:S(2)}) collective-permute-start(bf16[64,128]{1,0:T(8,128)(2,1)S(1)} %get-tuple-element.60), channel_id=1, source_target_pairs={{4,0},{8,4},{12,8},{16,12},{20,16},{24,20},{28,24},{5,1},{9,5},{13... | collective-permute-start | bytes 49160 | tf_op jit(solution)/shard_map/ppermute | solution.py:657
  5.0 3.9 %collective-permute-done.1.right_ref = bf16[64,128]{1,0:T(8,128)(2,1)S(1)} collective-permute-done((bf16[64,128]{1,0:T(8,128)(2,1)S(1)}, bf16[64,128]{1,0:T(8,128)(2,1)S(1)}, u32[]{:S(2)}, u32[]{:S(2)}) %collective-permute-start.1) | collective-permute-done | bytes 16416 | tf_op jit(solution)/shard_map/ppermute | solution.py:657
  8.9 0.6 copy-done.8
  9.5 17.4 %atom_attention.1 = (bf16[3072,128]{1,0:T(8,128)(2,1)}, bf16[400,128]{1,0:T(8,128)(2,1)}) custom-call(s32[96]{0:T(128)} %shift_ref.1, s32[1]{0:T(128)} %bitcast.pos_ref, bf16[3072,128]{1,0:T(8,128)(2,1)} %atoms_ref.1, bf16[64,128]{1,0:T(8,128)(2,1)} %copy-done.7, bf16[64,128]{1,0:T(8,128)(2,1)} %copy-done.8, f32[128]{0:T(128)} %gain_ref.3, ...), custom_call_target="tpu_custom_call" | custom-call | flops 8000000000 | bytes 6000000 | tf_op jit(solution)/shard_map/atom_attention/pallas_call | solution.py:169
  26.9 4.4 %collective-permute-start.2 = (bf16[400,128]{1,0:T(8,128)(2,1)}, bf16[400,128]{1,0:T(8,128)(2,1)S(1)}, u32[]{:S(2)}, u32[]{:S(2)}) collective-permute-start(bf16[400,128]{1,0:T(8,128)(2,1)} %get-tuple-element.32), channel_id=1, source_target_pairs={{0,4},{4,8},{8,12},{12,16},{16,20},{20,24},{24,28},{1,5},{5,9},{9,... | collective-permute-start | bytes 307208 | tf_op jit(solution)/shard_map/ppermute | solution.py:662
  31.4 1.1 %copy-done.6 = bf16[3072,128]{1,0:T(8,128)(2,1)S(1)} copy-done((bf16[3072,128]{1,0:T(8,128)(2,1)S(1)}, bf16[3072,128]{1,0:T(8,128)(2,1)}, u32[]{:S(2)}) %copy-start.6) | copy-done | bytes 786456
  32.5 3.0 %pool.2 = (f32[384,384]{1,0:T(8,128)S(1)}, f32[384,128]{1,0:T(8,128)S(1)}) custom-call(s32[1]{0:T(128)} %bitcast.pos_ref, bf16[3072,128]{1,0:T(8,128)(2,1)S(1)} %copy-done.6, bf16[128,768]{1,0:T(8,128)(2,1)S(1)} %copy-done.2, s32[24,128]{1,0:T(8,128)S(1)} %bitcast.6), custom_call_target="tpu_custom_call" | custom-call | flops 2000000000 | bytes 2000000 | tf_op jit(solution)/shard_map/pool/pallas_call | solution.py:241
  36.1 4.4 %collective-permute-start.3 = (bf16[384,384]{1,0:T(8,128)(2,1)S(1)}, bf16[384,384]{1,0:T(8,128)(2,1)S(1)}, u32[]{:S(2)}, u32[]{:S(2)}) collective-permute-start(bf16[384,384]{1,0:T(8,128)(2,1)S(1)} %token_finish.2.a_ref), channel_id=1, source_target_pairs={{0,8},{9,1},{18,26},{27,19},{4,20},{13,29},{22,6},{31,15}} | collective-permute-start | bytes 884744 | tf_op jit(solution)/shard_map/ppermute | solution.py:628
  40.5 3.0 %pool.3 = (f32[384,384]{1,0:T(8,128)S(1)}, f32[384,128]{1,0:T(8,128)S(1)}) custom-call(s32[1]{0:T(128)} %bitcast.pos_ref, bf16[3072,128]{1,0:T(8,128)(2,1)S(1)} %copy-done.6, bf16[128,768]{1,0:T(8,128)(2,1)S(1)} %copy-done.2, s32[24,128]{1,0:T(8,128)S(1)} %bitcast.7), custom_call_target="tpu_custom_call" | custom-call | flops 2000000000 | bytes 2000000 | tf_op jit(solution)/shard_map/pool/pallas_call | solution.py:241
  44.1 1.3 %collective-permute-start.5 = (bf16[384,384]{1,0:T(8,128)(2,1)S(1)}, bf16[384,384]{1,0:T(8,128)(2,1)S(1)}, u32[]{:S(2)}, u32[]{:S(2)}) collective-permute-start(bf16[384,384]{1,0:T(8,128)(2,1)S(1)} %token_finish.3.b_ref), channel_id=1, source_target_pairs={{0,8},{9,1},{18,26},{27,19},{4,20},{13,29},{22,6},{31,15}} | collective-permute-start | bytes 884744 | tf_op jit(solution)/shard_map/ppermute | solution.py:628
  45.5 1.3 %collective-permute-start.4 = (bf16[384,384]{1,0:T(8,128)(2,1)S(1)}, bf16[384,384]{1,0:T(8,128)(2,1)S(1)}, u32[]{:S(2)}, u32[]{:S(2)}) collective-permute-start(bf16[384,384]{1,0:T(8,128)(2,1)S(1)} %broadcast_select_fusion.1), channel_id=1, source_target_pairs={{0,16},{8,24},{1,17},{9,25},{18,2},{26,10},{19,3},{27,11},{4,12},{... | collective-permute-start | bytes 884744 | tf_op jit(solution)/shard_map/ppermute | solution.py:628
  46.9 5.9 %collective-permute-done.5 = bf16[384,384]{1,0:T(8,128)(2,1)S(1)} collective-permute-done((bf16[384,384]{1,0:T(8,128)(2,1)S(1)}, bf16[384,384]{1,0:T(8,128)(2,1)S(1)}, u32[]{:S(2)}, u32[]{:S(2)}) %collective-permute-start.5) | collective-permute-done | bytes 294944 | tf_op jit(solution)/shard_map/ppermute | solution.py:628
  52.8 1.5 %collective-permute-start.6 = (bf16[384,384]{1,0:T(8,128)(2,1)S(1)}, bf16[384,384]{1,0:T(8,128)(2,1)S(1)}, u32[]{:S(2)}, u32[]{:S(2)}) collective-permute-start(bf16[384,384]{1,0:T(8,128)(2,1)S(1)} %broadcast_select_fusion), channel_id=1, source_target_pairs={{0,16},{8,24},{1,17},{9,25},{18,2},{26,10},{19,3},{27,11},{4,12},{... | collective-permute-start | bytes 884744 | tf_op jit(solution)/shard_map/ppermute | solution.py:628
  54.3 1.3 %queries.1.q_ref = bf16[384,768]{1,0:T(8,128)(2,1)S(1)} custom-call(bf16[384,384]{1,0:T(8,128)(2,1)S(1)} %token_finish.2.a_ref, bf16[384,384]{1,0:T(8,128)(2,1)S(1)} %token_finish.3.b_ref, f32[768]{0:T(1024)S(1)} %copy-done.3, bf16[768,768]{1,0:T(8,128)(2,1)S(1)} %copy-done.1), custom_call_target="tpu_custom_call" | custom-call | flops 500000000 | bytes 3000000 | tf_op jit(solution)/shard_map/queries/pallas_call | solution.py:309
  55.6 2.6 %collective-permute-done.6 = bf16[384,384]{1,0:T(8,128)(2,1)S(1)} collective-permute-done((bf16[384,384]{1,0:T(8,128)(2,1)S(1)}, bf16[384,384]{1,0:T(8,128)(2,1)S(1)}, u32[]{:S(2)}, u32[]{:S(2)}) %collective-permute-start.6) | collective-permute-done | bytes 294944 | tf_op jit(solution)/shard_map/ppermute | solution.py:628
  58.9 2.9 %constant_dynamic-slice_fusion.1.bias_ref = bf16[16,192,768]{2,1,0:T(8,128)(2,1)S(1)} fusion(bf16[16,384,768]{2,1,0:T(8,128)(2,1)} %param.25, s32[]{:T(128)S(6)} %select_n.40), kind=kLoop, calls=%fused_computation.5 | loop fusion | bytes 9437188 | tf_op jit(solution)/shard_map/dynamic_slice | solution.py:676
  62.0 4.7 %attend_first.1 = (bf16[768,768]{1,0:T(8,128)(2,1)S(1)}, bf16[384,768]{1,0:T(8,128)(2,1)S(1)}, bf16[768,384]{1,0:T(8,128)(2,1)S(1)}, bf16[208,384]{1,0:T(8,128)(2,1)S(1)}) custom-call(s32[1]{0:T(128)} %bitcast.3.half_ref, s32[1]{0:T(128)} %bitcast.4.core_ref, bf16[384,768]{1,0:T(8,128)(2,1)S(1)} %queries.1.q_ref, ...), custom_call_target="tpu_custom_call" | custom-call | flops 4000000000 | bytes 4000000 | tf_op jit(solution)/shard_map/attend_first/pallas_call | solution.py:532
  66.7 4.2 %attend_next.1 = (bf16[384,768]{1,0:T(8,128)(2,1)S(1)}, bf16[768,384]{1,0:T(8,128)(2,1)S(1)}, bf16[208,384]{1,0:T(8,128)(2,1)S(1)}) custom-call(s32[1]{0:T(128)} %bitcast.3.half_ref, bf16[384,768]{1,0:T(8,128)(2,1)S(1)} %queries.1.q_ref, bf16[768,768]{1,0:T(8,128)(2,1)S(1)} %get-tuple-element.52.x_ref, bf16[768,1536]{1,0:T(8,128)(2,1)S(1)} %copy-done.4, ...), custom_call_target="tpu_custom_call" | custom-call | flops 4000000000 | bytes 4000000 | tf_op jit(solution)/shard_map/attend_next/pallas_call | solution.py:532
  71.0 1.4 %collective-permute-start.11 = (bf16[208,384]{1,0:T(8,128)(2,1)S(1)}, bf16[208,384]{1,0:T(8,128)(2,1)S(1)}, u32[]{:S(2)}, u32[]{:S(2)}) collective-permute-start(bf16[208,384]{1,0:T(8,128)(2,1)S(1)} %get-tuple-element.55), channel_id=1, source_target_pairs={{0,1},{1,0},{2,3},{3,2},{4,5},{5,4},{6,7},{7,6},{8,9},{9,8},{10,11... | collective-permute-start | bytes 479240 | tf_op jit(solution)/shard_map/ppermute | solution.py:696
  72.4 0.7 collective-permute-start.9
  73.4 7.1 %collective-permute-done.9.near_ref = bf16[208,384]{1,0:T(8,128)(2,1)S(1)} collective-permute-done((bf16[208,384]{1,0:T(8,128)(2,1)S(1)}, bf16[208,384]{1,0:T(8,128)(2,1)S(1)}, u32[]{:S(2)}, u32[]{:S(2)}) %collective-permute-start.9) | collective-permute-done | bytes 159776 | tf_op jit(solution)/shard_map/ppermute | solution.py:687
  80.6 2.4 %attend_keep.2 = (f32[192,384]{1,0:T(8,128)S(1)}, f32[192,128]{1,0:T(8,128)S(1)}, bf16[208,384]{1,0:T(8,128)(2,1)S(1)}) custom-call(s32[1]{0:T(128)} %bitcast.2.half_ref, bf16[384,768]{1,0:T(8,128)(2,1)S(1)} %queries.1.q_ref, bf16[384,768]{1,0:T(8,128)(2,1)S(1)} %get-tuple-element.42.k_ref, bf16[768,384]{1,0:T(8,128)(2,1)S(1)} %get-tuple-element.43.v_ref, ...), custom_call_target="tpu_custom_call" | custom-call | flops 4000000000 | bytes 4000000 | tf_op jit(solution)/shard_map/attend_keep/pallas_call | solution.py:532
  83.0 2.5 %attend_keep.3 = (f32[192,384]{1,0:T(8,128)S(1)}, f32[192,128]{1,0:T(8,128)S(1)}, bf16[208,384]{1,0:T(8,128)(2,1)S(1)}) custom-call(s32[1]{0:T(128)} %bitcast.2.half_ref, bf16[384,768]{1,0:T(8,128)(2,1)S(1)} %queries.1.q_ref, bf16[384,768]{1,0:T(8,128)(2,1)S(1)} %get-tuple-element.53.k_ref, bf16[768,384]{1,0:T(8,128)(2,1)S(1)} %get-tuple-element.54.v_ref, ...), custom_call_target="tpu_custom_call" | custom-call | flops 4000000000 | bytes 4000000 | tf_op jit(solution)/shard_map/attend_keep/pallas_call | solution.py:532
  85.5 5.1 %collective-permute-start.12 = (bf16[208,384]{1,0:T(8,128)(2,1)S(1)}, bf16[208,384]{1,0:T(8,128)(2,1)S(1)}, u32[]{:S(2)}, u32[]{:S(2)}) collective-permute-start(bf16[208,384]{1,0:T(8,128)(2,1)S(1)} %get-tuple-element.59), channel_id=1, source_target_pairs={{0,3},{1,2},{2,1},{3,0},{4,7},{5,6},{6,5},{7,4},{8,11},{9,10},{10,... | collective-permute-start | bytes 479240 | tf_op jit(solution)/shard_map/ppermute | solution.py:681
  90.7 4.5 %collective-permute-done.12.msg_ref = bf16[208,384]{1,0:T(8,128)(2,1)S(1)} collective-permute-done((bf16[208,384]{1,0:T(8,128)(2,1)S(1)}, bf16[208,384]{1,0:T(8,128)(2,1)S(1)}, u32[]{:S(2)}, u32[]{:S(2)}) %collective-permute-start.12) | collective-permute-done | bytes 159776 | tf_op jit(solution)/shard_map/ppermute | solution.py:681
  95.6 6.5 %collective-permute-start.14 = (bf16[192,384]{1,0:T(8,128)(2,1)S(1)}, bf16[192,384]{1,0:T(8,128)(2,1)S(1)}, u32[]{:S(2)}, u32[]{:S(2)}) collective-permute-start(bf16[192,384]{1,0:T(8,128)(2,1)S(1)} %settle.3.own_b), channel_id=1, source_target_pairs={{0,1},{1,0},{2,3},{3,2},{4,5},{5,4},{6,7},{7,6},{8,9},{9,8},{10,11... | collective-permute-start | bytes 442376 | tf_op jit(solution)/shard_map/ppermute | solution.py:713
  102.6 2.0 %collective-permute-start.13 = (bf16[192,384]{1,0:T(8,128)(2,1)S(1)}, bf16[192,384]{1,0:T(8,128)(2,1)S(1)}, u32[]{:S(2)}, u32[]{:S(2)}) collective-permute-start(bf16[192,384]{1,0:T(8,128)(2,1)S(1)} %settle.2.own_a), channel_id=1, source_target_pairs={{0,1},{1,0},{2,3},{3,2},{4,5},{5,4},{6,7},{7,6},{8,9},{9,8},{10,11... | collective-permute-start | bytes 442376 | tf_op jit(solution)/shard_map/ppermute | solution.py:713
  104.6 1.4 %collective-permute-done.14.other_b = bf16[192,384]{1,0:T(8,128)(2,1)S(1)} collective-permute-done((bf16[192,384]{1,0:T(8,128)(2,1)S(1)}, bf16[192,384]{1,0:T(8,128)(2,1)S(1)}, u32[]{:S(2)}, u32[]{:S(2)}) %collective-permute-start.14) | collective-permute-done | bytes 147488 | tf_op jit(solution)/shard_map/ppermute | solution.py:713
  106.0 2.5 %collective-permute-done.13.other_a = bf16[192,384]{1,0:T(8,128)(2,1)S(1)} collective-permute-done((bf16[192,384]{1,0:T(8,128)(2,1)S(1)}, bf16[192,384]{1,0:T(8,128)(2,1)S(1)}, u32[]{:S(2)}, u32[]{:S(2)}) %collective-permute-start.13) | collective-permute-done | bytes 147488 | tf_op jit(solution)/shard_map/ppermute | solution.py:713
  108.5 1.6 %output_rows.1 = bf16[384,768]{1,0:T(8,128)(2,1)} custom-call(s32[1]{0:T(128)} %bitcast.2.half_ref, bf16[192,384]{1,0:T(8,128)(2,1)S(1)} %settle.2.own_a, bf16[192,384]{1,0:T(8,128)(2,1)S(1)} %settle.3.own_b, bf16[192,384]{1,0:T(8,128)(2,1)S(1)} %collective-permute-done.13.other_a, bf16[192,384]{1,0:T(8,128)(2,1)S(1)} %collective-permute-done.14.other_b, ...), custom_call_target="tpu_custom_call" | custom-call | tf_op jit(solution)/shard_map/output_rows/pallas_call | solution.py:594
  (43 shorter events, 3.4 us)
Async XLA Ops:
  1.4 3.7 %collective-permute-start = (bf16[64,128]{1,0:T(8,128)(2,1)S(1)}, bf16[64,128]{1,0:T(8,128)(2,1)S(1)}, u32[]{:S(2)}, u32[]{:S(2)}) collective-permute-start(bf16[64,128]{1,0:T(8,128)(2,1)S(1)} %get-tuple-element.61), channel_id=1, source_target_pairs={{0,4},{4,8},{8,12},{12,16},{16,20},{20,24},{24,28},{1,5},{5,9},{9,... | collective-permute-start | bytes 49160 | tf_op jit(solution)/shard_map/ppermute | solution.py:656
  3.7 5.2 %collective-permute-start.1 = (bf16[64,128]{1,0:T(8,128)(2,1)S(1)}, bf16[64,128]{1,0:T(8,128)(2,1)S(1)}, u32[]{:S(2)}, u32[]{:S(2)}) collective-permute-start(bf16[64,128]{1,0:T(8,128)(2,1)S(1)} %get-tuple-element.60), channel_id=1, source_target_pairs={{4,0},{8,4},{12,8},{16,12},{20,16},{24,20},{28,24},{5,1},{9,5},{13... | collective-permute-start | bytes 49160 | tf_op jit(solution)/shard_map/ppermute | solution.py:657
  5.0 3.9 %copy-start.7 = (bf16[64,128]{1,0:T(8,128)(2,1)}, bf16[64,128]{1,0:T(8,128)(2,1)S(1)}, u32[]{:S(2)}) copy-start(bf16[64,128]{1,0:T(8,128)(2,1)S(1)} %collective-permute-done.left_ref) | copy-start | bytes 49156
  8.9 0.6 copy-start.8
  9.5 21.8 %copy-start.2 = (bf16[128,768]{1,0:T(8,128)(2,1)S(1)}, bf16[128,768]{1,0:T(8,128)(2,1)}, u32[]{:S(2)}) copy-start(bf16[128,768]{1,0:T(8,128)(2,1)} %weight_ref.8) | copy-start | bytes 589828
  9.5 21.8 %copy-start.5 = (s32[3072]{0:T(1024)S(1)}, s32[3072]{0:T(1024)}, u32[]{:S(2)}) copy-start(s32[3072]{0:T(1024)} %param.19) | copy-start | bytes 36868
  26.9 8.5 %collective-permute-start.2 = (bf16[400,128]{1,0:T(8,128)(2,1)}, bf16[400,128]{1,0:T(8,128)(2,1)S(1)}, u32[]{:S(2)}, u32[]{:S(2)}) collective-permute-start(bf16[400,128]{1,0:T(8,128)(2,1)} %get-tuple-element.32), channel_id=1, source_target_pairs={{0,4},{4,8},{8,12},{12,16},{16,20},{20,24},{24,28},{1,5},{5,9},{9,... | collective-permute-start | bytes 307208 | tf_op jit(solution)/shard_map/ppermute | solution.py:662
  31.3 1.1 %copy-start.6 = (bf16[3072,128]{1,0:T(8,128)(2,1)S(1)}, bf16[3072,128]{1,0:T(8,128)(2,1)}, u32[]{:S(2)}) copy-start(bf16[3072,128]{1,0:T(8,128)(2,1)} %get-tuple-element.29.out_ref) | copy-start | bytes 2359300
  36.1 18.2 %copy-start.1 = (bf16[768,768]{1,0:T(8,128)(2,1)S(1)}, bf16[768,768]{1,0:T(8,128)(2,1)}, u32[]{:S(2)}) copy-start(bf16[768,768]{1,0:T(8,128)(2,1)} %weight_hbm.3) | copy-start | bytes 3538948
  36.1 18.2 %copy-start.3 = (f32[768]{0:T(1024)S(1)}, f32[768]{0:T(1024)}, u32[]{:S(2)}) copy-start(f32[768]{0:T(1024)} %gain_ref.5) | copy-start | bytes 9220
  36.1 9.4 %collective-permute-start.3 = (bf16[384,384]{1,0:T(8,128)(2,1)S(1)}, bf16[384,384]{1,0:T(8,128)(2,1)S(1)}, u32[]{:S(2)}, u32[]{:S(2)}) collective-permute-start(bf16[384,384]{1,0:T(8,128)(2,1)S(1)} %token_finish.2.a_ref), channel_id=1, source_target_pairs={{0,8},{9,1},{18,26},{27,19},{4,20},{13,29},{22,6},{31,15}} | collective-permute-start | bytes 884744 | tf_op jit(solution)/shard_map/ppermute | solution.py:628
  44.1 8.6 %collective-permute-start.5 = (bf16[384,384]{1,0:T(8,128)(2,1)S(1)}, bf16[384,384]{1,0:T(8,128)(2,1)S(1)}, u32[]{:S(2)}, u32[]{:S(2)}) collective-permute-start(bf16[384,384]{1,0:T(8,128)(2,1)S(1)} %token_finish.3.b_ref), channel_id=1, source_target_pairs={{0,8},{9,1},{18,26},{27,19},{4,20},{13,29},{22,6},{31,15}} | collective-permute-start | bytes 884744 | tf_op jit(solution)/shard_map/ppermute | solution.py:628
  45.5 10.0 %collective-permute-start.4 = (bf16[384,384]{1,0:T(8,128)(2,1)S(1)}, bf16[384,384]{1,0:T(8,128)(2,1)S(1)}, u32[]{:S(2)}, u32[]{:S(2)}) collective-permute-start(bf16[384,384]{1,0:T(8,128)(2,1)S(1)} %broadcast_select_fusion.1), channel_id=1, source_target_pairs={{0,16},{8,24},{1,17},{9,25},{18,2},{26,10},{19,3},{27,11},{4,12},{... | collective-permute-start | bytes 884744 | tf_op jit(solution)/shard_map/ppermute | solution.py:628
  52.8 5.5 %collective-permute-start.6 = (bf16[384,384]{1,0:T(8,128)(2,1)S(1)}, bf16[384,384]{1,0:T(8,128)(2,1)S(1)}, u32[]{:S(2)}, u32[]{:S(2)}) collective-permute-start(bf16[384,384]{1,0:T(8,128)(2,1)S(1)} %broadcast_select_fusion), channel_id=1, source_target_pairs={{0,16},{8,24},{1,17},{9,25},{18,2},{26,10},{19,3},{27,11},{4,12},{... | collective-permute-start | bytes 884744 | tf_op jit(solution)/shard_map/ppermute | solution.py:628
  58.3 3.5 %collective-permute-start.8 = (bf16[384,384]{1,0:T(8,128)(2,1)S(1)}, bf16[384,384]{1,0:T(8,128)(2,1)S(1)}, u32[]{:S(2)}, u32[]{:S(2)}) collective-permute-start(bf16[384,384]{1,0:T(8,128)(2,1)S(1)} %broadcast_select_fusion.2.own_b), channel_id=1, source_target_pairs={{0,4},{4,0},{8,12},{12,8},{16,20},{20,16},{24,28},{28,24},{1,5},{5... | collective-permute-start | bytes 884744 | tf_op jit(solution)/shard_map/ppermute | solution.py:674
  58.4 3.4 %collective-permute-start.7 = (bf16[384,384]{1,0:T(8,128)(2,1)S(1)}, bf16[384,384]{1,0:T(8,128)(2,1)S(1)}, u32[]{:S(2)}, u32[]{:S(2)}) collective-permute-start(bf16[384,384]{1,0:T(8,128)(2,1)S(1)} %broadcast_select_fusion.3.own_a), channel_id=1, source_target_pairs={{0,4},{4,0},{8,12},{12,8},{16,20},{20,16},{24,28},{28,24},{1,5},{5... | collective-permute-start | bytes 884744 | tf_op jit(solution)/shard_map/ppermute | solution.py:674
  58.9 3.1 %copy-start.4 = (bf16[768,1536]{1,0:T(8,128)(2,1)S(1)}, bf16[768,1536]{1,0:T(8,128)(2,1)}, u32[]{:S(2)}) copy-start(bf16[768,1536]{1,0:T(8,128)(2,1)} %weight_hbm.5) | copy-start | bytes 7077892
  62.0 11.1 %slice-start = ((s8[9437184]{0:T(1024)(128)(4,1)}), s8[4194304]{0:T(1024)(128)(4,1)S(1)}, s32[]{:S(2)}) async-start(s8[9437184]{0:T(1024)(128)(4,1)} %bitcast.8), calls=%async_computation | async-start | bytes 8388608
  62.0 11.1 %slice-start.1 = ((s8[9437184]{0:T(1024)(128)(4,1)}), s8[4194304]{0:T(1024)(128)(4,1)S(1)}, s32[]{:S(2)}) async-start(s8[9437184]{0:T(1024)(128)(4,1)} %bitcast.8), calls=%async_computation.1 | async-start | bytes 8388608
  66.7 6.4 %slice-start.2 = ((s8[9437184]{0:T(1024)(128)(4,1)}), s8[1048576]{0:T(1024)(128)(4,1)S(1)}, s32[]{:S(2)}) async-start(s8[9437184]{0:T(1024)(128)(4,1)} %bitcast.8), calls=%async_computation.2 | async-start | bytes 2097152
  71.0 12.0 %collective-permute-start.11 = (bf16[208,384]{1,0:T(8,128)(2,1)S(1)}, bf16[208,384]{1,0:T(8,128)(2,1)S(1)}, u32[]{:S(2)}, u32[]{:S(2)}) collective-permute-start(bf16[208,384]{1,0:T(8,128)(2,1)S(1)} %get-tuple-element.55), channel_id=1, source_target_pairs={{0,1},{1,0},{2,3},{3,2},{4,5},{5,4},{6,7},{7,6},{8,9},{9,8},{10,11... | collective-permute-start | bytes 479240 | tf_op jit(solution)/shard_map/ppermute | solution.py:696
  72.4 8.2 %collective-permute-start.9 = (bf16[208,384]{1,0:T(8,128)(2,1)S(1)}, bf16[208,384]{1,0:T(8,128)(2,1)S(1)}, u32[]{:S(2)}, u32[]{:S(2)}) collective-permute-start(bf16[208,384]{1,0:T(8,128)(2,1)S(1)} %get-tuple-element.44), channel_id=1, source_target_pairs={{0,1},{1,0},{2,3},{3,2},{4,5},{5,4},{6,7},{7,6},{8,9},{9,8},{10,11... | collective-permute-start | bytes 479240 | tf_op jit(solution)/shard_map/ppermute | solution.py:687
  83.0 25.5 %copy-start = (bf16[768,768]{1,0:T(8,128)(2,1)S(1)}, bf16[768,768]{1,0:T(8,128)(2,1)}, u32[]{:S(2)}) copy-start(bf16[768,768]{1,0:T(8,128)(2,1)} %weight_ref.9) | copy-start | bytes 3538948
  85.5 9.7 %collective-permute-start.12 = (bf16[208,384]{1,0:T(8,128)(2,1)S(1)}, bf16[208,384]{1,0:T(8,128)(2,1)S(1)}, u32[]{:S(2)}, u32[]{:S(2)}) collective-permute-start(bf16[208,384]{1,0:T(8,128)(2,1)S(1)} %get-tuple-element.59), channel_id=1, source_target_pairs={{0,3},{1,2},{2,1},{3,0},{4,7},{5,6},{6,5},{7,4},{8,11},{9,10},{10,... | collective-permute-start | bytes 479240 | tf_op jit(solution)/shard_map/ppermute | solution.py:681
  90.6 11.6 %collective-permute-start.10 = (bf16[208,384]{1,0:T(8,128)(2,1)S(1)}, bf16[208,384]{1,0:T(8,128)(2,1)S(1)}, u32[]{:S(2)}, u32[]{:S(2)}) collective-permute-start(bf16[208,384]{1,0:T(8,128)(2,1)S(1)} %get-tuple-element.50), channel_id=1, source_target_pairs={{0,3},{1,2},{2,1},{3,0},{4,7},{5,6},{6,5},{7,4},{8,11},{9,10},{10,... | collective-permute-start | bytes 479240 | tf_op jit(solution)/shard_map/ppermute | solution.py:681
  95.6 10.4 %collective-permute-start.14 = (bf16[192,384]{1,0:T(8,128)(2,1)S(1)}, bf16[192,384]{1,0:T(8,128)(2,1)S(1)}, u32[]{:S(2)}, u32[]{:S(2)}) collective-permute-start(bf16[192,384]{1,0:T(8,128)(2,1)S(1)} %settle.3.own_b), channel_id=1, source_target_pairs={{0,1},{1,0},{2,3},{3,2},{4,5},{5,4},{6,7},{7,6},{8,9},{9,8},{10,11... | collective-permute-start | bytes 442376 | tf_op jit(solution)/shard_map/ppermute | solution.py:713
  102.6 5.8 %collective-permute-start.13 = (bf16[192,384]{1,0:T(8,128)(2,1)S(1)}, bf16[192,384]{1,0:T(8,128)(2,1)S(1)}, u32[]{:S(2)}, u32[]{:S(2)}) collective-permute-start(bf16[192,384]{1,0:T(8,128)(2,1)S(1)} %settle.2.own_a), channel_id=1, source_target_pairs={{0,1},{1,0},{2,3},{3,2},{4,5},{5,4},{6,7},{7,6},{8,9},{9,8},{10,11... | collective-permute-start | bytes 442376 | tf_op jit(solution)/shard_map/ppermute | solution.py:713

commit v6 on v4

--- a/solution.py
+++ b/solution.py
@@ -687,6 +687,7 @@
     held, near = [(k, v)], [lax.ppermute(msg, "ka", swap)]
     bias, x = lax.optimization_barrier((bias, x))
     keep_bias = lax.dynamic_slice_in_dim(bias, parity * share, share, axis=1)
+    x, keep_bias = lax.optimization_barrier((x, keep_bias))
     for g in range(1, GROUPS):
         k, v, msg = group_call(
             functools.partial(next_kernel, g), g, send, (), queries, (x,), token_kv,

time: 105 us -> 102 us (0.971)
  waiting for transfers between devices: 21.9 us -> 9.77 us
  starting transfers between devices: 32.9 us -> 42.1 us
    ppermute x1, waiting for transfers between devices: 4.59 us -> 0.01 us  [body(): near.append(lax.ppermute(msg, 'ka', swap))]
    ppermute x1, starting transfers between devices: 0.69 us -> 5.12 us  [body(): held, near = ([(k, v)], [lax.ppermute(msg, 'ka', swap)])]
    ppermute x4, waiting for transfers between devices: 8.52 us -> 4.64 us  [key_parts(): lax.ppermute(part, ('pb', 'ka'), pairs)]
    ppermute x1, waiting for transfers between devices: 3.86 us -> 0.01 us  [body(): right = lax.ppermute(atoms[:half], 'pb', down)]
    ppermute x2, starting transfers between devices: 5.26 us -> 9.1 us  [far(): return lax.ppermute(msg, 'ka', [(i, i ^ 2 * bit - 1) for i in range(n_ka)])]
    ppermute x4, starting transfers between devices: 8.55 us -> 9.89 us  [key_parts(): lax.ppermute(part, ('pb', 'ka'), pairs)]
    ppermute x1, starting transfers between devices: 1.4 us -> 0.1 us  [body(): near.append(lax.ppermute(msg, 'ka', swap))]
  transfers between devices with their start and end apart: 15 -> 15, of which waited for: 7 -> 7; matrix products, arithmetic and copies ran while one was open for 3% -> 3% of each run, Pallas kernels for 13% -> 18%
where the time goes in v6:
time: 102 us; the launch traced here: 101 us
  Pallas kernels  42.3 us (41%)
  starting transfers between devices  42.1 us (41%)
  waiting for transfers between devices  9.77 us (10%)
  local copies, waits for them, and re-layouts  5.86 us (6%)
  between operations  1.03 us (1%)
    pallas_call x1, Pallas kernels, atom_attention(): pl.pallas_call(functools.partial(atom_kernel, chunks, atom_total, tok_row...  17.4 us
    pallas_call x4, Pallas kernels, group_call(): pl.pallas_call(functools.partial(kernel, heads, feats // heads), grid_spe...  13.9 us
    ppermute x4, starting transfers between devices, key_parts(): lax.ppermute(part, ('pb', 'ka'), pairs)  9.89 us
    ppermute x2, starting transfers between devices, far(): return lax.ppermute(msg, 'ka', [(i, i ^ 2 * bit - 1) for i in range(n_ka)])  9.1 us
    ppermute x2, starting transfers between devices, body(): other_mix.append(lax.ppermute(own_mix[g], 'ka', swap))  8.31 us
    pallas_call x2, Pallas kernels, pool(): pl.pallas_call(functools.partial(pool_kernel, tok_rows), grid_spec=pltpu....  6 us
    ppermute x1, starting transfers between devices, body(): held, near = ([(k, v)], [lax.ppermute(msg, 'ka', swap)])  5.12 us
    ppermute x4, waiting for transfers between devices, key_parts(): lax.ppermute(part, ('pb', 'ka'), pairs)  4.64 us
  transfers between devices with their start and end apart: 15, of which 7 were waited for; matrix products, arithmetic and copies ran while one was open for 3% of the time, Pallas kernels for 18%

profile of v6, /device:TPU:0, one launch (start us, length us, event | category | flops | bytes accessed | tf_op | source)
XLA Modules:
  0.0 101.1 jit_solution(14593733898849424238)
XLA Ops:
  0.6 0.7 fusion
  1.4 1.3 %collective-permute-start.1 = (bf16[64,128]{1,0:T(8,128)(2,1)S(1)}, bf16[64,128]{1,0:T(8,128)(2,1)S(1)}, u32[]{:S(2)}, u32[]{:S(2)}) collective-permute-start(bf16[64,128]{1,0:T(8,128)(2,1)S(1)} %get-tuple-element.58), channel_id=1, source_target_pairs={{4,0},{8,4},{12,8},{16,12},{20,16},{24,20},{28,24},{5,1},{9,5},{13... | collective-permute-start | bytes 49160 | tf_op jit(solution)/shard_map/ppermute | solution.py:657
  2.7 3.0 %collective-permute-start = (bf16[64,128]{1,0:T(8,128)(2,1)S(1)}, bf16[64,128]{1,0:T(8,128)(2,1)S(1)}, u32[]{:S(2)}, u32[]{:S(2)}) collective-permute-start(bf16[64,128]{1,0:T(8,128)(2,1)S(1)} %get-tuple-element.59), channel_id=1, source_target_pairs={{0,4},{4,8},{8,12},{12,16},{16,20},{20,24},{24,28},{1,5},{5,9},{9,... | collective-permute-start | bytes 49160 | tf_op jit(solution)/shard_map/ppermute | solution.py:656
  5.7 0.8 collective-permute-done.left_ref
  6.5 0.6 copy-done.8
  7.1 17.4 %atom_attention.1 = (bf16[3072,128]{1,0:T(8,128)(2,1)}, bf16[400,128]{1,0:T(8,128)(2,1)}) custom-call(s32[96]{0:T(128)} %shift_ref.1, s32[1]{0:T(128)} %bitcast.pos_ref, bf16[3072,128]{1,0:T(8,128)(2,1)} %atoms_ref.1, bf16[64,128]{1,0:T(8,128)(2,1)} %copy-done.8, bf16[64,128]{1,0:T(8,128)(2,1)} %copy-done.7, f32[128]{0:T(128)} %gain_ref.3, ...), custom_call_target="tpu_custom_call" | custom-call | flops 8000000000 | bytes 6000000 | tf_op jit(solution)/shard_map/atom_attention/pallas_call | solution.py:169
  24.6 4.5 %collective-permute-start.2 = (bf16[400,128]{1,0:T(8,128)(2,1)}, bf16[400,128]{1,0:T(8,128)(2,1)S(1)}, u32[]{:S(2)}, u32[]{:S(2)}) collective-permute-start(bf16[400,128]{1,0:T(8,128)(2,1)} %get-tuple-element.31), channel_id=1, source_target_pairs={{0,4},{4,8},{8,12},{12,16},{16,20},{20,24},{24,28},{1,5},{5,9},{9,... | collective-permute-start | bytes 307208 | tf_op jit(solution)/shard_map/ppermute | solution.py:662
  29.1 1.1 %copy-done.6 = bf16[3072,128]{1,0:T(8,128)(2,1)S(1)} copy-done((bf16[3072,128]{1,0:T(8,128)(2,1)S(1)}, bf16[3072,128]{1,0:T(8,128)(2,1)}, u32[]{:S(2)}) %copy-start.6) | copy-done | bytes 786456
  30.2 3.0 %pool.3 = (f32[384,384]{1,0:T(8,128)S(1)}, f32[384,128]{1,0:T(8,128)S(1)}) custom-call(s32[1]{0:T(128)} %bitcast.pos_ref, bf16[3072,128]{1,0:T(8,128)(2,1)S(1)} %copy-done.6, bf16[128,768]{1,0:T(8,128)(2,1)S(1)} %copy-done.2, s32[24,128]{1,0:T(8,128)S(1)} %bitcast.6), custom_call_target="tpu_custom_call" | custom-call | flops 2000000000 | bytes 2000000 | tf_op jit(solution)/shard_map/pool/pallas_call | solution.py:241
  33.8 4.4 %collective-permute-start.5 = (bf16[384,384]{1,0:T(8,128)(2,1)S(1)}, bf16[384,384]{1,0:T(8,128)(2,1)S(1)}, u32[]{:S(2)}, u32[]{:S(2)}) collective-permute-start(bf16[384,384]{1,0:T(8,128)(2,1)S(1)} %token_finish.3.b_ref), channel_id=1, source_target_pairs={{0,8},{9,1},{18,26},{27,19},{4,20},{13,29},{22,6},{31,15}} | collective-permute-start | bytes 884744 | tf_op jit(solution)/shard_map/ppermute | solution.py:628
  38.2 3.0 %pool.2 = (f32[384,384]{1,0:T(8,128)S(1)}, f32[384,128]{1,0:T(8,128)S(1)}) custom-call(s32[1]{0:T(128)} %bitcast.pos_ref, bf16[3072,128]{1,0:T(8,128)(2,1)S(1)} %copy-done.6, bf16[128,768]{1,0:T(8,128)(2,1)S(1)} %copy-done.2, s32[24,128]{1,0:T(8,128)S(1)} %bitcast.7), custom_call_target="tpu_custom_call" | custom-call | flops 2000000000 | bytes 2000000 | tf_op jit(solution)/shard_map/pool/pallas_call | solution.py:241
  41.2 0.6 token_finish.2.a_ref
  41.8 1.3 %collective-permute-start.3 = (bf16[384,384]{1,0:T(8,128)(2,1)S(1)}, bf16[384,384]{1,0:T(8,128)(2,1)S(1)}, u32[]{:S(2)}, u32[]{:S(2)}) collective-permute-start(bf16[384,384]{1,0:T(8,128)(2,1)S(1)} %token_finish.2.a_ref), channel_id=1, source_target_pairs={{0,8},{9,1},{18,26},{27,19},{4,20},{13,29},{22,6},{31,15}} | collective-permute-start | bytes 884744 | tf_op jit(solution)/shard_map/ppermute | solution.py:628
  43.2 2.7 %collective-permute-start.6 = (bf16[384,384]{1,0:T(8,128)(2,1)S(1)}, bf16[384,384]{1,0:T(8,128)(2,1)S(1)}, u32[]{:S(2)}, u32[]{:S(2)}) collective-permute-start(bf16[384,384]{1,0:T(8,128)(2,1)S(1)} %broadcast_select_fusion), channel_id=1, source_target_pairs={{0,16},{8,24},{1,17},{9,25},{18,2},{26,10},{19,3},{27,11},{4,12},{... | collective-permute-start | bytes 884744 | tf_op jit(solution)/shard_map/ppermute | solution.py:628
  45.9 2.1 %collective-permute-done.3 = bf16[384,384]{1,0:T(8,128)(2,1)S(1)} collective-permute-done((bf16[384,384]{1,0:T(8,128)(2,1)S(1)}, bf16[384,384]{1,0:T(8,128)(2,1)S(1)}, u32[]{:S(2)}, u32[]{:S(2)}) %collective-permute-start.3) | collective-permute-done | bytes 294944 | tf_op jit(solution)/shard_map/ppermute | solution.py:628
  48.1 1.5 %collective-permute-start.4 = (bf16[384,384]{1,0:T(8,128)(2,1)S(1)}, bf16[384,384]{1,0:T(8,128)(2,1)S(1)}, u32[]{:S(2)}, u32[]{:S(2)}) collective-permute-start(bf16[384,384]{1,0:T(8,128)(2,1)S(1)} %broadcast_select_fusion.1), channel_id=1, source_target_pairs={{0,16},{8,24},{1,17},{9,25},{18,2},{26,10},{19,3},{27,11},{4,12},{... | collective-permute-start | bytes 884744 | tf_op jit(solution)/shard_map/ppermute | solution.py:628
  49.6 1.3 %queries.1.q_ref = bf16[384,768]{1,0:T(8,128)(2,1)S(1)} custom-call(bf16[384,384]{1,0:T(8,128)(2,1)S(1)} %token_finish.2.a_ref, bf16[384,384]{1,0:T(8,128)(2,1)S(1)} %token_finish.3.b_ref, f32[768]{0:T(1024)S(1)} %copy-done.3, bf16[768,768]{1,0:T(8,128)(2,1)S(1)} %copy-done.1), custom_call_target="tpu_custom_call" | custom-call | flops 500000000 | bytes 3000000 | tf_op jit(solution)/shard_map/queries/pallas_call | solution.py:309
  51.0 0.7 collective-permute-start.8
  51.7 2.4 %collective-permute-done.4 = bf16[384,384]{1,0:T(8,128)(2,1)S(1)} collective-permute-done((bf16[384,384]{1,0:T(8,128)(2,1)S(1)}, bf16[384,384]{1,0:T(8,128)(2,1)S(1)}, u32[]{:S(2)}, u32[]{:S(2)}) %collective-permute-start.4) | collective-permute-done | bytes 294944 | tf_op jit(solution)/shard_map/ppermute | solution.py:628
  54.3 2.9 %constant_dynamic-slice_fusion.1.bias_ref = bf16[16,192,768]{2,1,0:T(8,128)(2,1)S(1)} fusion(bf16[16,384,768]{2,1,0:T(8,128)(2,1)} %param.25, s32[]{:T(128)S(6)} %select_n.40), kind=kLoop, calls=%fused_computation.5 | loop fusion | bytes 9437188 | tf_op jit(solution)/shard_map/dynamic_slice | solution.py:676
  57.4 4.8 %attend_first.1 = (bf16[768,768]{1,0:T(8,128)(2,1)S(1)}, bf16[384,768]{1,0:T(8,128)(2,1)S(1)}, bf16[768,384]{1,0:T(8,128)(2,1)S(1)}, bf16[208,384]{1,0:T(8,128)(2,1)S(1)}) custom-call(s32[1]{0:T(128)} %bitcast.3.half_ref, s32[1]{0:T(128)} %bitcast.4.core_ref, bf16[384,768]{1,0:T(8,128)(2,1)S(1)} %queries.1.q_ref, ...), custom_call_target="tpu_custom_call" | custom-call | flops 4000000000 | bytes 4000000 | tf_op jit(solution)/shard_map/attend_first/pallas_call | solution.py:532
  62.2 5.1 %collective-permute-start.9 = (bf16[208,384]{1,0:T(8,128)(2,1)S(1)}, bf16[208,384]{1,0:T(8,128)(2,1)S(1)}, u32[]{:S(2)}, u32[]{:S(2)}) collective-permute-start(bf16[208,384]{1,0:T(8,128)(2,1)S(1)} %get-tuple-element.43), channel_id=1, source_target_pairs={{0,1},{1,0},{2,3},{3,2},{4,5},{5,4},{6,7},{7,6},{8,9},{9,8},{10,11... | collective-permute-start | bytes 479240 | tf_op jit(solution)/shard_map/ppermute | solution.py:687
  67.7 4.2 %attend_next.1 = (bf16[384,768]{1,0:T(8,128)(2,1)S(1)}, bf16[768,384]{1,0:T(8,128)(2,1)S(1)}, bf16[208,384]{1,0:T(8,128)(2,1)S(1)}) custom-call(s32[1]{0:T(128)} %bitcast.3.half_ref, bf16[384,768]{1,0:T(8,128)(2,1)S(1)} %queries.1.q_ref, bf16[768,768]{1,0:T(8,128)(2,1)S(1)} %get-tuple-element.51.x_ref, bf16[768,1536]{1,0:T(8,128)(2,1)S(1)} %copy-done.4, ...), custom_call_target="tpu_custom_call" | custom-call | flops 4000000000 | bytes 4000000 | tf_op jit(solution)/shard_map/attend_next/pallas_call | solution.py:532
  72.0 2.5 %attend_keep.2 = (f32[192,384]{1,0:T(8,128)S(1)}, f32[192,128]{1,0:T(8,128)S(1)}, bf16[208,384]{1,0:T(8,128)(2,1)S(1)}) custom-call(s32[1]{0:T(128)} %bitcast.2.half_ref, bf16[384,768]{1,0:T(8,128)(2,1)S(1)} %queries.1.q_ref, bf16[384,768]{1,0:T(8,128)(2,1)S(1)} %get-tuple-element.41.k_ref, bf16[768,384]{1,0:T(8,128)(2,1)S(1)} %get-tuple-element.42.v_ref, ...), custom_call_target="tpu_custom_call" | custom-call | flops 4000000000 | bytes 4000000 | tf_op jit(solution)/shard_map/attend_keep/pallas_call | solution.py:532
  74.4 7.1 %collective-permute-start.10 = (bf16[208,384]{1,0:T(8,128)(2,1)S(1)}, bf16[208,384]{1,0:T(8,128)(2,1)S(1)}, u32[]{:S(2)}, u32[]{:S(2)}) collective-permute-start(bf16[208,384]{1,0:T(8,128)(2,1)S(1)} %get-tuple-element.50), channel_id=1, source_target_pairs={{0,3},{1,2},{2,1},{3,0},{4,7},{5,6},{6,5},{7,4},{8,11},{9,10},{10,... | collective-permute-start | bytes 479240 | tf_op jit(solution)/shard_map/ppermute | solution.py:681
  81.5 2.4 %attend_keep.3 = (f32[192,384]{1,0:T(8,128)S(1)}, f32[192,128]{1,0:T(8,128)S(1)}, bf16[208,384]{1,0:T(8,128)(2,1)S(1)}) custom-call(s32[1]{0:T(128)} %bitcast.2.half_ref, bf16[384,768]{1,0:T(8,128)(2,1)S(1)} %queries.1.q_ref, bf16[384,768]{1,0:T(8,128)(2,1)S(1)} %get-tuple-element.52.k_ref, bf16[768,384]{1,0:T(8,128)(2,1)S(1)} %get-tuple-element.53.v_ref, ...), custom_call_target="tpu_custom_call" | custom-call | flops 4000000000 | bytes 4000000 | tf_op jit(solution)/shard_map/attend_keep/pallas_call | solution.py:532
  83.9 2.0 %collective-permute-start.12 = (bf16[208,384]{1,0:T(8,128)(2,1)S(1)}, bf16[208,384]{1,0:T(8,128)(2,1)S(1)}, u32[]{:S(2)}, u32[]{:S(2)}) collective-permute-start(bf16[208,384]{1,0:T(8,128)(2,1)S(1)} %get-tuple-element.57), channel_id=1, source_target_pairs={{0,3},{1,2},{2,1},{3,0},{4,7},{5,6},{6,5},{7,4},{8,11},{9,10},{10,... | collective-permute-start | bytes 479240 | tf_op jit(solution)/shard_map/ppermute | solution.py:681
  86.0 0.7 collective-permute-done.10.msg_ref
  87.2 5.9 %collective-permute-start.13 = (bf16[192,384]{1,0:T(8,128)(2,1)S(1)}, bf16[192,384]{1,0:T(8,128)(2,1)S(1)}, u32[]{:S(2)}, u32[]{:S(2)}) collective-permute-start(bf16[192,384]{1,0:T(8,128)(2,1)S(1)} %settle.2.own_a), channel_id=1, source_target_pairs={{0,1},{1,0},{2,3},{3,2},{4,5},{5,4},{6,7},{7,6},{8,9},{9,8},{10,11... | collective-permute-start | bytes 442376 | tf_op jit(solution)/shard_map/ppermute | solution.py:713
  93.5 2.4 %collective-permute-start.14 = (bf16[192,384]{1,0:T(8,128)(2,1)S(1)}, bf16[192,384]{1,0:T(8,128)(2,1)S(1)}, u32[]{:S(2)}, u32[]{:S(2)}) collective-permute-start(bf16[192,384]{1,0:T(8,128)(2,1)S(1)} %settle.3.own_b), channel_id=1, source_target_pairs={{0,1},{1,0},{2,3},{3,2},{4,5},{5,4},{6,7},{7,6},{8,9},{9,8},{10,11... | collective-permute-start | bytes 442376 | tf_op jit(solution)/shard_map/ppermute | solution.py:713
  96.1 3.4 %collective-permute-done.14.other_b = bf16[192,384]{1,0:T(8,128)(2,1)S(1)} collective-permute-done((bf16[192,384]{1,0:T(8,128)(2,1)S(1)}, bf16[192,384]{1,0:T(8,128)(2,1)S(1)}, u32[]{:S(2)}, u32[]{:S(2)}) %collective-permute-start.14) | collective-permute-done | bytes 147488 | tf_op jit(solution)/shard_map/ppermute | solution.py:713
  99.5 1.6 %output_rows.1 = bf16[384,768]{1,0:T(8,128)(2,1)} custom-call(s32[1]{0:T(128)} %bitcast.2.half_ref, bf16[192,384]{1,0:T(8,128)(2,1)S(1)} %settle.2.own_a, bf16[192,384]{1,0:T(8,128)(2,1)S(1)} %settle.3.own_b, bf16[192,384]{1,0:T(8,128)(2,1)S(1)} %collective-permute-done.13.other_a, bf16[192,384]{1,0:T(8,128)(2,1)S(1)} %collective-permute-done.14.other_b, ...), custom_call_target="tpu_custom_call" | custom-call | tf_op jit(solution)/shard_map/output_rows/pallas_call | solution.py:594
  (43 shorter events, 2.6 us)
Async XLA Ops:
  1.4 4.3 %collective-permute-start.1 = (bf16[64,128]{1,0:T(8,128)(2,1)S(1)}, bf16[64,128]{1,0:T(8,128)(2,1)S(1)}, u32[]{:S(2)}, u32[]{:S(2)}) collective-permute-start(bf16[64,128]{1,0:T(8,128)(2,1)S(1)} %get-tuple-element.58), channel_id=1, source_target_pairs={{4,0},{8,4},{12,8},{16,12},{20,16},{24,20},{28,24},{5,1},{9,5},{13... | collective-permute-start | bytes 49160 | tf_op jit(solution)/shard_map/ppermute | solution.py:657
  2.7 3.9 %collective-permute-start = (bf16[64,128]{1,0:T(8,128)(2,1)S(1)}, bf16[64,128]{1,0:T(8,128)(2,1)S(1)}, u32[]{:S(2)}, u32[]{:S(2)}) collective-permute-start(bf16[64,128]{1,0:T(8,128)(2,1)S(1)} %get-tuple-element.59), channel_id=1, source_target_pairs={{0,4},{4,8},{8,12},{12,16},{16,20},{20,24},{24,28},{1,5},{5,9},{9,... | collective-permute-start | bytes 49160 | tf_op jit(solution)/shard_map/ppermute | solution.py:656
  5.7 0.8 copy-start.7
  6.5 0.6 copy-start.8
  7.1 21.9 %copy-start.2 = (bf16[128,768]{1,0:T(8,128)(2,1)S(1)}, bf16[128,768]{1,0:T(8,128)(2,1)}, u32[]{:S(2)}) copy-start(bf16[128,768]{1,0:T(8,128)(2,1)} %weight_ref.8) | copy-start | bytes 589828
  7.1 21.9 %copy-start.5 = (s32[3072]{0:T(1024)S(1)}, s32[3072]{0:T(1024)}, u32[]{:S(2)}) copy-start(s32[3072]{0:T(1024)} %param.19) | copy-start | bytes 36868
  24.6 8.6 %collective-permute-start.2 = (bf16[400,128]{1,0:T(8,128)(2,1)}, bf16[400,128]{1,0:T(8,128)(2,1)S(1)}, u32[]{:S(2)}, u32[]{:S(2)}) collective-permute-start(bf16[400,128]{1,0:T(8,128)(2,1)} %get-tuple-element.31), channel_id=1, source_target_pairs={{0,4},{4,8},{8,12},{12,16},{16,20},{20,24},{24,28},{1,5},{5,9},{9,... | collective-permute-start | bytes 307208 | tf_op jit(solution)/shard_map/ppermute | solution.py:662
  29.1 1.1 %copy-start.6 = (bf16[3072,128]{1,0:T(8,128)(2,1)S(1)}, bf16[3072,128]{1,0:T(8,128)(2,1)}, u32[]{:S(2)}) copy-start(bf16[3072,128]{1,0:T(8,128)(2,1)} %get-tuple-element.28.out_ref) | copy-start | bytes 2359300
  33.8 15.8 %copy-start.1 = (bf16[768,768]{1,0:T(8,128)(2,1)S(1)}, bf16[768,768]{1,0:T(8,128)(2,1)}, u32[]{:S(2)}) copy-start(bf16[768,768]{1,0:T(8,128)(2,1)} %weight_hbm.3) | copy-start | bytes 3538948
  33.8 15.8 %copy-start.3 = (f32[768]{0:T(1024)S(1)}, f32[768]{0:T(1024)}, u32[]{:S(2)}) copy-start(f32[768]{0:T(1024)} %gain_ref.5) | copy-start | bytes 9220
  33.8 9.4 %collective-permute-start.5 = (bf16[384,384]{1,0:T(8,128)(2,1)S(1)}, bf16[384,384]{1,0:T(8,128)(2,1)S(1)}, u32[]{:S(2)}, u32[]{:S(2)}) collective-permute-start(bf16[384,384]{1,0:T(8,128)(2,1)S(1)} %token_finish.3.b_ref), channel_id=1, source_target_pairs={{0,8},{9,1},{18,26},{27,19},{4,20},{13,29},{22,6},{31,15}} | collective-permute-start | bytes 884744 | tf_op jit(solution)/shard_map/ppermute | solution.py:628
  41.8 6.2 %collective-permute-start.3 = (bf16[384,384]{1,0:T(8,128)(2,1)S(1)}, bf16[384,384]{1,0:T(8,128)(2,1)S(1)}, u32[]{:S(2)}, u32[]{:S(2)}) collective-permute-start(bf16[384,384]{1,0:T(8,128)(2,1)S(1)} %token_finish.2.a_ref), channel_id=1, source_target_pairs={{0,8},{9,1},{18,26},{27,19},{4,20},{13,29},{22,6},{31,15}} | collective-permute-start | bytes 884744 | tf_op jit(solution)/shard_map/ppermute | solution.py:628
  43.2 7.8 %collective-permute-start.6 = (bf16[384,384]{1,0:T(8,128)(2,1)S(1)}, bf16[384,384]{1,0:T(8,128)(2,1)S(1)}, u32[]{:S(2)}, u32[]{:S(2)}) collective-permute-start(bf16[384,384]{1,0:T(8,128)(2,1)S(1)} %broadcast_select_fusion), channel_id=1, source_target_pairs={{0,16},{8,24},{1,17},{9,25},{18,2},{26,10},{19,3},{27,11},{4,12},{... | collective-permute-start | bytes 884744 | tf_op jit(solution)/shard_map/ppermute | solution.py:628
  48.1 6.1 %collective-permute-start.4 = (bf16[384,384]{1,0:T(8,128)(2,1)S(1)}, bf16[384,384]{1,0:T(8,128)(2,1)S(1)}, u32[]{:S(2)}, u32[]{:S(2)}) collective-permute-start(bf16[384,384]{1,0:T(8,128)(2,1)S(1)} %broadcast_select_fusion.1), channel_id=1, source_target_pairs={{0,16},{8,24},{1,17},{9,25},{18,2},{26,10},{19,3},{27,11},{4,12},{... | collective-permute-start | bytes 884744 | tf_op jit(solution)/shard_map/ppermute | solution.py:628
  51.0 6.2 %collective-permute-start.8 = (bf16[384,384]{1,0:T(8,128)(2,1)S(1)}, bf16[384,384]{1,0:T(8,128)(2,1)S(1)}, u32[]{:S(2)}, u32[]{:S(2)}) collective-permute-start(bf16[384,384]{1,0:T(8,128)(2,1)S(1)} %broadcast_select_fusion.2.own_b), channel_id=1, source_target_pairs={{0,4},{4,0},{8,12},{12,8},{16,20},{20,16},{24,28},{28,24},{1,5},{5... | collective-permute-start | bytes 884744 | tf_op jit(solution)/shard_map/ppermute | solution.py:674
  54.2 3.1 %collective-permute-start.7 = (bf16[384,384]{1,0:T(8,128)(2,1)S(1)}, bf16[384,384]{1,0:T(8,128)(2,1)S(1)}, u32[]{:S(2)}, u32[]{:S(2)}) collective-permute-start(bf16[384,384]{1,0:T(8,128)(2,1)S(1)} %broadcast_select_fusion.3.own_a), channel_id=1, source_target_pairs={{0,4},{4,0},{8,12},{12,8},{16,20},{20,16},{24,28},{28,24},{1,5},{5... | collective-permute-start | bytes 884744 | tf_op jit(solution)/shard_map/ppermute | solution.py:674
  54.3 3.1 %copy-start.4 = (bf16[768,1536]{1,0:T(8,128)(2,1)S(1)}, bf16[768,1536]{1,0:T(8,128)(2,1)}, u32[]{:S(2)}) copy-start(bf16[768,1536]{1,0:T(8,128)(2,1)} %weight_hbm.5) | copy-start | bytes 7077892
  54.3 13.0 %slice-start = ((s8[9437184]{0:T(1024)(128)(4,1)}), s8[4194304]{0:T(1024)(128)(4,1)S(1)}, s32[]{:S(2)}) async-start(s8[9437184]{0:T(1024)(128)(4,1)} %bitcast.8), calls=%async_computation | async-start | bytes 8388608
  54.3 13.0 %slice-start.1 = ((s8[9437184]{0:T(1024)(128)(4,1)}), s8[4194304]{0:T(1024)(128)(4,1)S(1)}, s32[]{:S(2)}) async-start(s8[9437184]{0:T(1024)(128)(4,1)} %bitcast.8), calls=%async_computation.1 | async-start | bytes 8388608
  57.4 9.9 %slice-start.2 = ((s8[9437184]{0:T(1024)(128)(4,1)}), s8[1048576]{0:T(1024)(128)(4,1)S(1)}, s32[]{:S(2)}) async-start(s8[9437184]{0:T(1024)(128)(4,1)} %bitcast.8), calls=%async_computation.2 | async-start | bytes 2097152
  62.2 9.8 %collective-permute-start.9 = (bf16[208,384]{1,0:T(8,128)(2,1)S(1)}, bf16[208,384]{1,0:T(8,128)(2,1)S(1)}, u32[]{:S(2)}, u32[]{:S(2)}) collective-permute-start(bf16[208,384]{1,0:T(8,128)(2,1)S(1)} %get-tuple-element.43), channel_id=1, source_target_pairs={{0,1},{1,0},{2,3},{3,2},{4,5},{5,4},{6,7},{7,6},{8,9},{9,8},{10,11... | collective-permute-start | bytes 479240 | tf_op jit(solution)/shard_map/ppermute | solution.py:687
  71.9 9.6 %collective-permute-start.11 = (bf16[208,384]{1,0:T(8,128)(2,1)S(1)}, bf16[208,384]{1,0:T(8,128)(2,1)S(1)}, u32[]{:S(2)}, u32[]{:S(2)}) collective-permute-start(bf16[208,384]{1,0:T(8,128)(2,1)S(1)} %get-tuple-element.54), channel_id=1, source_target_pairs={{0,1},{1,0},{2,3},{3,2},{4,5},{5,4},{6,7},{7,6},{8,9},{9,8},{10,11... | collective-permute-start | bytes 479240 | tf_op jit(solution)/shard_map/ppermute | solution.py:697
  74.4 12.2 %collective-permute-start.10 = (bf16[208,384]{1,0:T(8,128)(2,1)S(1)}, bf16[208,384]{1,0:T(8,128)(2,1)S(1)}, u32[]{:S(2)}, u32[]{:S(2)}) collective-permute-start(bf16[208,384]{1,0:T(8,128)(2,1)S(1)} %get-tuple-element.50), channel_id=1, source_target_pairs={{0,3},{1,2},{2,1},{3,0},{4,7},{5,6},{6,5},{7,4},{8,11},{9,10},{10,... | collective-permute-start | bytes 479240 | tf_op jit(solution)/shard_map/ppermute | solution.py:681
  81.5 18.0 %copy-start = (bf16[768,768]{1,0:T(8,128)(2,1)S(1)}, bf16[768,768]{1,0:T(8,128)(2,1)}, u32[]{:S(2)}) copy-start(bf16[768,768]{1,0:T(8,128)(2,1)} %weight_ref.9) | copy-start | bytes 3538948
  83.9 9.1 %collective-permute-start.12 = (bf16[208,384]{1,0:T(8,128)(2,1)S(1)}, bf16[208,384]{1,0:T(8,128)(2,1)S(1)}, u32[]{:S(2)}, u32[]{:S(2)}) collective-permute-start(bf16[208,384]{1,0:T(8,128)(2,1)S(1)} %get-tuple-element.57), channel_id=1, source_target_pairs={{0,3},{1,2},{2,1},{3,0},{4,7},{5,6},{6,5},{7,4},{8,11},{9,10},{10,... | collective-permute-start | bytes 479240 | tf_op jit(solution)/shard_map/ppermute | solution.py:681
  87.2 9.0 %collective-permute-start.13 = (bf16[192,384]{1,0:T(8,128)(2,1)S(1)}, bf16[192,384]{1,0:T(8,128)(2,1)S(1)}, u32[]{:S(2)}, u32[]{:S(2)}) collective-permute-start(bf16[192,384]{1,0:T(8,128)(2,1)S(1)} %settle.2.own_a), channel_id=1, source_target_pairs={{0,1},{1,0},{2,3},{3,2},{4,5},{5,4},{6,7},{7,6},{8,9},{9,8},{10,11... | collective-permute-start | bytes 442376 | tf_op jit(solution)/shard_map/ppermute | solution.py:713
  93.5 6.0 %collective-permute-start.14 = (bf16[192,384]{1,0:T(8,128)(2,1)S(1)}, bf16[192,384]{1,0:T(8,128)(2,1)S(1)}, u32[]{:S(2)}, u32[]{:S(2)}) collective-permute-start(bf16[192,384]{1,0:T(8,128)(2,1)S(1)} %settle.3.own_b), channel_id=1, source_target_pairs={{0,1},{1,0},{2,3},{3,2},{4,5},{5,4},{6,7},{7,6},{8,9},{9,8},{10,11... | collective-permute-start | bytes 442376 | tf_op jit(solution)/shard_map/ppermute | solution.py:713
